TPU v7x, 512 devices: a whole 4x8x8 slice. The times are simulated.
512 devices in a mesh: dp: 32 (over y_lo, x, core), seq: 16 (over y_hi, z).
Axes of the slice: x: 4, y: 8 (y_hi: 2, y_lo: 4; y = y_hi * 4 + y_lo), z: 8, core: 2. Of those that a mesh axis runs over, the one named last changes fastest.
Arguments:
- bins: bfloat16 [32, 2048, 1536], P('dp', 'seq'), may hold values from -6 to 6
- pair_in: bfloat16 [32, 128, 128, 128], P('dp', 'seq'), may hold values from -12 to 12
- valid: int32 [32], P('dp'), may hold values from 1024 to 2048, as said below
- gain: float32 [1536], replicated, may hold values from 0.5 to 1.5
- w_qkv: bfloat16 [1536, 2304], P('dp'), may hold values from -0.15625 to 0.15625
- w_pair: bfloat16 [1536, 256], P('dp'), may hold values from -0.15625 to 0.15625
- w_bias: float32 [128, 6], replicated, may hold values from -2 to 2
- w_out: bfloat16 [768, 1536], P(None, 'dp'), may hold values from -0.21875 to 0.21875
Outputs:
- mixed: bfloat16 [32, 2048, 1536], P('dp', 'seq')
- pair_out: bfloat16 [32, 128, 128, 128], P('dp', 'seq')
Inputs may be any that keep to these rules, and one draw needn't show every extreme that they name: `valid`: the first window is full.
All inputs are finite; a program needn't handle non-finite values.
Results may differ from a plain program's by a relative error of at most 0.006.
Values may be sent and summed in bfloat16 or wider, within the bound.
No kernel may reach another device: no remote copies, remote signals or barrier semaphores. Data moves between devices by JAX's collectives and lax.ppermute only.
A program may use at most 64 MiB of HBM per device.

v0:
```python
import jax
import jax.numpy as jnp
from jax import lax
from jax.sharding import PartitionSpec as P

HEADS = 6
HD = 128
CP = 128
POOL = 16


def on_device(bins, pair_in, valid, gain, w_qkv, w_pair, w_bias, w_out):
    feats = bins[0].astype(jnp.float32)
    count = feats.shape[0]
    meansq = jnp.mean(feats * feats, axis=-1, keepdims=True)
    normed = (feats * lax.rsqrt(meansq + 1e-06) * gain).astype(jnp.bfloat16)
    columns = normed
    first = jnp.dot(
        columns, lax.all_gather(w_qkv, "dp", axis=0, tiled=True), preferred_element_type=jnp.float32
    )
    second = jnp.dot(
        columns,
        lax.all_gather(w_pair, "dp", axis=0, tiled=True),
        preferred_element_type=jnp.float32,
    )
    pooled = second.reshape(count // POOL, POOL, 2 * CP).mean(axis=1).astype(jnp.bfloat16)
    right_all = lax.all_gather(pooled[:, CP:], "seq", axis=0, tiled=True)
    left = pooled[:, :CP].astype(jnp.float32)
    pair_out = (
        pair_in[0].astype(jnp.float32)
        + left[:, None, :] * right_all.astype(jnp.float32)[None, :, :]
    ).astype(jnp.bfloat16)
    pbias = jnp.einsum("ijc,ch->hij", pair_out.astype(jnp.float32), w_bias)
    npairs = pbias.shape[2]
    qkv = first.astype(jnp.bfloat16)
    query = qkv[:, : HEADS * HD].reshape(count, HEADS, HD)
    keyval = qkv[:, HEADS * HD :]
    limit = valid[0]
    scale = 1.0 / jnp.sqrt(jnp.float32(HD))
    whole = lax.all_gather(keyval, "seq", axis=0, tiled=True)
    running = jnp.full((HEADS, count), -1e30, jnp.float32)
    width = whole.shape[0]
    keys = whole[:, : HEADS * HD].reshape(width, HEADS, HD)
    values = whole[:, HEADS * HD :].reshape(width, HEADS, HD)
    scores = jnp.einsum("ihd,jhd->hij", query, keys, preferred_element_type=jnp.float32) * scale
    columns = jnp.arange(width, dtype=jnp.int32)
    onehot = (columns[:, None] // POOL == jnp.arange(npairs, dtype=jnp.int32)[None, :]).astype(
        jnp.float32
    )
    key_bias = jnp.einsum("hrp,jp->hrj", pbias, onehot)
    scores = scores + jnp.repeat(key_bias, POOL, axis=1)
    live = (columns < limit)[None, None, :]
    scores = jnp.where(live, scores, jnp.float32(-1e30))
    newmax = jnp.maximum(running, jnp.max(scores, axis=-1))
    expo = jnp.where(live, jnp.exp(scores - newmax[..., None]), 0.0)
    total = jnp.sum(expo, axis=-1)
    accum = jnp.einsum(
        "hij,jhd->hid", expo.astype(jnp.bfloat16), values, preferred_element_type=jnp.float32
    )
    running, total, accum = (newmax, total, accum)
    attn = accum / total[..., None]
    attn = jnp.transpose(attn, (1, 0, 2)).reshape(count, HEADS * HD).astype(jnp.bfloat16)
    update = jnp.dot(
        attn, lax.all_gather(w_out, "dp", axis=1, tiled=True), preferred_element_type=jnp.float32
    )
    mixed = (feats + update).astype(jnp.bfloat16)
    return (mixed[None], pair_out[None])


def solution(mesh):
    placed = (
        P("dp", "seq", None),
        P("dp", "seq", None, None),
        P("dp"),
        P(),
        P("dp", None),
        P("dp", None),
        P(),
        P(None, "dp"),
    )
    return jax.shard_map(
        on_device,
        mesh=mesh,
        in_specs=placed,
        out_specs=(P("dp", "seq", None), P("dp", "seq", None, None)),
        check_vma=False,
    )
```

profile of v0, /device:TPU:1, one launch (start us, length us, event | category | flops | bytes accessed | tf_op | source)
XLA Modules:
  0.0 322.5 jit_solution(6400514863498792242)
XLA Ops:
  7.2 0.0 copy-start
  7.2 0.0 copy-start.1
  7.2 0.0 copy-start.6
  7.2 0.0 copy-start.5
  7.2 0.0 all-gather.4.cloned.1.call-start
  7.3 0.7 all-gather.4.cloned.1.call-update
  8.0 0.0 all-gather.6.cloned.1.call-start
  8.0 1.2 fusion.12
  9.2 77.3 %all-gather.4.cloned.1.call-done = bf16[1536,2304]{1,0:T(8,128)(2,1)} async-done(((bf16[48,2304]{1,0:T(8,128)(2,1)}), bf16[1536,2304]{1,0:T(8,128)(2,1)}) %all-gather.4.cloned.1.call-update) | async-done | bytes 7077904 | tf_op jit(solution)/shard_map/all_gather | solution.py:19
  86.4 4.3 %convolution_convert_fusion = bf16[128,2304]{1,0:T(8,128)(2,1)S(1)} fusion(bf16[1536,2304]{1,0:T(8,128)(2,1)} %all-gather.4.cloned.1.call-done, bf16[1,128,1536]{2,1,0:T(8,128)(2,1)} %param.8, f32[1536]{0:T(1024)} %param.11, f32[128]{0:T(128)S(1)} %add_rsqrt_fusion), kind=kOutput, calls=%fused_computation.6 | convolution fusion | flops 907051008 | bytes 8067584 | tf_op jit(solution)/shard_map/dot_general | solution.py:18
  90.8 0.8 slice.25
  91.5 0.0 all-gather.6.cloned.1.call-update
  91.6 0.0 all-gather.8.cloned.1.call-start
  91.6 0.7 all-gather.8.cloned.1.call-update
  92.3 0.1 rsqrt.13
  92.4 43.4 %all_gather.17 = bf16[1536,256]{1,0:T(8,128)(2,1)S(1)} all-gather(bf16[48,256]{1,0:T(8,128)(2,1)S(1)} %copy-done.5), channel_id=1, replica_groups=mesh['dp'=32,'seq'=16] {'dp'}, dimensions={0}, use_global_device_ids=true | all-gather | bytes 811008 | tf_op jit(solution)/shard_map/all_gather | solution.py:23
  135.8 0.3 convolution_reduce_fusion
  136.1 46.8 %all_gather.18 = bf16[128,128]{1,0:T(8,128)(2,1)S(1)} all-gather(bf16[8,128]{1,0:T(8,128)(2,1)S(1)} %get-tuple-element.7), channel_id=1, replica_groups=mesh['dp'=32,'seq'=16] {'seq'}, dimensions={0}, use_global_device_ids=true | all-gather | bytes 34816 | tf_op jit(solution)/shard_map/all_gather | solution.py:27
  183.6 0.2 fusion.24
  183.8 0.5 fusion.9
  184.3 0.8 fusion.17
  185.1 0.8 copy.13
  185.9 66.0 %all-gather.6.cloned.1.call-done = bf16[2048,1536]{1,0:T(8,128)(2,1)} async-done(((bf16[128,1536]{1,0:T(8,128)(2,1)}), bf16[2048,1536]{1,0:T(8,128)(2,1)}) %all-gather.6.cloned.1.call-update) | async-done | bytes 6291472 | tf_op jit(solution)/shard_map/all_gather | solution.py:40
  252.0 5.9 %fusion.35 = (bf16[2048,768]{1,0:T(8,128)(2,1)}, bf16[2048,768]{1,0:T(8,128)(2,1)}) fusion(bf16[2048,1536]{1,0:T(8,128)(2,1)} %all-gather.6.cloned.1.call-done), kind=kLoop, calls=%fused_computation.52 | loop fusion | bytes 12582912 | tf_op jit(solution)/shard_map/slice | solution.py:44
  257.9 3.2 copy.14
  261.1 4.7 %copy.17 = bf16[2048,768]{0,1:T(8,128)(2,1)} copy(bf16[2048,768]{1,0:T(8,128)(2,1)} %get-tuple-element.4) | data formatting | bytes 6291456 | tf_op jit(solution)/shard_map/slice | solution.py:44
  265.7 2.5 fusion.3
  268.3 2.0 fusion.1
  270.3 0.0 copy-start.2
  270.3 1.0 fusion.7
  271.3 41.4 %all-gather.8.cloned.1.call-done = bf16[768,1536]{0,1:T(8,128)(2,1)} async-done(((bf16[768,48]{0,1:T(8,128)(2,1)}), bf16[768,1536]{0,1:T(8,128)(2,1)}) %all-gather.8.cloned.1.call-update) | async-done | bytes 2359312 | tf_op jit(solution)/shard_map/all_gather | solution.py:64
  312.7 3.3 %fusion.5 = bf16[1,128,1536]{2,1,0:T(8,128)(2,1)} fusion(bf16[128,768]{0,1:T(8,128)(2,1)S(1)} %bitcast.77, bf16[768,1536]{0,1:T(8,128)(2,1)} %all-gather.8.cloned.1.call-done, bf16[1,128,1536]{2,1,0:T(8,128)(2,1)S(1)} %copy-done.2), kind=kOutput, calls=%fused_computation.9 | convolution fusion | flops 302579712 | bytes 3342336 | tf_op jit(solution)/shard_map/dot_general | solution.py:63
  (17 shorter events, 0.1 us)
Async XLA Ops:
  7.2 176.5 %copy-start = (f32[128,6]{0,1:T(8,128)S(1)}, f32[128,6]{0,1:T(8,128)}, u32[]{:S(2)}) copy-start(f32[128,6]{0,1:T(8,128)} %param.14) | copy-start | bytes 9220
  7.2 128.6 %copy-start.1 = (bf16[1,128,1536]{2,1,0:T(8,128)(2,1)S(1)}, bf16[1,128,1536]{2,1,0:T(8,128)(2,1)}, u32[]{:S(2)}) copy-start(bf16[1,128,1536]{2,1,0:T(8,128)(2,1)} %param.8) | copy-start | bytes 1179652
  7.2 128.6 %copy-start.6 = (f32[1536]{0:T(1024)S(1)}, f32[1536]{0:T(1024)}, u32[]{:S(2)}) copy-start(f32[1536]{0:T(1024)} %param.11) | copy-start | bytes 18436
  7.2 85.2 %copy-start.5 = (bf16[48,256]{1,0:T(8,128)(2,1)S(1)}, bf16[48,256]{1,0:T(8,128)(2,1)}, u32[]{:S(2)}) copy-start(bf16[48,256]{1,0:T(8,128)(2,1)} %param.13) | copy-start | bytes 73732
  7.2 176.4 %copy-start.4 = (bf16[1,8,128,128]{3,2,1,0:T(8,128)(2,1)S(1)}, bf16[1,8,128,128]{3,2,1,0:T(8,128)(2,1)}, u32[]{:S(2)}) copy-start(bf16[1,8,128,128]{3,2,1,0:T(8,128)(2,1)} %param.9) | copy-start | bytes 786436
  7.2 79.2 %all-gather.4.cloned.1.call-start = ((), (), s32[]{:S(2)}) async-start(), calls=%async_computation | async-start | bytes 7299072 | tf_op jit(solution)/shard_map/all_gather | solution.py:19
  8.0 244.0 %all-gather.6.cloned.1.call-start = ((), (), s32[]{:S(2)}) async-start(), calls=%async_computation.1 | async-start | bytes 6684672 | tf_op jit(solution)/shard_map/all_gather | solution.py:40
  91.6 221.1 %all-gather.8.cloned.1.call-start = ((), (), s32[]{:S(2)}) async-start(), calls=%async_computation.2 | async-start | bytes 2433024 | tf_op jit(solution)/shard_map/all_gather | solution.py:64
  268.2 2.1 copy-start.3
  270.3 42.4 %copy-start.2 = (bf16[1,128,1536]{2,1,0:T(8,128)(2,1)S(1)}, bf16[1,128,1536]{2,1,0:T(8,128)(2,1)}, u32[]{:S(2)}) copy-start(bf16[1,128,1536]{2,1,0:T(8,128)(2,1)} %param.8) | copy-start | bytes 1179652
Sparse Core Ops, SparseCore 0:
  10.2 76.1 all-gather.3
  91.7 160.2 all-gather.5
  254.1 58.5 all-gather.7
where the time goes:
time: 323 us
  waiting for transfers between devices  186 us (58%)
  blocking collectives  90.2 us (28%)
  local copies, waits for them, and re-layouts  15.5 us (5%)
  between operations  14.6 us (5%)
  matrix products  12.2 us (4%)
  other arithmetic  4.02 us (1%)
    all_gather x1, waiting for transfers between devices, on_device(): lax.all_gather(w_qkv, 'dp', axis=0, tiled=True)  77.3 us
    all_gather x1, waiting for transfers between devices, on_device(): whole = lax.all_gather(keyval, 'seq', axis=0, tiled=True)  66 us
    all_gather x1, blocking collectives, on_device(): right_all = lax.all_gather(pooled[:, CP:], 'seq', axis=0, tiled=True)  46.8 us
    all_gather x1, blocking collectives, on_device(): lax.all_gather(w_pair, 'dp', axis=0, tiled=True)  43.4 us
    all_gather x1, waiting for transfers between devices, on_device(): lax.all_gather(w_out, 'dp', axis=1, tiled=True)  41.4 us
    slice x2, local copies, waits for them, and re-layouts, on_device(): values = whole[:, HEADS * HD:].reshape(width, HEADS, HD)  10.6 us
  transfers between devices with their start and end apart: 3, of which 3 were waited for; matrix products, arithmetic and copies ran while one was open for 7% of the time, Pallas kernels for 0%

commit v1 on v0

v1 whole, which is shorter than its diff:
```python
import functools

import jax
import jax.numpy as jnp
from jax import lax
from jax.experimental import pallas as pl
from jax.experimental.pallas import tpu as pltpu
from jax.sharding import Mesh, PartitionSpec as P

HEADS = 6
HD = 128
CP = 128
POOL = 16
HALF = HEADS // 2
HW = HALF * HD
VMEM = 48 * 1024 * 1024

BF = jnp.bfloat16
F32 = jnp.float32


def params():
    return pltpu.CompilerParams(vmem_limit_bytes=VMEM)


def vm():
    return pl.BlockSpec(memory_space=pltpu.VMEM)


def sm():
    return pl.BlockSpec(memory_space=pltpu.SMEM)


def hbm():
    return pl.BlockSpec(memory_space=pl.ANY)


def nt(a, b):
    return lax.dot_general(a, b, (((1,), (1,)), ((), ())), preferred_element_type=F32)


def weight_copies(place, own, other, buf, sem):
    nx, ny, rows = own.shape[0], own.shape[1], own.shape[2]
    me = place[1]
    copies = []
    for which, src in ((0, own), (1, other)):
        core = me if which == 0 else 1 - me
        for y in range(ny):
            for x in range(nx):
                at = ((y * nx + x) * 2 + core) * rows
                copies.append(
                    pltpu.make_async_copy(
                        src.at[x, y],
                        buf.at[pl.ds(pl.multiple_of(at, 16), rows), :],
                        sem.at[which, y * nx + x],
                    )
                )
    return copies


def norm_rows(x, gain):
    f = x.astype(F32)
    meansq = jnp.mean(f * f, axis=-1, keepdims=True)
    return (f * lax.rsqrt(meansq + 1e-06) * gain).astype(BF)


def kv_body(place, x_own, x_oth, gain, w_own, w_oth, kv, normed, buf, sem):
    copies = weight_copies(place, w_own, w_oth, buf, sem)
    for c in copies:
        c.start()
    rows = x_own.shape[0]
    side = place[0]
    g = gain[...]
    normed[pl.ds(pl.multiple_of(side * rows, 16), rows), :] = norm_rows(x_own[...], g)
    normed[pl.ds(pl.multiple_of((1 - side) * rows, 16), rows), :] = norm_rows(x_oth[...], g)
    for c in copies:
        c.wait()
    n = normed[...]
    kv[...] = jnp.dot(n, buf[...], preferred_element_type=F32).astype(BF)


def q_body(place, normed, w_own, w_oth, q, pooled, buf, sem):
    copies = weight_copies(place, w_own, w_oth, buf, sem)
    for c in copies:
        c.start()
    rows = normed.shape[0] // 2
    for c in copies:
        c.wait()
    own = normed[pl.ds(pl.multiple_of(place[0] * rows, 16), rows), :]
    second = jnp.dot(own, buf[:, : 2 * CP], preferred_element_type=F32)
    pooled[...] = second.reshape(rows // POOL, POOL, 2 * CP).mean(axis=1).astype(BF)
    q[...] = jnp.dot(normed[...], buf[:, 2 * CP :], preferred_element_type=F32).astype(BF)


def pair_body(pair_in, left, right, wt, pair_out, bias):
    r = right[...].astype(F32)
    w = wt[...]
    for i in range(pair_in.shape[0]):
        l = left[i : i + 1, :].astype(F32)
        out = (pair_in[i].astype(F32) + l * r).astype(BF)
        pair_out[i] = out
        both = nt(w, out)
        bias[i] = both[:8] + both[8:]


def split(x):
    hi = x.astype(BF)
    return hi, (x - hi.astype(F32)).astype(BF)


def attn_body(place, q, kvg, pb_own, pb_oth, mine, theirs):
    side = place[0]
    limit = place[2]
    nz, nrow = kvg.shape[0], kvg.shape[1]
    width = nz * nrow
    rows = nrow // 2
    half_bins = nz * rows
    npair = half_bins * 2 // POOL
    col = lax.broadcasted_iota(jnp.int32, (1, width), 1)
    z = col // nrow
    within = col % nrow
    bin_at = (within // rows) * half_bins + z * rows + within % rows
    live = bin_at < limit
    pair_at = bin_at // POOL
    onehot = (lax.broadcasted_iota(jnp.int32, (npair, width), 0) == pair_at).astype(F32).astype(BF)
    scale = 1.0 / (HD**0.5)
    own = pb_own[...]
    oth = pb_oth[...]
    for s in range(2):
        pb = jnp.where(side == s, own, oth)
        for h in range(HALF):
            qh = q[s * rows : (s + 1) * rows, h * HD : (h + 1) * HD]
            k = kvg[:, :, h * HD : (h + 1) * HD].reshape(width, HD)
            v = kvg[:, :, HW + h * HD : HW + (h + 1) * HD].reshape(width, HD)
            hi, lo = split(pb[:, h, :])
            bexp = jnp.dot(hi, onehot, preferred_element_type=F32) + jnp.dot(
                lo, onehot, preferred_element_type=F32
            )
            bexp = jnp.where(live, bexp, F32(-1e30))
            sc = nt(qh, k) * scale
            sc = (sc.reshape(rows // POOL, POOL, width) + bexp[:, None, :]).reshape(rows, width)
            top = jnp.max(sc, axis=-1, keepdims=True)
            e = jnp.exp(sc - top)
            total = jnp.sum(e, axis=-1, keepdims=True)
            acc = jnp.dot(e.astype(BF), v, preferred_element_type=F32)
            res = (acc / total).astype(BF)

            @pl.when(side == s)
            def _():
                mine[:, h * HD : (h + 1) * HD] = res

            @pl.when(side != s)
            def _():
                theirs[:, h * HD : (h + 1) * HD] = res


def out_body(place, x_own, a_own, a_oth, w_own, w_oth, mixed, buf, sem, full):
    copies = weight_copies(place, w_own, w_oth, buf, sem)
    for c in copies:
        c.start()
    side = place[0]
    full[:, pl.ds(pl.multiple_of(side * HW, 128), HW)] = a_own[...]
    full[:, pl.ds(pl.multiple_of((1 - side) * HW, 128), HW)] = a_oth[...]
    for c in copies:
        c.wait()
    update = nt(full[...], buf[...])
    mixed[...] = (x_own[...].astype(F32) + update).astype(BF)


def spread(x, axis, n):
    return lax.all_to_all(jnp.broadcast_to(x[None], (n,) + x.shape), axis, 0, 0, tiled=True)


def on_device(sizes, bins, pair_in, valid, gain, w_qkv, w_pair, w_bias, w_out):
    ny, nx, nz = sizes
    side = lax.axis_index("yh")
    core = lax.axis_index("c")
    swap = [(0, 1), (1, 0)]
    place = jnp.stack([side, core, valid[0]]).astype(jnp.int32)
    x_own = bins[0]
    rows, depth = x_own.shape
    shard = w_qkv.shape[0]
    x_oth = lax.ppermute(x_own, "yh", swap)

    def gather(w):
        w = spread(spread(w, "yl", ny), "x", nx)
        return w, lax.ppermute(w, "c", swap)

    def mine(first):
        return lax.dynamic_slice_in_dim(w_qkv, first * HEADS * HD + side * HW, HW, axis=1)

    kv_own, kv_oth = gather(jnp.concatenate([mine(1), mine(2)], axis=1))
    buf_sem = lambda n: [pltpu.VMEM((depth, n), BF), pltpu.SemaphoreType.DMA((2, nx * ny))]
    kv, normed = pl.pallas_call(
        kv_body,
        out_shape=(
            jax.ShapeDtypeStruct((2 * rows, 2 * HW), BF),
            jax.ShapeDtypeStruct((2 * rows, depth), BF),
        ),
        in_specs=[sm(), vm(), vm(), vm(), hbm(), hbm()],
        out_specs=(vm(), vm()),
        scratch_shapes=buf_sem(2 * HW),
        compiler_params=params(),
        name="kv",
    )(place, x_own, x_oth, gain[None], kv_own, kv_oth)
    kvg = lax.all_gather(kv, "z", axis=0)

    pq_own, pq_oth = gather(jnp.concatenate([w_pair, mine(0)], axis=1))
    q, pooled = pl.pallas_call(
        q_body,
        out_shape=(
            jax.ShapeDtypeStruct((2 * rows, HW), BF),
            jax.ShapeDtypeStruct((rows // POOL, 2 * CP), BF),
        ),
        in_specs=[sm(), vm(), hbm(), hbm()],
        out_specs=(vm(), vm()),
        scratch_shapes=buf_sem(2 * CP + HW),
        compiler_params=params(),
        name="q",
    )(place, normed, pq_own, pq_oth)
    right = spread(pooled[:, CP:], ("yh", "z"), 2 * nz).reshape(-1, CP)
    wt = w_bias.T
    zero = jnp.zeros((1, CP), F32)
    own_heads = lax.dynamic_slice_in_dim(wt, side * HALF, HALF, axis=0)
    oth_heads = lax.dynamic_slice_in_dim(wt, (1 - side) * HALF, HALF, axis=0)
    wt = jnp.concatenate([own_heads, zero, oth_heads, zero], axis=0)
    wt = jnp.concatenate(split(wt), axis=0)
    npr = pair_in.shape[1]
    pair_out, bias = pl.pallas_call(
        pair_body,
        out_shape=(
            jax.ShapeDtypeStruct(pair_in.shape[1:], BF),
            jax.ShapeDtypeStruct((npr, 8, pair_in.shape[2]), F32),
        ),
        in_specs=[vm()] * 4,
        out_specs=(vm(), vm()),
        compiler_params=params(),
        name="pair",
    )(pair_in[0], pooled[:, :CP], right, wt)
    pb_oth = lax.ppermute(bias[:, 4:], "yh", swap)

    wo_own, wo_oth = gather(w_out.T)
    mine_rows, their_rows = pl.pallas_call(
        attn_body,
        out_shape=(jax.ShapeDtypeStruct((rows, HW), BF),) * 2,
        in_specs=[sm(), vm(), vm(), vm(), vm()],
        out_specs=(vm(), vm()),
        compiler_params=params(),
        name="attn",
    )(place, q, kvg, bias[:, :4], pb_oth)
    got = lax.ppermute(their_rows, "yh", swap)
    mixed = pl.pallas_call(
        out_body,
        out_shape=jax.ShapeDtypeStruct((rows, depth), BF),
        in_specs=[sm(), vm(), vm(), vm(), hbm(), hbm()],
        out_specs=vm(),
        scratch_shapes=buf_sem(HEADS * HD) + [pltpu.VMEM((rows, HEADS * HD), BF)],
        compiler_params=params(),
        name="out",
    )(place, x_own, mine_rows, got, wo_own, wo_oth)
    return (mixed[None], pair_out[None])


def solution(mesh):
    fine = Mesh(mesh.devices.reshape(4, 4, 2, 2, 8), ("yl", "x", "c", "yh", "z"))
    dp, seq = ("yl", "x", "c"), ("yh", "z")
    placed = (
        P(dp, seq, None),
        P(dp, seq, None, None),
        P(dp),
        P(),
        P(dp, None),
        P(dp, None),
        P(),
        P(None, dp),
    )
    return jax.shard_map(
        functools.partial(on_device, (4, 4, 8)),
        mesh=fine,
        in_specs=placed,
        out_specs=(P(dp, seq, None), P(dp, seq, None, None)),
        check_vma=False,
    )
```

time: 323 us -> 212 us (0.66)
  the two profiles are of different devices: /device:TPU:1 before, /device:TPU:24 now
where the time goes in v1:
time: 212 us; the launch traced here: 211 us
  blocking collectives  71.5 us (34%)
  waiting for transfers between devices  59.4 us (28%)
  starting transfers between devices  34.5 us (16%)
  Pallas kernels  22 us (10%)
  between operations  15 us (7%)
  local copies, waits for them, and re-layouts  8.4 us (4%)
    all_to_all x5, blocking collectives, spread(): lax.all_to_all(jnp.broadcast_to(x[None], (n,) + x.shape), axis, 0, 0, til...  71.5 us
    all_to_all x2, waiting for transfers between devices, spread(): lax.all_to_all(jnp.broadcast_to(x[None], (n,) + x.shape), axis, 0, 0, til...  25.7 us
    ppermute x1, waiting for transfers between devices, on_device(): x_oth = lax.ppermute(x_own, 'yh', swap)  18.8 us
    all_to_all x2, starting transfers between devices, spread(): lax.all_to_all(jnp.broadcast_to(x[None], (n,) + x.shape), axis, 0, 0, til...  17.5 us
    ppermute x1, waiting for transfers between devices, on_device(): got = lax.ppermute(their_rows, 'yh', swap)  7.92 us
    ppermute x1, waiting for transfers between devices, on_device(): pb_oth = lax.ppermute(bias[:, 4:], 'yh', swap)  7.04 us
    ppermute x1, starting transfers between devices, on_device(): x_oth = lax.ppermute(x_own, 'yh', swap)  6.26 us
    pallas_call x1, Pallas kernels, on_device(): pl.pallas_call(attn_body, out_shape=(jax.ShapeDtypeStruct((rows, HW), BF)...  6 us
  transfers between devices with their start and end apart: 9, of which 5 were waited for; matrix products, arithmetic and copies ran while one was open for 1% of the time, Pallas kernels for 5%

profile of v1, /device:TPU:24, one launch (start us, length us, event | category | flops | bytes accessed | tf_op | source)
XLA Modules:
  0.0 211.0 jit_solution(16055254158104274140)
XLA Ops:
  7.2 0.8 constant_dynamic-slice_fusion
  8.1 13.2 %all_to_all.35 = bf16[4,48,768]{2,1,0:T(8,128)(2,1)S(1)} all-to-all(bf16[4,48,768]{2,1,0:T(8,128)(2,1)S(1)} %broadcast_in_dim.23), channel_id=1, replica_groups=mesh['yl'=4,'x'=4,'c'=2,'yh'=2,'z'=8] {'yl'}, dimensions={0} | all-to-all | bytes 589824 | tf_op jit(solution)/shard_map/all_to_all | solution.py:171
  21.4 18.9 %all_to_all.36.w_own = bf16[4,4,48,768]{3,2,1,0:T(8,128)(2,1)S(1)} all-to-all(bf16[4,4,48,768]{3,2,1,0:T(8,128)(2,1)S(1)} %broadcast_in_dim.24), channel_id=1, replica_groups=mesh['yl'=4,'x'=4,'c'=2,'yh'=2,'z'=8] {'x'}, dimensions={0} | all-to-all | bytes 2359296 | tf_op jit(solution)/shard_map/all_to_all | solution.py:171
  40.3 1.9 collective-permute-start.1
  42.2 6.3 %collective-permute-start = (bf16[128,1536]{1,0:T(8,128)(2,1)S(1)}, bf16[128,1536]{1,0:T(8,128)(2,1)S(1)}, u32[]{:S(2)}, u32[]{:S(2)}) collective-permute-start(bf16[128,1536]{1,0:T(8,128)(2,1)S(1)} %bitcast.14), channel_id=1, source_target_pairs={{0,8},{8,0},{1,9},{9,1},{2,10},{10,2},{3,11},{11,3},{4,12},{12,4},... | collective-permute-start | bytes 1179656 | tf_op jit(solution)/shard_map/ppermute | solution.py:183
  49.2 0.1 pad_add_fusion.place
  49.3 18.8 %collective-permute-done.x_oth = bf16[128,1536]{1,0:T(8,128)(2,1)S(1)} collective-permute-done((bf16[128,1536]{1,0:T(8,128)(2,1)S(1)}, bf16[128,1536]{1,0:T(8,128)(2,1)S(1)}, u32[]{:S(2)}, u32[]{:S(2)}) %collective-permute-start) | collective-permute-done | bytes 393248 | tf_op jit(solution)/shard_map/ppermute | solution.py:183
  68.0 5.4 %kv.1 = (bf16[256,768]{1,0:T(8,128)(2,1)}, bf16[256,1536]{1,0:T(8,128)(2,1)S(1)}) custom-call(s32[3]{0:T(128)S(1)} %pad_add_fusion.place, bf16[128,1536]{1,0:T(8,128)(2,1)S(1)} %bitcast.15, bf16[128,1536]{1,0:T(8,128)(2,1)S(1)} %collective-permute-done.x_oth, f32[1,1536]{1,0:T(1,128)S(1)} %broadcast_in_dim.22.gain, ...), custom_call_target="tpu_custom_call" | custom-call | tf_op jit(solution)/shard_map/kv/pallas_call | solution.py:194
  73.6 11.0 %all_to_all.37 = bf16[4,48,640]{2,1,0:T(8,128)(2,1)S(1)} all-to-all(bf16[4,48,640]{2,1,0:T(8,128)(2,1)S(1)} %broadcast_in_dim.25), channel_id=1, replica_groups=mesh['yl'=4,'x'=4,'c'=2,'yh'=2,'z'=8] {'yl'}, dimensions={0} | all-to-all | bytes 491520 | tf_op jit(solution)/shard_map/all_to_all | solution.py:171
  84.6 11.7 %all_to_all.38 = bf16[4,48,768]{2,1,0:T(8,128)(2,1)S(1)} all-to-all(bf16[4,48,768]{2,1,0:T(8,128)(2,1)S(1)} %broadcast_in_dim.29), channel_id=1, replica_groups=mesh['yl'=4,'x'=4,'c'=2,'yh'=2,'z'=8] {'yl'}, dimensions={0} | all-to-all | bytes 589824 | tf_op jit(solution)/shard_map/all_to_all | solution.py:171
  96.4 16.7 %all_to_all.39.w_own = bf16[4,4,48,640]{3,2,1,0:T(8,128)(2,1)S(1)} all-to-all(bf16[4,4,48,640]{3,2,1,0:T(8,128)(2,1)S(1)} %broadcast_in_dim.26), channel_id=1, replica_groups=mesh['yl'=4,'x'=4,'c'=2,'yh'=2,'z'=8] {'x'}, dimensions={0} | all-to-all | bytes 1966080 | tf_op jit(solution)/shard_map/all_to_all | solution.py:171
  113.1 1.1 broadcast_in_dim.30
  114.2 3.7 %all-to-all-start.6 = ((bf16[4,4,48,768]{3,2,1,0:T(8,128)(2,1)}), bf16[4,4,48,768]{3,2,1,0:T(8,128)(2,1)S(1)}, u32[]{:S(2)}, u32[]{:S(2)}) async-start(bf16[4,4,48,768]{3,2,1,0:T(8,128)(2,1)} %broadcast_in_dim.30), calls=%async_computation.6 | async-start | bytes 2359296 | tf_op jit(solution)/shard_map/all_to_all | solution.py:171
  117.9 1.9 collective-permute-start.2
  119.8 13.3 %all-to-all-done.6.w_own = bf16[4,4,48,768]{3,2,1,0:T(8,128)(2,1)S(1)} async-done(((bf16[4,4,48,768]{3,2,1,0:T(8,128)(2,1)}), bf16[4,4,48,768]{3,2,1,0:T(8,128)(2,1)S(1)}, u32[]{:S(2)}, u32[]{:S(2)}) %all-to-all-start.6) | async-done | bytes 1179680 | tf_op jit(solution)/shard_map/all_to_all | solution.py:171
  133.1 1.9 collective-permute-start.5
  135.1 1.1 copy-done.3
  136.2 4.5 %q.1 = (bf16[256,384]{1,0:T(8,128)(2,1)S(1)}, bf16[8,256]{1,0:T(8,128)(2,1)S(1)}) custom-call(s32[3]{0:T(128)S(1)} %pad_add_fusion.place, bf16[256,1536]{1,0:T(8,128)(2,1)S(1)} %copy-done.3, bf16[4,4,48,640]{3,2,1,0:T(8,128)(2,1)S(1)} %all_to_all.39.w_own, bf16[4,4,48,640]{3,2,1,0:T(8,128)(2,1)S(1)} %collective-permute-done.2.w_oth), custom_call_target="tpu_custom_call" | custom-call | tf_op jit(solution)/shard_map/q/pallas_call | solution.py:209
  140.7 0.7 copy-done.5
  141.4 0.6 broadcast_in_dim.27
  142.0 13.8 %all-to-all-start.4 = ((bf16[16,8,128]{2,1,0:T(8,128)(2,1)}), bf16[16,8,128]{2,1,0:T(8,128)(2,1)S(1)}, u32[]{:S(2)}, u32[]{:S(2)}) async-start(bf16[16,8,128]{2,1,0:T(8,128)(2,1)} %broadcast_in_dim.27), calls=%async_computation.4 | async-start | bytes 65536 | tf_op jit(solution)/shard_map/all_to_all | solution.py:171
  155.8 12.4 %all-to-all-done.4 = bf16[16,8,128]{2,1,0:T(8,128)(2,1)S(1)} async-done(((bf16[16,8,128]{2,1,0:T(8,128)(2,1)}), bf16[16,8,128]{2,1,0:T(8,128)(2,1)S(1)}, u32[]{:S(2)}, u32[]{:S(2)}) %all-to-all-start.4) | async-done | bytes 32800 | tf_op jit(solution)/shard_map/all_to_all | solution.py:171
  168.2 0.9 copy-done.4
  169.2 0.8 pair.1
  170.0 2.5 %collective-permute-start.3 = (f32[8,4,128]{2,1,0:T(4,128)S(1)}, f32[8,4,128]{2,1,0:T(4,128)S(1)}, u32[]{:S(2)}, u32[]{:S(2)}) collective-permute-start(f32[8,4,128]{2,1,0:T(4,128)S(1)} %get-tuple-element.21), channel_id=1, source_target_pairs={{0,8},{8,0},{1,9},{9,1},{2,10},{10,2},{3,11},{11,3},{4,12},{12,4},... | collective-permute-start | bytes 49160 | tf_op jit(solution)/shard_map/ppermute | solution.py:240
  172.5 7.0 %collective-permute-done.3.pb_oth = f32[8,4,128]{2,1,0:T(4,128)S(1)} collective-permute-done((f32[8,4,128]{2,1,0:T(4,128)S(1)}, f32[8,4,128]{2,1,0:T(4,128)S(1)}, u32[]{:S(2)}, u32[]{:S(2)}) %collective-permute-start.3) | collective-permute-done | bytes 16416 | tf_op jit(solution)/shard_map/ppermute | solution.py:240
  179.5 1.9 copy-done
  181.4 0.9 copy-done.6
  182.3 6.0 %attn.1 = (bf16[128,384]{1,0:T(8,128)(2,1)S(1)}, bf16[128,384]{1,0:T(8,128)(2,1)S(1)}) custom-call(s32[3]{0:T(128)S(1)} %pad_add_fusion.place, bf16[256,384]{1,0:T(8,128)(2,1)S(1)} %copy-done.6, bf16[8,256,768]{2,1,0:T(8,128)(2,1)S(1)} %bitcast.13, f32[8,4,128]{2,1,0:T(4,128)S(1)} %get-tuple-element.22.pb_own, f32[8,4,128]{2,1,0:T(4,128)S(1)} %collective-permute-done.3.pb_oth), custom_call_target="tpu_custom_call" | custom-call | tf_op jit(solution)/shard_map/attn/pallas_call | solution.py:243
  188.3 2.5 %collective-permute-start.4 = (bf16[128,384]{1,0:T(8,128)(2,1)S(1)}, bf16[128,384]{1,0:T(8,128)(2,1)S(1)}, u32[]{:S(2)}, u32[]{:S(2)}) collective-permute-start(bf16[128,384]{1,0:T(8,128)(2,1)S(1)} %get-tuple-element.16), channel_id=1, source_target_pairs={{0,8},{8,0},{1,9},{9,1},{2,10},{10,2},{3,11},{11,3},{4,12},{12,4},... | collective-permute-start | bytes 294920 | tf_op jit(solution)/shard_map/ppermute | solution.py:251
  190.8 7.9 %collective-permute-done.4.a_oth = bf16[128,384]{1,0:T(8,128)(2,1)S(1)} collective-permute-done((bf16[128,384]{1,0:T(8,128)(2,1)S(1)}, bf16[128,384]{1,0:T(8,128)(2,1)S(1)}, u32[]{:S(2)}, u32[]{:S(2)}) %collective-permute-start.4) | collective-permute-done | bytes 98336 | tf_op jit(solution)/shard_map/ppermute | solution.py:251
  198.7 5.4 %out.1 = bf16[128,1536]{1,0:T(8,128)(2,1)} custom-call(s32[3]{0:T(128)S(1)} %pad_add_fusion.place, bf16[128,1536]{1,0:T(8,128)(2,1)S(1)} %bitcast.16, bf16[128,384]{1,0:T(8,128)(2,1)S(1)} %get-tuple-element.15.a_own, bf16[128,384]{1,0:T(8,128)(2,1)S(1)} %collective-permute-done.4.a_oth, bf16[4,4,48,768]{3,2,1,0:T(8,128)(2,1)S(1)} %all-to-all-done.6.w_own, ...), custom_call_target="tpu_custom_call" | custom-call | tf_op jit(solution)/shard_map/out/pallas_call | solution.py:252
  (38 shorter events, 0.4 us)
Async XLA Ops:
  7.2 172.3 %all-gather.3.cloned.1.call-start = ((), (), s32[]{:S(2)}) async-start(), calls=%async_computation.7 | async-start | bytes 3538944 | tf_op jit(solution)/shard_map/all_gather | solution.py:206
  21.4 20.8 %copy-start.1 = (bf16[1,128,1536]{2,1,0:T(8,128)(2,1)S(1)}, bf16[1,128,1536]{2,1,0:T(8,128)(2,1)}, u32[]{:S(2)}) copy-start(bf16[1,128,1536]{2,1,0:T(8,128)(2,1)} %param.8) | copy-start | bytes 1179652
  21.4 27.7 %copy-start.9 = (f32[1536]{0:T(1024)S(1)}, f32[1536]{0:T(1024)}, u32[]{:S(2)}) copy-start(f32[1536]{0:T(1024)} %param.11) | copy-start | bytes 18436
  40.3 27.7 %collective-permute-start.1 = (bf16[4,4,48,768]{3,2,1,0:T(8,128)(2,1)S(1)}, bf16[4,4,48,768]{3,2,1,0:T(8,128)(2,1)}, u32[]{:S(2)}, u32[]{:S(2)}) collective-permute-start(bf16[4,4,48,768]{3,2,1,0:T(8,128)(2,1)S(1)} %all_to_all.36.w_own), channel_id=1, source_target_pairs={{0,16},{16,0},{1,17},{17,1},{2,18},{18,2},{3,19},{19,3},{4,20},{20... | collective-permute-start | bytes 3538952 | tf_op jit(solution)/shard_map/ppermute | solution.py:187
  42.2 25.8 %collective-permute-start = (bf16[128,1536]{1,0:T(8,128)(2,1)S(1)}, bf16[128,1536]{1,0:T(8,128)(2,1)S(1)}, u32[]{:S(2)}, u32[]{:S(2)}) collective-permute-start(bf16[128,1536]{1,0:T(8,128)(2,1)S(1)} %bitcast.14), channel_id=1, source_target_pairs={{0,8},{8,0},{1,9},{9,1},{2,10},{10,2},{3,11},{11,3},{4,12},{12,4},... | collective-permute-start | bytes 1179656 | tf_op jit(solution)/shard_map/ppermute | solution.py:183
  49.3 24.3 %copy-start.8 = (bf16[48,256]{1,0:T(8,128)(2,1)S(1)}, bf16[48,256]{1,0:T(8,128)(2,1)}, u32[]{:S(2)}) copy-start(bf16[48,256]{1,0:T(8,128)(2,1)} %param.13) | copy-start | bytes 73732
  73.5 22.8 %copy-start.2 = (bf16[256,1536]{1,0:T(8,128)(2,1)}, bf16[256,1536]{1,0:T(8,128)(2,1)S(1)}, u32[]{:S(2)}) copy-start(bf16[256,1536]{1,0:T(8,128)(2,1)S(1)} %get-tuple-element.10.normed) | copy-start | bytes 2359300
  73.5 11.1 %copy-start.7 = (bf16[768,48]{0,1:T(8,128)(2,1)S(1)}, bf16[768,48]{0,1:T(8,128)(2,1)}, u32[]{:S(2)}) copy-start(bf16[768,48]{0,1:T(8,128)(2,1)} %param.15) | copy-start | bytes 221188
  114.2 20.8 %copy-start.10 = (f32[128,6]{0,1:T(8,128)S(1)}, f32[128,6]{0,1:T(8,128)}, u32[]{:S(2)}) copy-start(f32[128,6]{0,1:T(8,128)} %param.14) | copy-start | bytes 9220
  114.2 18.9 %all-to-all-start.6 = ((bf16[4,4,48,768]{3,2,1,0:T(8,128)(2,1)}), bf16[4,4,48,768]{3,2,1,0:T(8,128)(2,1)S(1)}, u32[]{:S(2)}, u32[]{:S(2)}) async-start(bf16[4,4,48,768]{3,2,1,0:T(8,128)(2,1)} %broadcast_in_dim.30), calls=%async_computation.6 | async-start | bytes 2359296 | tf_op jit(solution)/shard_map/all_to_all | solution.py:171
  117.9 17.2 %collective-permute-start.2 = (bf16[4,4,48,640]{3,2,1,0:T(8,128)(2,1)S(1)}, bf16[4,4,48,640]{3,2,1,0:T(8,128)(2,1)S(1)}, u32[]{:S(2)}, u32[]{:S(2)}) collective-permute-start(bf16[4,4,48,640]{3,2,1,0:T(8,128)(2,1)S(1)} %all_to_all.39.w_own), channel_id=1, source_target_pairs={{0,16},{16,0},{1,17},{17,1},{2,18},{18,2},{3,19},{19,3},{4,20},{20... | collective-permute-start | bytes 2949128 | tf_op jit(solution)/shard_map/ppermute | solution.py:187
  133.1 57.7 %collective-permute-start.5 = (bf16[4,4,48,768]{3,2,1,0:T(8,128)(2,1)S(1)}, bf16[4,4,48,768]{3,2,1,0:T(8,128)(2,1)}, u32[]{:S(2)}, u32[]{:S(2)}) collective-permute-start(bf16[4,4,48,768]{3,2,1,0:T(8,128)(2,1)S(1)} %all-to-all-done.6.w_own), channel_id=1, source_target_pairs={{0,16},{16,0},{1,17},{17,1},{2,18},{18,2},{3,19},{19,3},{4,20},{20... | collective-permute-start | bytes 3538952 | tf_op jit(solution)/shard_map/ppermute | solution.py:187
  135.1 1.1 copy-start.3
  140.7 0.7 copy-start.5
  142.0 26.2 %all-to-all-start.4 = ((bf16[16,8,128]{2,1,0:T(8,128)(2,1)}), bf16[16,8,128]{2,1,0:T(8,128)(2,1)S(1)}, u32[]{:S(2)}, u32[]{:S(2)}) async-start(bf16[16,8,128]{2,1,0:T(8,128)(2,1)} %broadcast_in_dim.27), calls=%async_computation.4 | async-start | bytes 65536 | tf_op jit(solution)/shard_map/all_to_all | solution.py:171
  168.2 1.0 copy-start.4
  170.0 9.5 %collective-permute-start.3 = (f32[8,4,128]{2,1,0:T(4,128)S(1)}, f32[8,4,128]{2,1,0:T(4,128)S(1)}, u32[]{:S(2)}, u32[]{:S(2)}) collective-permute-start(f32[8,4,128]{2,1,0:T(4,128)S(1)} %get-tuple-element.21), channel_id=1, source_target_pairs={{0,8},{8,0},{1,9},{9,1},{2,10},{10,2},{3,11},{11,3},{4,12},{12,4},... | collective-permute-start | bytes 49160 | tf_op jit(solution)/shard_map/ppermute | solution.py:240
  179.5 1.9 copy-start
  181.4 0.9 copy-start.6
  188.3 10.4 %collective-permute-start.4 = (bf16[128,384]{1,0:T(8,128)(2,1)S(1)}, bf16[128,384]{1,0:T(8,128)(2,1)S(1)}, u32[]{:S(2)}, u32[]{:S(2)}) collective-permute-start(bf16[128,384]{1,0:T(8,128)(2,1)S(1)} %get-tuple-element.16), channel_id=1, source_target_pairs={{0,8},{8,0},{1,9},{9,1},{2,10},{10,2},{3,11},{11,3},{4,12},{12,4},... | collective-permute-start | bytes 294920 | tf_op jit(solution)/shard_map/ppermute | solution.py:251
Sparse Core Ops, SparseCore 0:
  73.6 49.5 all-gather.2

commit v2 on v1

v2 whole, which is shorter than its diff:
```python
import functools

import jax
import jax.numpy as jnp
from jax import lax
from jax.experimental import pallas as pl
from jax.experimental.pallas import tpu as pltpu
from jax.sharding import Mesh, PartitionSpec as P

HEADS = 6
HD = 128
CP = 128
POOL = 16
HALF = HEADS // 2
HW = HALF * HD
VMEM = 48 * 1024 * 1024

BF = jnp.bfloat16
F32 = jnp.float32

AXES = ("yl", "xh", "xl", "c", "yh", "zh", "zl")
SIZES = (4, 2, 2, 2, 2, 4, 2)
DP, X, SEQ = AXES[:4], AXES[1:3], AXES[4:]
NY, NX = 4, 4


def params():
    return pltpu.CompilerParams(vmem_limit_bytes=VMEM)


def vm():
    return pl.BlockSpec(memory_space=pltpu.VMEM)


def sm():
    return pl.BlockSpec(memory_space=pltpu.SMEM)


def hbm():
    return pl.BlockSpec(memory_space=pl.ANY)


def nt(a, b):
    return lax.dot_general(a, b, (((1,), (1,)), ((), ())), preferred_element_type=F32)


def split(x):
    hi = x.astype(BF)
    return hi, (x - hi.astype(F32)).astype(BF)


def weight_copies(place, own, other, buf, sem, across):
    rows = own.shape[2]
    me = place[1]
    copies = []
    for which, src in ((0, own), (1, other)):
        core = me if which == 0 else 1 - me
        for y in range(NY):
            for x in range(NX):
                at = ((y * NX + x) * 2 + core) * rows
                copies.append(
                    pltpu.make_async_copy(
                        src.at[x, y] if across else src.at[y, x],
                        buf.at[pl.ds(pl.multiple_of(at, 16), rows), :],
                        sem.at[which, y * NX + x],
                    )
                )
    return copies


def norm_rows(x, gain):
    f = x.astype(F32)
    meansq = jnp.mean(f * f, axis=-1, keepdims=True)
    return (f * lax.rsqrt(meansq + 1e-06) * gain).astype(BF)


def norm_body(place, x_own, near, far, gain, normed, means):
    rows, depth = x_own.shape
    side = place[0]
    g = gain[...]
    n = norm_rows(x_own[...], g).astype(F32)
    hi, lo = split(n.reshape(rows // POOL, POOL, depth).mean(axis=1))
    means[...] = jnp.concatenate([hi, lo], axis=0)
    normed[pl.ds(pl.multiple_of(side * rows, 16), rows), :] = norm_rows(near[...], g)
    normed[pl.ds(pl.multiple_of((1 - side) * rows, 16), rows), :] = norm_rows(far[...], g)


def kv_body(place, normed, means, w_own, w_oth, kv, pooled, buf, sem):
    copies = weight_copies(place, w_own, w_oth, buf, sem, True)
    for c in copies:
        c.start()
    for c in copies:
        c.wait()
    kv[...] = jnp.dot(normed[...], buf[:, : 2 * HW], preferred_element_type=F32).astype(BF)
    both = jnp.dot(means[...], buf[:, 2 * HW :], preferred_element_type=F32)
    n = both.shape[0] // 2
    pooled[...] = (both[:n] + both[n:]).astype(BF)


def q_body(place, normed, w_own, w_oth, q, buf, sem):
    copies = weight_copies(place, w_own, w_oth, buf, sem, False)
    for c in copies:
        c.start()
    for c in copies:
        c.wait()
    q[...] = jnp.dot(normed[...], buf[...], preferred_element_type=F32).astype(BF)


def pair_body(place, pair_in, left, right, wt, pair_out, bias):
    r = right[...].astype(F32)
    w = wt[...]
    limit = place[2].astype(F32)
    row = lax.broadcasted_iota(jnp.int32, (8, r.shape[0]), 0)
    spare = (row == 3) | (row == 7)
    for i in range(pair_in.shape[0]):
        l = left[i : i + 1, :].astype(F32)
        out = (pair_in[i].astype(F32) + l * r).astype(BF)
        pair_out[i] = out
        both = nt(w, out)
        bias[i] = jnp.where(spare, limit, both[:8] + both[8:])


def attn_body(place, q, kv_own, kv_oth, pb_near, pb_far, near, far):
    side = place[0]
    core = place[1]
    nchip, nrow = kv_own.shape[0], kv_own.shape[1]
    width = nchip * nrow
    rows = nrow // 2
    half_bins = 2 * nchip * rows
    npair = half_bins * 2 // POOL
    limit = pb_near[0:1, 3, 0:1]
    scale = 1.0 / (HD**0.5)

    col = lax.broadcasted_iota(jnp.int32, (1, width), 1)
    chip = col // nrow
    within = col % nrow
    pairs = lax.broadcasted_iota(jnp.int32, (npair, width), 0)
    live, onehot = [], []
    for cc in (core, 1 - core):
        z = (chip // 2) * 4 + cc * 2 + chip % 2
        bin_at = (within // rows) * half_bins + z * rows + within % rows
        live.append(bin_at.astype(F32) < limit)
        onehot.append((pairs == bin_at // POOL).astype(F32).astype(BF))
    pbn = pb_near[...]
    pbf = pb_far[...]
    for s in range(2):
        pb = jnp.where(side == s, pbn, pbf)
        for h in range(HALF):
            qh = q[s * rows : (s + 1) * rows, h * HD : (h + 1) * HD]
            hi, lo = split(pb[:, h, :])
            scores = []
            for kv, ok, hot in ((kv_own, live[0], onehot[0]), (kv_oth, live[1], onehot[1])):
                k = kv[:, :, h * HD : (h + 1) * HD].reshape(width, HD)
                bexp = jnp.dot(hi, hot, preferred_element_type=F32) + jnp.dot(
                    lo, hot, preferred_element_type=F32
                )
                bexp = jnp.where(ok, bexp, F32(-1e30))
                sc = nt(qh, k) * scale
                sc = sc.reshape(rows // POOL, POOL, width) + bexp[:, None, :]
                scores.append(sc.reshape(rows, width))
            top = jnp.maximum(
                jnp.max(scores[0], axis=-1, keepdims=True),
                jnp.max(scores[1], axis=-1, keepdims=True),
            )
            total, acc = 0.0, 0.0
            for sc, kv in zip(scores, (kv_own, kv_oth)):
                v = kv[:, :, HW + h * HD : HW + (h + 1) * HD].reshape(width, HD)
                e = jnp.exp(sc - top)
                total += jnp.sum(e, axis=-1, keepdims=True)
                acc += jnp.dot(e.astype(BF), v, preferred_element_type=F32)
            res = (acc / total).astype(BF)

            @pl.when(side == s)
            def _():
                near[:, h * HD : (h + 1) * HD] = res

            @pl.when(side != s)
            def _():
                far[:, h * HD : (h + 1) * HD] = res


def out_body(place, x_own, a_near, a_far, w_own, w_oth, mixed, buf, sem, full):
    copies = weight_copies(place, w_own, w_oth, buf, sem, False)
    for c in copies:
        c.start()
    side = place[0]
    full[:, pl.ds(pl.multiple_of(side * HW, 128), HW)] = a_near[...]
    full[:, pl.ds(pl.multiple_of((1 - side) * HW, 128), HW)] = a_far[...]
    for c in copies:
        c.wait()
    update = nt(full[...], buf[...])
    mixed[...] = (x_own[...].astype(F32) + update).astype(BF)


def spread(x, axis, n):
    return lax.all_to_all(jnp.broadcast_to(x[None], (n,) + x.shape), axis, 0, 0, tiled=True)


def core_swap(x):
    return lax.ppermute(x, "c", [(0, 1), (1, 0)])


def relocate(x, flip):
    moves = []
    for xl in range(2):
        for c in range(2):
            for yh in range(2):
                for zh in range(4):
                    here = ((xl * 2 + c) * 2 + yh) * 4 + zh
                    there = ((zh // 2 * 2 + zh % 2) * 2 + (yh ^ flip)) * 4 + xl * 2 + c
                    moves.append((here, there))
    return lax.ppermute(x, ("xl", "c", "yh", "zh"), moves)


def after(x, *others):
    return lax.optimization_barrier((x,) + others)[0]


def on_device(bins, pair_in, valid, gain, w_qkv, w_pair, w_bias, w_out):
    side = lax.axis_index("yh")
    core = lax.axis_index("c")
    place = jnp.stack([side, core, valid[0]]).astype(jnp.int32)
    x_own = bins[0]
    rows, depth = x_own.shape

    def mine(first):
        return lax.dynamic_slice_in_dim(w_qkv, first * HEADS * HD + side * HW, HW, axis=1)

    def weights(n):
        return [pltpu.VMEM((depth, n), BF), pltpu.SemaphoreType.DMA((2, NX * NY))]

    x_near = relocate(x_own, 0)
    x_far = relocate(x_own, 1)
    w = jnp.concatenate([mine(1), mine(2), w_pair], axis=1)
    w = spread(spread(w, "yl", NY), X, NX)
    normed, means = pl.pallas_call(
        norm_body,
        out_shape=(
            jax.ShapeDtypeStruct((2 * rows, depth), BF),
            jax.ShapeDtypeStruct((2 * rows // POOL, depth), BF),
        ),
        in_specs=[sm(), vm(), vm(), vm(), vm()],
        out_specs=(vm(), vm()),
        compiler_params=params(),
        name="norm",
    )(place, x_own, x_near, x_far, gain[None])
    w = after(w, normed)
    w_oth = core_swap(w)
    q_own = spread(after(mine(0), w), ("yl",) + X, NY * NX).reshape(NY, NX, -1, HW)
    kv, pooled = pl.pallas_call(
        kv_body,
        out_shape=(
            jax.ShapeDtypeStruct((2 * rows, 2 * HW), BF),
            jax.ShapeDtypeStruct((rows // POOL, 2 * CP), BF),
        ),
        in_specs=[sm(), vm(), vm(), hbm(), hbm()],
        out_specs=(vm(), vm()),
        scratch_shapes=weights(2 * HW + 2 * CP),
        compiler_params=params(),
        name="kv",
    )(place, normed, means, w, w_oth)
    kv_own = spread(kv, ("xl", "zl"), 4)
    right = spread(pooled[:, CP:], SEQ, 16).reshape(-1, CP)

    q_own = after(q_own, kv)
    q_oth = core_swap(q_own)
    q = pl.pallas_call(
        q_body,
        out_shape=jax.ShapeDtypeStruct((2 * rows, HW), BF),
        in_specs=[sm(), vm(), hbm(), hbm()],
        out_specs=vm(),
        scratch_shapes=weights(HW),
        compiler_params=params(),
        name="q",
    )(place, normed, q_own, q_oth)

    wt = w_bias.T
    zero = jnp.zeros((1, CP), F32)
    own_heads = lax.dynamic_slice_in_dim(wt, side * HALF, HALF, axis=0)
    oth_heads = lax.dynamic_slice_in_dim(wt, (1 - side) * HALF, HALF, axis=0)
    wt = jnp.concatenate([own_heads, zero, oth_heads, zero], axis=0)
    wt = jnp.concatenate(split(wt), axis=0)
    npr = pair_in.shape[1]
    pair_out, bias = pl.pallas_call(
        pair_body,
        out_shape=(
            jax.ShapeDtypeStruct(pair_in.shape[1:], BF),
            jax.ShapeDtypeStruct((npr, 8, pair_in.shape[2]), F32),
        ),
        in_specs=[sm()] + [vm()] * 4,
        out_specs=(vm(), vm()),
        compiler_params=params(),
        name="pair",
    )(place, pair_in[0], pooled[:, :CP], right, wt)
    pb_near = relocate(bias[:, :4], 0)
    pb_far = relocate(bias[:, 4:], 1)

    wo = after(w_out.T, q_own)
    wo = spread(wo, ("yl",) + X, NY * NX).reshape(NY, NX, -1, HEADS * HD)
    kv_oth = core_swap(kv_own)
    near, far = pl.pallas_call(
        attn_body,
        out_shape=(jax.ShapeDtypeStruct((rows, HW), BF),) * 2,
        in_specs=[sm()] + [vm()] * 5,
        out_specs=(vm(), vm()),
        compiler_params=params(),
        name="attn",
    )(place, q, kv_own, kv_oth, pb_near, pb_far)
    a_near = relocate(near, 0)
    a_far = relocate(far, 1)
    wo_oth = core_swap(wo)
    mixed = pl.pallas_call(
        out_body,
        out_shape=jax.ShapeDtypeStruct((rows, depth), BF),
        in_specs=[sm(), vm(), vm(), vm(), hbm(), hbm()],
        out_specs=vm(),
        scratch_shapes=weights(HEADS * HD) + [pltpu.VMEM((rows, HEADS * HD), BF)],
        compiler_params=params(),
        name="out",
    )(place, x_own, a_near, a_far, wo, wo_oth)
    return (mixed[None], pair_out[None])


def solution(mesh):
    fine = Mesh(mesh.devices.reshape(SIZES), AXES)
    placed = (
        P(DP, SEQ, None),
        P(DP, SEQ, None, None),
        P(DP),
        P(),
        P(DP, None),
        P(DP, None),
        P(),
        P(None, DP),
    )
    return jax.shard_map(
        on_device,
        mesh=fine,
        in_specs=placed,
        out_specs=(P(DP, SEQ, None), P(DP, SEQ, None, None)),
        check_vma=False,
    )
```

time: 212 us -> 243 us (1.15)
  the two profiles are of different devices: /device:TPU:24 before, /device:TPU:14 now
where the time goes in v2:
time: 243 us; the launch traced here: 242 us
  waiting for transfers between devices  103 us (42%)
  starting transfers between devices  86.1 us (35%)
  Pallas kernels  23.6 us (10%)
  blocking collectives  15 us (6%)
  local copies, waits for them, and re-layouts  10.3 us (4%)
    all_to_all x5, waiting for transfers between devices, spread(): lax.all_to_all(jnp.broadcast_to(x[None], (n,) + x.shape), axis, 0, 0, til...  64.1 us
    ppermute x6, starting transfers between devices, relocate(): return lax.ppermute(x, ('xl', 'c', 'yh', 'zh'), moves)  39.1 us
    ppermute x6, waiting for transfers between devices, relocate(): return lax.ppermute(x, ('xl', 'c', 'yh', 'zh'), moves)  39 us
    all_to_all x5, starting transfers between devices, spread(): lax.all_to_all(jnp.broadcast_to(x[None], (n,) + x.shape), axis, 0, 0, til...  33.9 us
    all_to_all x1, blocking collectives, spread(): lax.all_to_all(jnp.broadcast_to(x[None], (n,) + x.shape), axis, 0, 0, til...  15 us
    ppermute x4, starting transfers between devices, core_swap(): return lax.ppermute(x, 'c', [(0, 1), (1, 0)])  13.1 us
    pallas_call x1, Pallas kernels, on_device(): pl.pallas_call(attn_body, out_shape=(jax.ShapeDtypeStruct((rows, HW), BF)...  6.92 us
    broadcast_in_dim x6, local copies, waits for them, and re-layouts, spread(): jnp.broadcast_to(x[None], (n,) + x.shape)  6.14 us
  transfers between devices with their start and end apart: 15, of which 8 were waited for; matrix products, arithmetic and copies ran while one was open for 2% of the time, Pallas kernels for 8%

profile of v2, /device:TPU:14, one launch (start us, length us, event | category | flops | bytes accessed | tf_op | source)
XLA Modules:
  0.0 241.7 jit_solution(9069528893944324431)
XLA Ops:
  0.6 1.4 constant_dynamic-slice_fusion.1
  2.9 15.0 %all_to_all.30 = bf16[4,48,1024]{2,1,0:T(8,128)(2,1)S(1)} all-to-all(bf16[4,48,1024]{2,1,0:T(8,128)(2,1)S(1)} %broadcast_in_dim.21), channel_id=1, replica_groups=mesh['yl'=4,'xh'=2,'xl'=2,'c'=2,'yh'=2,'zh'=4,'zl'=2] {'yl'}, dimensions={0} | all-to-all | bytes 786432 | tf_op jit(solution)/shard_map/all_to_all | solution.py:196
  17.9 1.4 broadcast_in_dim.22
  19.2 4.9 %all-to-all-start.1 = ((bf16[4,4,48,1024]{3,2,1,0:T(8,128)(2,1)}), bf16[4,4,48,1024]{3,2,1,0:T(8,128)(2,1)S(1)}, u32[]{:S(2)}, u32[]{:S(2)}) async-start(bf16[4,4,48,1024]{3,2,1,0:T(8,128)(2,1)} %broadcast_in_dim.22), calls=%async_computation.1 | async-start | bytes 3145728 | tf_op jit(solution)/shard_map/all_to_all | solution.py:196
  24.1 11.2 %collective-permute-start = (bf16[128,1536]{1,0:T(8,128)(2,1)S(1)}, bf16[128,1536]{1,0:T(8,128)(2,1)S(1)}, u32[]{:S(2)}, u32[]{:S(2)}) collective-permute-start(bf16[128,1536]{1,0:T(8,128)(2,1)S(1)} %bitcast.18), channel_id=1, source_target_pairs={{0,0},{2,16},{4,32},{6,48},{8,8},{10,24},{12,40},{14,56},{16,2},{1... | collective-permute-start | bytes 1179656 | tf_op jit(solution)/shard_map/ppermute | solution.py:212
  35.4 5.2 %collective-permute-start.1 = (bf16[128,1536]{1,0:T(8,128)(2,1)S(1)}, bf16[128,1536]{1,0:T(8,128)(2,1)S(1)}, u32[]{:S(2)}, u32[]{:S(2)}) collective-permute-start(bf16[128,1536]{1,0:T(8,128)(2,1)S(1)} %bitcast.19), channel_id=1, source_target_pairs={{0,8},{2,24},{4,40},{6,56},{8,0},{10,16},{12,32},{14,48},{16,10},{... | collective-permute-start | bytes 1179656 | tf_op jit(solution)/shard_map/ppermute | solution.py:212
  41.4 23.0 %collective-permute-done.1.far = bf16[128,1536]{1,0:T(8,128)(2,1)S(1)} collective-permute-done((bf16[128,1536]{1,0:T(8,128)(2,1)S(1)}, bf16[128,1536]{1,0:T(8,128)(2,1)S(1)}, u32[]{:S(2)}, u32[]{:S(2)}) %collective-permute-start.1) | collective-permute-done | bytes 393248 | tf_op jit(solution)/shard_map/ppermute | solution.py:212
  66.2 6.9 %collective-permute-start.2 = (bf16[4,4,48,1024]{3,2,1,0:T(8,128)(2,1)S(1)}, bf16[4,4,48,1024]{3,2,1,0:T(8,128)(2,1)}, u32[]{:S(2)}, u32[]{:S(2)}) collective-permute-start(bf16[4,4,48,1024]{3,2,1,0:T(8,128)(2,1)S(1)} %all-to-all-done.1.w_own), channel_id=1, source_target_pairs={{0,16},{16,0},{1,17},{17,1},{2,18},{18,2},{3,19},{19,3},{4,20},{20... | collective-permute-start | bytes 4718600 | tf_op jit(solution)/shard_map/ppermute | solution.py:200
  73.1 1.6 broadcast_in_dim.23
  74.8 13.5 %all-to-all-start.2 = ((bf16[16,48,384]{2,1,0:T(8,128)(2,1)}), bf16[16,48,384]{2,1,0:T(8,128)(2,1)S(1)}, u32[]{:S(2)}, u32[]{:S(2)}) async-start(bf16[16,48,384]{2,1,0:T(8,128)(2,1)} %broadcast_in_dim.23), calls=%async_computation.2 | async-start | bytes 1179648 | tf_op jit(solution)/shard_map/all_to_all | solution.py:196
  88.3 5.3 %kv.1 = (bf16[256,768]{1,0:T(8,128)(2,1)S(1)}, bf16[8,256]{1,0:T(8,128)(2,1)S(1)}) custom-call(s32[3]{0:T(128)S(1)} %pad_add_fusion.place, bf16[256,1536]{1,0:T(8,128)(2,1)S(1)} %get-tuple-element.14.normed, bf16[16,1536]{1,0:T(8,128)(2,1)S(1)} %copy-done.6, bf16[4,4,48,1024]{3,2,1,0:T(8,128)(2,1)S(1)} %all-to-all-done.1.w_own, ...), custom_call_target="tpu_custom_call" | custom-call | tf_op jit(solution)/shard_map/kv/pallas_call | solution.py:250
  93.6 9.6 %all-to-all-done.2 = bf16[16,48,384]{2,1,0:T(8,128)(2,1)S(1)} async-done(((bf16[16,48,384]{2,1,0:T(8,128)(2,1)}), bf16[16,48,384]{2,1,0:T(8,128)(2,1)S(1)}, u32[]{:S(2)}, u32[]{:S(2)}) %all-to-all-start.2) | async-done | bytes 589856 | tf_op jit(solution)/shard_map/all_to_all | solution.py:196
  103.2 1.4 broadcast_in_dim.24
  104.5 5.0 %all-to-all-start.3 = ((bf16[4,256,768]{2,1,0:T(8,128)(2,1)}), bf16[4,256,768]{2,1,0:T(8,128)(2,1)S(1)}, u32[]{:S(2)}, u32[]{:S(2)}) async-start(bf16[4,256,768]{2,1,0:T(8,128)(2,1)} %broadcast_in_dim.24), calls=%async_computation.3 | async-start | bytes 3145728 | tf_op jit(solution)/shard_map/all_to_all | solution.py:196
  109.6 18.3 %all-to-all-done.3.kv_own = bf16[4,256,768]{2,1,0:T(8,128)(2,1)S(1)} async-done(((bf16[4,256,768]{2,1,0:T(8,128)(2,1)}), bf16[4,256,768]{2,1,0:T(8,128)(2,1)S(1)}, u32[]{:S(2)}, u32[]{:S(2)}) %all-to-all-start.3) | async-done | bytes 1572896 | tf_op jit(solution)/shard_map/all_to_all | solution.py:196
  128.9 6.0 %all-to-all-start.5 = ((bf16[16,48,768]{2,1,0:T(8,128)(2,1)}), bf16[16,48,768]{2,1,0:T(8,128)(2,1)S(1)}, u32[]{:S(2)}, u32[]{:S(2)}) async-start(bf16[16,48,768]{2,1,0:T(8,128)(2,1)} %broadcast_in_dim.27), calls=%async_computation.5 | async-start | bytes 2359296 | tf_op jit(solution)/shard_map/all_to_all | solution.py:196
  134.9 1.9 collective-permute-start.4
  136.8 24.4 %all-to-all-done.5 = bf16[16,48,768]{2,1,0:T(8,128)(2,1)S(1)} async-done(((bf16[16,48,768]{2,1,0:T(8,128)(2,1)}), bf16[16,48,768]{2,1,0:T(8,128)(2,1)S(1)}, u32[]{:S(2)}, u32[]{:S(2)}) %all-to-all-start.5) | async-done | bytes 1179680 | tf_op jit(solution)/shard_map/all_to_all | solution.py:196
  161.3 1.9 collective-permute-start.9
  163.3 2.4 collective-permute-start.3
  166.9 4.5 %all-to-all-start.4 = ((bf16[16,8,128]{2,1,0:T(8,128)(2,1)}), bf16[16,8,128]{2,1,0:T(8,128)(2,1)}, u32[]{:S(2)}, u32[]{:S(2)}) async-start(bf16[16,8,128]{2,1,0:T(8,128)(2,1)} %broadcast_in_dim.25), calls=%async_computation.4 | async-start | bytes 65536 | tf_op jit(solution)/shard_map/all_to_all | solution.py:196
  172.0 11.8 %all-to-all-done.4 = bf16[16,8,128]{2,1,0:T(8,128)(2,1)} async-done(((bf16[16,8,128]{2,1,0:T(8,128)(2,1)}), bf16[16,8,128]{2,1,0:T(8,128)(2,1)}, u32[]{:S(2)}, u32[]{:S(2)}) %all-to-all-start.4) | async-done | bytes 32800 | tf_op jit(solution)/shard_map/all_to_all | solution.py:196
  184.8 1.5 pair.1
  186.3 3.3 %collective-permute-start.5 = (f32[8,4,128]{2,1,0:T(4,128)S(1)}, f32[8,4,128]{2,1,0:T(4,128)S(1)}, u32[]{:S(2)}, u32[]{:S(2)}) collective-permute-start(f32[8,4,128]{2,1,0:T(4,128)S(1)} %get-tuple-element.30), channel_id=1, source_target_pairs={{0,0},{2,16},{4,32},{6,48},{8,8},{10,24},{12,40},{14,56},{16,2},{1... | collective-permute-start | bytes 49160 | tf_op jit(solution)/shard_map/ppermute | solution.py:212
  189.6 7.4 %collective-permute-start.6 = (f32[8,4,128]{2,1,0:T(4,128)S(1)}, f32[8,4,128]{2,1,0:T(4,128)S(1)}, u32[]{:S(2)}, u32[]{:S(2)}) collective-permute-start(f32[8,4,128]{2,1,0:T(4,128)S(1)} %get-tuple-element.29), channel_id=1, source_target_pairs={{0,8},{2,24},{4,40},{6,56},{8,0},{10,16},{12,32},{14,48},{16,10},{... | collective-permute-start | bytes 49160 | tf_op jit(solution)/shard_map/ppermute | solution.py:212
  198.1 3.3 %q.1 = bf16[256,384]{1,0:T(8,128)(2,1)S(1)} custom-call(s32[3]{0:T(128)S(1)} %pad_add_fusion.place, bf16[256,1536]{1,0:T(8,128)(2,1)S(1)} %get-tuple-element.14.normed, bf16[4,4,48,384]{3,2,1,0:T(8,128)(2,1)S(1)} %bitcast.17, bf16[4,4,48,384]{3,2,1,0:T(8,128)(2,1)} %collective-permute-done.3.w_oth), custom_call_target="tpu_custom_call" | custom-call | tf_op jit(solution)/shard_map/q/pallas_call | solution.py:267
  201.4 3.5 %collective-permute-done.6.pb_far = f32[8,4,128]{2,1,0:T(4,128)S(1)} collective-permute-done((f32[8,4,128]{2,1,0:T(4,128)S(1)}, f32[8,4,128]{2,1,0:T(4,128)S(1)}, u32[]{:S(2)}, u32[]{:S(2)}) %collective-permute-start.6) | collective-permute-done | bytes 16416 | tf_op jit(solution)/shard_map/ppermute | solution.py:212
  204.8 6.9 %attn.1 = (bf16[128,384]{1,0:T(8,128)(2,1)S(1)}, bf16[128,384]{1,0:T(8,128)(2,1)S(1)}) custom-call(s32[3]{0:T(128)S(1)} %pad_add_fusion.place, bf16[256,384]{1,0:T(8,128)(2,1)S(1)} %q.1, bf16[4,256,768]{2,1,0:T(8,128)(2,1)S(1)} %all-to-all-done.3.kv_own, bf16[4,256,768]{2,1,0:T(8,128)(2,1)} %collective-permute-done.4.kv_oth, ...), custom_call_target="tpu_custom_call" | custom-call | tf_op jit(solution)/shard_map/attn/pallas_call | solution.py:301
  211.8 7.4 %collective-permute-start.7 = (bf16[128,384]{1,0:T(8,128)(2,1)S(1)}, bf16[128,384]{1,0:T(8,128)(2,1)S(1)}, u32[]{:S(2)}, u32[]{:S(2)}) collective-permute-start(bf16[128,384]{1,0:T(8,128)(2,1)S(1)} %get-tuple-element.22), channel_id=1, source_target_pairs={{0,0},{2,16},{4,32},{6,48},{8,8},{10,24},{12,40},{14,56},{16,2},{1... | collective-permute-start | bytes 294920 | tf_op jit(solution)/shard_map/ppermute | solution.py:212
  219.1 4.7 %collective-permute-start.8 = (bf16[128,384]{1,0:T(8,128)(2,1)S(1)}, bf16[128,384]{1,0:T(8,128)(2,1)S(1)}, u32[]{:S(2)}, u32[]{:S(2)}) collective-permute-start(bf16[128,384]{1,0:T(8,128)(2,1)S(1)} %get-tuple-element.23), channel_id=1, source_target_pairs={{0,8},{2,24},{4,40},{6,56},{8,0},{10,16},{12,32},{14,48},{16,10},{... | collective-permute-start | bytes 294920 | tf_op jit(solution)/shard_map/ppermute | solution.py:212
  223.8 12.5 %collective-permute-done.8.a_far = bf16[128,384]{1,0:T(8,128)(2,1)S(1)} collective-permute-done((bf16[128,384]{1,0:T(8,128)(2,1)S(1)}, bf16[128,384]{1,0:T(8,128)(2,1)S(1)}, u32[]{:S(2)}, u32[]{:S(2)}) %collective-permute-start.8) | collective-permute-done | bytes 98336 | tf_op jit(solution)/shard_map/ppermute | solution.py:212
  236.3 5.4 %out.1 = bf16[128,1536]{1,0:T(8,128)(2,1)} custom-call(s32[3]{0:T(128)S(1)} %pad_add_fusion.place, bf16[128,1536]{1,0:T(8,128)(2,1)S(1)} %bitcast.21, bf16[128,384]{1,0:T(8,128)(2,1)S(1)} %collective-permute-done.7.a_near, bf16[128,384]{1,0:T(8,128)(2,1)S(1)} %collective-permute-done.8.a_far, bf16[4,4,48,768]{3,2,1,0:T(8,128)(2,1)S(1)} %bitcast.15, ...), custom_call_target="tpu_custom_call" | custom-call | tf_op jit(solution)/shard_map/out/pallas_call | solution.py:312
  (42 shorter events, 7.9 us)
Async XLA Ops:
  19.2 4.9 %copy-start.2 = (bf16[1,128,1536]{2,1,0:T(8,128)(2,1)S(1)}, bf16[1,128,1536]{2,1,0:T(8,128)(2,1)}, u32[]{:S(2)}) copy-start(bf16[1,128,1536]{2,1,0:T(8,128)(2,1)} %param.8) | copy-start | bytes 1179652
  19.2 22.0 %copy-start.8 = (f32[1536]{0:T(1024)S(1)}, f32[1536]{0:T(1024)}, u32[]{:S(2)}) copy-start(f32[1536]{0:T(1024)} %param.11) | copy-start | bytes 18436
  19.2 47.0 %all-to-all-start.1 = ((bf16[4,4,48,1024]{3,2,1,0:T(8,128)(2,1)}), bf16[4,4,48,1024]{3,2,1,0:T(8,128)(2,1)S(1)}, u32[]{:S(2)}, u32[]{:S(2)}) async-start(bf16[4,4,48,1024]{3,2,1,0:T(8,128)(2,1)} %broadcast_in_dim.22), calls=%async_computation.1 | async-start | bytes 3145728 | tf_op jit(solution)/shard_map/all_to_all | solution.py:196
  24.1 17.3 %collective-permute-start = (bf16[128,1536]{1,0:T(8,128)(2,1)S(1)}, bf16[128,1536]{1,0:T(8,128)(2,1)S(1)}, u32[]{:S(2)}, u32[]{:S(2)}) collective-permute-start(bf16[128,1536]{1,0:T(8,128)(2,1)S(1)} %bitcast.18), channel_id=1, source_target_pairs={{0,0},{2,16},{4,32},{6,48},{8,8},{10,24},{12,40},{14,56},{16,2},{1... | collective-permute-start | bytes 1179656 | tf_op jit(solution)/shard_map/ppermute | solution.py:212
  35.4 29.0 %collective-permute-start.1 = (bf16[128,1536]{1,0:T(8,128)(2,1)S(1)}, bf16[128,1536]{1,0:T(8,128)(2,1)S(1)}, u32[]{:S(2)}, u32[]{:S(2)}) collective-permute-start(bf16[128,1536]{1,0:T(8,128)(2,1)S(1)} %bitcast.19), channel_id=1, source_target_pairs={{0,8},{2,24},{4,40},{6,56},{8,0},{10,16},{12,32},{14,48},{16,10},{... | collective-permute-start | bytes 1179656 | tf_op jit(solution)/shard_map/ppermute | solution.py:212
  65.6 0.6 copy-start.5
  66.2 22.0 %copy-start.6 = (bf16[16,1536]{1,0:T(8,128)(2,1)S(1)}, bf16[16,1536]{1,0:T(8,128)(2,1)}, u32[]{:S(2)}) copy-start(bf16[16,1536]{1,0:T(8,128)(2,1)} %copy-done.5) | copy-start | bytes 147460
  66.2 22.0 %collective-permute-start.2 = (bf16[4,4,48,1024]{3,2,1,0:T(8,128)(2,1)S(1)}, bf16[4,4,48,1024]{3,2,1,0:T(8,128)(2,1)}, u32[]{:S(2)}, u32[]{:S(2)}) collective-permute-start(bf16[4,4,48,1024]{3,2,1,0:T(8,128)(2,1)S(1)} %all-to-all-done.1.w_own), channel_id=1, source_target_pairs={{0,16},{16,0},{1,17},{17,1},{2,18},{18,2},{3,19},{19,3},{4,20},{20... | collective-permute-start | bytes 4718600 | tf_op jit(solution)/shard_map/ppermute | solution.py:200
  74.8 28.4 %all-to-all-start.2 = ((bf16[16,48,384]{2,1,0:T(8,128)(2,1)}), bf16[16,48,384]{2,1,0:T(8,128)(2,1)S(1)}, u32[]{:S(2)}, u32[]{:S(2)}) async-start(bf16[16,48,384]{2,1,0:T(8,128)(2,1)} %broadcast_in_dim.23), calls=%async_computation.2 | async-start | bytes 1179648 | tf_op jit(solution)/shard_map/all_to_all | solution.py:196
  103.1 1.4 copy-start
  104.5 23.3 %copy-start.7 = (bf16[768,48]{0,1:T(8,128)(2,1)S(1)}, bf16[768,48]{0,1:T(8,128)(2,1)}, u32[]{:S(2)}) copy-start(bf16[768,48]{0,1:T(8,128)(2,1)} %param.15) | copy-start | bytes 221188
  104.5 23.3 %all-to-all-start.3 = ((bf16[4,256,768]{2,1,0:T(8,128)(2,1)}), bf16[4,256,768]{2,1,0:T(8,128)(2,1)S(1)}, u32[]{:S(2)}, u32[]{:S(2)}) async-start(bf16[4,256,768]{2,1,0:T(8,128)(2,1)} %broadcast_in_dim.24), calls=%async_computation.3 | async-start | bytes 3145728 | tf_op jit(solution)/shard_map/all_to_all | solution.py:196
  109.6 53.6 %copy-start.9 = (f32[128,6]{0,1:T(8,128)S(1)}, f32[128,6]{0,1:T(8,128)}, u32[]{:S(2)}) copy-start(f32[128,6]{0,1:T(8,128)} %param.14) | copy-start | bytes 9220
  128.9 32.4 %all-to-all-start.5 = ((bf16[16,48,768]{2,1,0:T(8,128)(2,1)}), bf16[16,48,768]{2,1,0:T(8,128)(2,1)S(1)}, u32[]{:S(2)}, u32[]{:S(2)}) async-start(bf16[16,48,768]{2,1,0:T(8,128)(2,1)} %broadcast_in_dim.27), calls=%async_computation.5 | async-start | bytes 2359296 | tf_op jit(solution)/shard_map/all_to_all | solution.py:196
  134.9 69.9 %collective-permute-start.4 = (bf16[4,256,768]{2,1,0:T(8,128)(2,1)S(1)}, bf16[4,256,768]{2,1,0:T(8,128)(2,1)}, u32[]{:S(2)}, u32[]{:S(2)}) collective-permute-start(bf16[4,256,768]{2,1,0:T(8,128)(2,1)S(1)} %all-to-all-done.3.kv_own), channel_id=1, source_target_pairs={{0,16},{16,0},{1,17},{17,1},{2,18},{18,2},{3,19},{19,3},{4,20},{20... | collective-permute-start | bytes 4718600 | tf_op jit(solution)/shard_map/ppermute | solution.py:200
  161.3 62.5 %collective-permute-start.9 = (bf16[4,4,48,768]{3,2,1,0:T(8,128)(2,1)S(1)}, bf16[4,4,48,768]{3,2,1,0:T(8,128)(2,1)}, u32[]{:S(2)}, u32[]{:S(2)}) collective-permute-start(bf16[4,4,48,768]{3,2,1,0:T(8,128)(2,1)S(1)} %bitcast.14), channel_id=1, source_target_pairs={{0,16},{16,0},{1,17},{17,1},{2,18},{18,2},{3,19},{19,3},{4,20},{20... | collective-permute-start | bytes 3538952 | tf_op jit(solution)/shard_map/ppermute | solution.py:200
  163.3 33.7 %collective-permute-start.3 = (bf16[4,4,48,384]{3,2,1,0:T(8,128)(2,1)}, bf16[4,4,48,384]{3,2,1,0:T(8,128)(2,1)}, u32[]{:S(2)}, u32[]{:S(2)}) collective-permute-start(bf16[4,4,48,384]{3,2,1,0:T(8,128)(2,1)} %bitcast.16), channel_id=1, source_target_pairs={{0,16},{16,0},{1,17},{17,1},{2,18},{18,2},{3,19},{19,3},{4,20},{20... | collective-permute-start | bytes 1769480 | tf_op jit(solution)/shard_map/ppermute | solution.py:200
  166.9 16.9 %all-to-all-start.4 = ((bf16[16,8,128]{2,1,0:T(8,128)(2,1)}), bf16[16,8,128]{2,1,0:T(8,128)(2,1)}, u32[]{:S(2)}, u32[]{:S(2)}) async-start(bf16[16,8,128]{2,1,0:T(8,128)(2,1)} %broadcast_in_dim.25), calls=%async_computation.4 | async-start | bytes 65536 | tf_op jit(solution)/shard_map/all_to_all | solution.py:196
  183.8 1.0 copy-start.4
  186.3 15.0 %collective-permute-start.5 = (f32[8,4,128]{2,1,0:T(4,128)S(1)}, f32[8,4,128]{2,1,0:T(4,128)S(1)}, u32[]{:S(2)}, u32[]{:S(2)}) collective-permute-start(f32[8,4,128]{2,1,0:T(4,128)S(1)} %get-tuple-element.30), channel_id=1, source_target_pairs={{0,0},{2,16},{4,32},{6,48},{8,8},{10,24},{12,40},{14,56},{16,2},{1... | collective-permute-start | bytes 49160 | tf_op jit(solution)/shard_map/ppermute | solution.py:212
  189.6 15.2 %collective-permute-start.6 = (f32[8,4,128]{2,1,0:T(4,128)S(1)}, f32[8,4,128]{2,1,0:T(4,128)S(1)}, u32[]{:S(2)}, u32[]{:S(2)}) collective-permute-start(f32[8,4,128]{2,1,0:T(4,128)S(1)} %get-tuple-element.29), channel_id=1, source_target_pairs={{0,8},{2,24},{4,40},{6,56},{8,0},{10,16},{12,32},{14,48},{16,10},{... | collective-permute-start | bytes 49160 | tf_op jit(solution)/shard_map/ppermute | solution.py:212
  197.0 1.1 copy-start.1
  201.3 35.0 %copy-start.3 = (bf16[1,128,1536]{2,1,0:T(8,128)(2,1)S(1)}, bf16[1,128,1536]{2,1,0:T(8,128)(2,1)}, u32[]{:S(2)}) copy-start(bf16[1,128,1536]{2,1,0:T(8,128)(2,1)} %param.8) | copy-start | bytes 1179652
  211.8 12.1 %collective-permute-start.7 = (bf16[128,384]{1,0:T(8,128)(2,1)S(1)}, bf16[128,384]{1,0:T(8,128)(2,1)S(1)}, u32[]{:S(2)}, u32[]{:S(2)}) collective-permute-start(bf16[128,384]{1,0:T(8,128)(2,1)S(1)} %get-tuple-element.22), channel_id=1, source_target_pairs={{0,0},{2,16},{4,32},{6,48},{8,8},{10,24},{12,40},{14,56},{16,2},{1... | collective-permute-start | bytes 294920 | tf_op jit(solution)/shard_map/ppermute | solution.py:212
  219.1 17.2 %collective-permute-start.8 = (bf16[128,384]{1,0:T(8,128)(2,1)S(1)}, bf16[128,384]{1,0:T(8,128)(2,1)S(1)}, u32[]{:S(2)}, u32[]{:S(2)}) collective-permute-start(bf16[128,384]{1,0:T(8,128)(2,1)S(1)} %get-tuple-element.23), channel_id=1, source_target_pairs={{0,8},{2,24},{4,40},{6,56},{8,0},{10,16},{12,32},{14,48},{16,10},{... | collective-permute-start | bytes 294920 | tf_op jit(solution)/shard_map/ppermute | solution.py:212

commit v3 on v2

v3 whole, which is shorter than its diff:
```python
import functools

import jax
import jax.numpy as jnp
from jax import lax
from jax.experimental import pallas as pl
from jax.experimental.pallas import tpu as pltpu
from jax.sharding import Mesh, PartitionSpec as P

HEADS = 6
HD = 128
CP = 128
POOL = 16
HALF = HEADS // 2
HW = HALF * HD
VMEM = 48 * 1024 * 1024

BF = jnp.bfloat16
F32 = jnp.float32

AXES = ("yl", "x", "c", "yh", "z")
SIZES = (4, 4, 2, 2, 8)
DP, SEQ = AXES[:3], AXES[3:]
NY, NX = 4, 4


def params():
    return pltpu.CompilerParams(vmem_limit_bytes=VMEM)


def vm():
    return pl.BlockSpec(memory_space=pltpu.VMEM)


def sm():
    return pl.BlockSpec(memory_space=pltpu.SMEM)


def hbm():
    return pl.BlockSpec(memory_space=pl.ANY)


def nt(a, b):
    return lax.dot_general(a, b, (((1,), (1,)), ((), ())), preferred_element_type=F32)


def split(x):
    hi = x.astype(BF)
    return hi, (x - hi.astype(F32)).astype(BF)


def weight_copies(place, own, other, buf, sem, first):
    rows = own.shape[2]
    cols = pl.ds(first, buf.shape[1])
    copies = []
    for which, src in ((0, own), (1, other)):
        core = place[1] if which == 0 else 1 - place[1]
        for y in range(NY):
            for x in range(NX):
                at = ((y * NX + x) * 2 + core) * rows
                copies.append(
                    pltpu.make_async_copy(
                        src.at[x, y, :, cols],
                        buf.at[pl.ds(pl.multiple_of(at, 16), rows), :],
                        sem.at[which, y * NX + x],
                    )
                )
    return copies


def norm_rows(x, gain):
    f = x.astype(F32)
    meansq = jnp.mean(f * f, axis=-1, keepdims=True)
    return (f * lax.rsqrt(meansq + 1e-06) * gain).astype(BF)


def norm_body(x_own, x_oth, gain, normed, means):
    rows, depth = x_own.shape
    g = gain[...]
    parts = []
    for at, x in ((0, x_own), (rows, x_oth)):
        n = norm_rows(x[...], g)
        normed[at : at + rows, :] = n
        parts.append(n.astype(F32).reshape(rows // POOL, POOL, depth).mean(axis=1))
    hi, lo = split(jnp.concatenate(parts, axis=0))
    means[...] = jnp.concatenate([hi, lo], axis=0)


def kv_body(place, normed, means, w_own, w_oth, kv, left, buf, sem):
    copies = weight_copies(place, w_own, w_oth, buf, sem, 0)
    for c in copies:
        c.start()
    for c in copies:
        c.wait()
    n = normed.shape[0]
    kv[:n, :] = jnp.dot(normed[...], buf[:, : 2 * HW], preferred_element_type=F32).astype(BF)
    both = jnp.dot(means[...], buf[:, 2 * HW :], preferred_element_type=F32)
    m = both.shape[0] // 2
    pooled = (both[:m] + both[m:]).astype(BF)
    left[...] = pooled[:, :CP].astype(F32)
    kv[n:, :CP] = pooled[:, CP:]
    kv[n:, CP:] = jnp.zeros((m, 2 * HW - CP), BF)


def q_body(place, normed, w_own, w_oth, q, buf, sem):
    copies = weight_copies(place, w_own, w_oth, buf, sem, 0)
    for c in copies:
        c.start()
    for c in copies:
        c.wait()
    q[...] = jnp.dot(normed[...], buf[...], preferred_element_type=F32).astype(BF)


def attn_body(place, q, kvg, pair_own, pair_oth, left, wt, pair_out, own, oth):
    side = place[0]
    limit = place[2]
    nz = kvg.shape[0]
    rows = q.shape[0] // 2
    npr = rows // POOL
    nrow = 2 * rows
    width = nz * nrow
    half_bins = nz * rows
    npair = half_bins * 2 // POOL
    scale = 1.0 / (HD**0.5)

    slots = ([], [])
    for z in range(nz):
        r = kvg[z, nrow:, :CP].astype(F32)
        slots[0].append(r[:npr])
        slots[1].append(r[npr:])
    first, second = (jnp.concatenate(x, axis=0) for x in slots)
    right = jnp.concatenate(
        [jnp.where(side == 0, first, second), jnp.where(side == 0, second, first)], axis=0
    )
    w = wt[...]

    col = lax.broadcasted_iota(jnp.int32, (1, width), 1)
    within = col % nrow
    yh = jnp.where(within // rows == 0, side, 1 - side)
    bin_at = yh * half_bins + (col // nrow) * rows + within % rows
    live = bin_at < limit
    onehot = (lax.broadcasted_iota(jnp.int32, (npair, width), 0) == bin_at // POOL).astype(F32)
    onehot = onehot.astype(BF)

    for s, (pair, dest) in enumerate(((pair_own, own), (pair_oth, oth))):
        biases = []
        for i in range(npr):
            l = left[s * npr + i : s * npr + i + 1, :]
            out = (pair[i].astype(F32) + l * right).astype(BF)
            if s == 0:
                pair_out[i] = out
            both = nt(w, out)
            biases.append(both[:8] + both[8:])
        pb = jnp.stack(biases)
        for h in range(HALF):
            qh = q[s * rows : (s + 1) * rows, h * HD : (h + 1) * HD]
            k = kvg[:, :nrow, h * HD : (h + 1) * HD].reshape(width, HD)
            v = kvg[:, :nrow, HW + h * HD : HW + (h + 1) * HD].reshape(width, HD)
            hi, lo = split(pb[:, h, :])
            bexp = jnp.dot(hi, onehot, preferred_element_type=F32) + jnp.dot(
                lo, onehot, preferred_element_type=F32
            )
            bexp = jnp.where(live, bexp, F32(-1e30))
            sc = nt(qh, k) * scale
            sc = (sc.reshape(npr, POOL, width) + bexp[:, None, :]).reshape(rows, width)
            top = jnp.max(sc, axis=-1, keepdims=True)
            e = jnp.exp(sc - top)
            total = jnp.sum(e, axis=-1, keepdims=True)
            acc = jnp.dot(e.astype(BF), v, preferred_element_type=F32)
            dest[:, h * HD : (h + 1) * HD] = (acc / total).astype(BF)


def out_body(place, x_own, a_own, a_oth, w_own, w_oth, mixed, buf, sem, full):
    copies = weight_copies(place, w_own, w_oth, buf, sem, HW)
    for c in copies:
        c.start()
    side = place[0]
    full[:, pl.ds(pl.multiple_of(side * HW, 128), HW)] = a_own[...]
    full[:, pl.ds(pl.multiple_of((1 - side) * HW, 128), HW)] = a_oth[...]
    for c in copies:
        c.wait()
    update = nt(full[...], buf[...])
    mixed[...] = (x_own[...].astype(F32) + update).astype(BF)


def spread(x, axis, n):
    return lax.all_to_all(jnp.broadcast_to(x[None], (n,) + x.shape), axis, 0, 0, tiled=True)


def swap(x, axis):
    return lax.ppermute(x, axis, [(0, 1), (1, 0)])


def after(x, *others):
    return lax.optimization_barrier((x,) + others)[0]


def on_device(bins, pair_in, valid, gain, w_qkv, w_pair, w_bias, w_out):
    side = lax.axis_index("yh")
    core = lax.axis_index("c")
    place = jnp.stack([side, core, valid[0]]).astype(jnp.int32)
    x_own = bins[0]
    rows, depth = x_own.shape
    npr = rows // POOL

    def mine(first):
        return lax.dynamic_slice_in_dim(w_qkv, first * HEADS * HD + side * HW, HW, axis=1)

    def weights(n):
        return [pltpu.VMEM((depth, n), BF), pltpu.SemaphoreType.DMA((2, NX * NY))]

    x_oth = swap(x_own, "yh")
    pair_oth = swap(pair_in[0], "yh")
    w = jnp.concatenate([mine(1), mine(2), w_pair], axis=1)
    w = spread(spread(w, "yl", NY), "x", NX)
    normed, means = pl.pallas_call(
        norm_body,
        out_shape=(
            jax.ShapeDtypeStruct((2 * rows, depth), BF),
            jax.ShapeDtypeStruct((4 * npr, depth), BF),
        ),
        in_specs=[vm()] * 3,
        out_specs=(vm(), vm()),
        compiler_params=params(),
        name="norm",
    )(x_own, x_oth, gain[None])
    w = after(w, normed)
    w_oth = swap(w, "c")
    kv, left = pl.pallas_call(
        kv_body,
        out_shape=(
            jax.ShapeDtypeStruct((2 * rows + 2 * npr, 2 * HW), BF),
            jax.ShapeDtypeStruct((2 * npr, CP), F32),
        ),
        in_specs=[sm(), vm(), vm(), hbm(), hbm()],
        out_specs=(vm(), vm()),
        scratch_shapes=weights(2 * HW + 2 * CP),
        compiler_params=params(),
        name="kv",
    )(place, normed, means, w, w_oth)
    kvg = lax.all_gather(kv, "z", axis=0)

    u = jnp.concatenate([mine(0), w_out.T], axis=1)
    u = spread(spread(after(u, w), "yl", NY), "x", NX)
    u_oth = swap(u, "c")
    q = pl.pallas_call(
        q_body,
        out_shape=jax.ShapeDtypeStruct((2 * rows, HW), BF),
        in_specs=[sm(), vm(), hbm(), hbm()],
        out_specs=vm(),
        scratch_shapes=weights(HW),
        compiler_params=params(),
        name="q",
    )(place, normed, u, u_oth)

    wt = lax.dynamic_slice_in_dim(w_bias.T, side * HALF, HALF, axis=0)
    wt = jnp.concatenate([wt, jnp.zeros((8 - HALF, CP), F32)], axis=0)
    wt = jnp.concatenate(split(wt), axis=0)
    pair_out, own, oth = pl.pallas_call(
        attn_body,
        out_shape=(jax.ShapeDtypeStruct(pair_in.shape[1:], BF),)
        + (jax.ShapeDtypeStruct((rows, HW), BF),) * 2,
        in_specs=[sm()] + [vm()] * 6,
        out_specs=(vm(), vm(), vm()),
        compiler_params=params(),
        name="attn",
    )(place, q, kvg, pair_in[0], pair_oth, left, wt)
    got = swap(oth, "yh")
    mixed = pl.pallas_call(
        out_body,
        out_shape=jax.ShapeDtypeStruct((rows, depth), BF),
        in_specs=[sm(), vm(), vm(), vm(), hbm(), hbm()],
        out_specs=vm(),
        scratch_shapes=weights(HEADS * HD) + [pltpu.VMEM((rows, HEADS * HD), BF)],
        compiler_params=params(),
        name="out",
    )(place, x_own, own, got, u, u_oth)
    return (mixed[None], pair_out[None])


def solution(mesh):
    fine = Mesh(mesh.devices.reshape(SIZES), AXES)
    placed = (
        P(DP, SEQ, None),
        P(DP, SEQ, None, None),
        P(DP),
        P(),
        P(DP, None),
        P(DP, None),
        P(),
        P(None, DP),
    )
    return jax.shard_map(
        on_device,
        mesh=fine,
        in_specs=placed,
        out_specs=(P(DP, SEQ, None), P(DP, SEQ, None, None)),
        check_vma=False,
    )
```

time: 243 us -> 164 us (0.67)
  the two profiles are of different devices: /device:TPU:14 before, /device:TPU:1 now
where the time goes in v3:
time: 164 us; the launch traced here: 163 us
  blocking collectives  53 us (32%)
  waiting for transfers between devices  37.3 us (23%)
  starting transfers between devices  31 us (19%)
  Pallas kernels  17.8 us (11%)
  between operations  14.9 us (9%)
  local copies, waits for them, and re-layouts  7.81 us (5%)
    all_to_all x3, blocking collectives, spread(): lax.all_to_all(jnp.broadcast_to(x[None], (n,) + x.shape), axis, 0, 0, til...  53 us
    ppermute x5, waiting for transfers between devices, swap(): return lax.ppermute(x, axis, [(0, 1), (1, 0)])  37.2 us
    ppermute x5, starting transfers between devices, swap(): return lax.ppermute(x, axis, [(0, 1), (1, 0)])  23.8 us
    all_to_all x1, starting transfers between devices, spread(): lax.all_to_all(jnp.broadcast_to(x[None], (n,) + x.shape), axis, 0, 0, til...  7.22 us
    pallas_call x1, Pallas kernels, on_device(): pl.pallas_call(attn_body, out_shape=(jax.ShapeDtypeStruct(pair_in.shape[1...  6.01 us
    pallas_call x1, Pallas kernels, on_device(): pl.pallas_call(kv_body, out_shape=(jax.ShapeDtypeStruct((2 * rows + 2 * n...  5.99 us
    unnamed x24, local copies, waits for them, and re-layouts  5.4 us
  transfers between devices with their start and end apart: 7, of which 4 were waited for; matrix products, arithmetic and copies ran while one was open for 0% of the time, Pallas kernels for 2%

profile of v3, /device:TPU:1, one launch (start us, length us, event | category | flops | bytes accessed | tf_op | source)
XLA Modules:
  0.0 162.6 jit_solution(1599512081065595406)
XLA Ops:
  7.2 0.0 copy-start
  7.2 0.8 constant_dynamic-slice_fusion.1
  8.0 0.7 pad_maximum_fusion.1
  8.8 13.0 %all_to_all.20 = bf16[4,48,1024]{2,1,0:T(8,128)(2,1)S(1)} all-to-all(bf16[4,48,1024]{2,1,0:T(8,128)(2,1)S(1)} %broadcast_in_dim.15), channel_id=1, replica_groups=mesh['yl'=4,'x'=4,'c'=2,'yh'=2,'z'=8] {'yl'}, dimensions={0} | all-to-all | bytes 786432 | tf_op jit(solution)/shard_map/all_to_all | solution.py:187
  21.8 1.4 broadcast_in_dim.16
  23.2 7.2 %all-to-all-start.1 = ((bf16[4,4,48,1024]{3,2,1,0:T(8,128)(2,1)}), bf16[4,4,48,1024]{3,2,1,0:T(8,128)(2,1)S(1)}, u32[]{:S(2)}, u32[]{:S(2)}) async-start(bf16[4,4,48,1024]{3,2,1,0:T(8,128)(2,1)} %broadcast_in_dim.16), calls=%async_computation.1 | async-start | bytes 3145728 | tf_op jit(solution)/shard_map/all_to_all | solution.py:187
  30.4 5.8 %collective-permute-start = (bf16[128,1536]{1,0:T(8,128)(2,1)S(1)}, bf16[128,1536]{1,0:T(8,128)(2,1)S(1)}, u32[]{:S(2)}, u32[]{:S(2)}) collective-permute-start(bf16[128,1536]{1,0:T(8,128)(2,1)S(1)} %bitcast.11), channel_id=1, source_target_pairs={{0,8},{8,0},{1,9},{9,1},{2,10},{10,2},{3,11},{11,3},{4,12},{12,4},... | collective-permute-start | bytes 1179656 | tf_op jit(solution)/shard_map/ppermute | solution.py:191
  36.3 17.9 %collective-permute-done.x_oth = bf16[128,1536]{1,0:T(8,128)(2,1)S(1)} collective-permute-done((bf16[128,1536]{1,0:T(8,128)(2,1)S(1)}, bf16[128,1536]{1,0:T(8,128)(2,1)S(1)}, u32[]{:S(2)}, u32[]{:S(2)}) %collective-permute-start) | collective-permute-done | bytes 393248 | tf_op jit(solution)/shard_map/ppermute | solution.py:191
  54.2 0.8 norm.1
  55.0 4.0 %collective-permute-start.2 = (bf16[4,4,48,1024]{3,2,1,0:T(8,128)(2,1)S(1)}, bf16[4,4,48,1024]{3,2,1,0:T(8,128)(2,1)}, u32[]{:S(2)}, u32[]{:S(2)}) collective-permute-start(bf16[4,4,48,1024]{3,2,1,0:T(8,128)(2,1)S(1)} %all-to-all-done.1.w_own), channel_id=1, source_target_pairs={{0,16},{16,0},{1,17},{17,1},{2,18},{18,2},{3,19},{19,3},{4,20},{20... | collective-permute-start | bytes 4718600 | tf_op jit(solution)/shard_map/ppermute | solution.py:191
  59.6 0.1 pad_add_fusion.place
  59.6 2.4 %collective-permute-done.2.w_oth = bf16[4,4,48,1024]{3,2,1,0:T(8,128)(2,1)} collective-permute-done((bf16[4,4,48,1024]{3,2,1,0:T(8,128)(2,1)S(1)}, bf16[4,4,48,1024]{3,2,1,0:T(8,128)(2,1)}, u32[]{:S(2)}, u32[]{:S(2)}) %collective-permute-start.2) | collective-permute-done | bytes 1572896 | tf_op jit(solution)/shard_map/ppermute | solution.py:191
  62.1 6.0 %kv.1 = (bf16[272,768]{1,0:T(8,128)(2,1)}, f32[16,128]{1,0:T(8,128)S(1)}) custom-call(s32[3]{0:T(128)S(1)} %pad_add_fusion.place, bf16[256,1536]{1,0:T(8,128)(2,1)S(1)} %get-tuple-element.11.normed, bf16[32,1536]{1,0:T(8,128)(2,1)S(1)} %get-tuple-element.14.means, bf16[4,4,48,1024]{3,2,1,0:T(8,128)(2,1)S(1)} %all-to-all-done.1.w_own, ...), custom_call_target="tpu_custom_call" | custom-call | tf_op jit(solution)/shard_map/kv/pallas_call | solution.py:229
  68.1 0.0 copy-start.8
  68.1 0.0 all-gather.3.cloned.1.call-update
  68.2 15.1 %all_to_all.21 = bf16[4,48,1152]{2,1,0:T(8,128)(2,1)S(1)} all-to-all(bf16[4,48,1152]{2,1,0:T(8,128)(2,1)S(1)} %broadcast_in_dim.17), channel_id=1, replica_groups=mesh['yl'=4,'x'=4,'c'=2,'yh'=2,'z'=8] {'yl'}, dimensions={0} | all-to-all | bytes 884736 | tf_op jit(solution)/shard_map/all_to_all | solution.py:187
  83.3 0.1 broadcast_in_dim.18
  83.4 24.9 %all_to_all.22.w_own = bf16[4,4,48,1152]{3,2,1,0:T(8,128)(2,1)S(1)} all-to-all(bf16[4,4,48,1152]{3,2,1,0:T(8,128)(2,1)S(1)} %broadcast_in_dim.18), channel_id=1, replica_groups=mesh['yl'=4,'x'=4,'c'=2,'yh'=2,'z'=8] {'x'}, dimensions={0} | all-to-all | bytes 3538944 | tf_op jit(solution)/shard_map/all_to_all | solution.py:187
  108.4 4.8 %collective-permute-start.1 = (bf16[4,4,48,1152]{3,2,1,0:T(8,128)(2,1)S(1)}, bf16[4,4,48,1152]{3,2,1,0:T(8,128)(2,1)S(1)}, u32[]{:S(2)}, u32[]{:S(2)}) collective-permute-start(bf16[4,4,48,1152]{3,2,1,0:T(8,128)(2,1)S(1)} %all_to_all.22.w_own), channel_id=1, source_target_pairs={{0,16},{16,0},{1,17},{17,1},{2,18},{18,2},{3,19},{19,3},{4,20},{20... | collective-permute-start | bytes 5308424 | tf_op jit(solution)/shard_map/ppermute | solution.py:191
  113.1 4.6 %collective-permute-start.3 = (bf16[8,128,128]{2,1,0:T(8,128)(2,1)}, bf16[8,128,128]{2,1,0:T(8,128)(2,1)}, u32[]{:S(2)}, u32[]{:S(2)}) collective-permute-start(bf16[8,128,128]{2,1,0:T(8,128)(2,1)} %bitcast.5.pair_own), channel_id=1, source_target_pairs={{0,8},{8,0},{1,9},{9,1},{2,10},{10,2},{3,11},{11,3},{4,12},{12,4},... | collective-permute-start | bytes 786440 | tf_op jit(solution)/shard_map/ppermute | solution.py:191
  117.8 1.1 copy-done.3
  118.9 1.8 %q.1 = bf16[256,384]{1,0:T(8,128)(2,1)S(1)} custom-call(s32[3]{0:T(128)S(1)} %pad_add_fusion.place, bf16[256,1536]{1,0:T(8,128)(2,1)S(1)} %copy-done.3, bf16[4,4,48,1152]{3,2,1,0:T(8,128)(2,1)S(1)} %all_to_all.22.w_own, bf16[4,4,48,1152]{3,2,1,0:T(8,128)(2,1)S(1)} %collective-permute-done.1.w_oth), custom_call_target="tpu_custom_call" | custom-call | tf_op jit(solution)/shard_map/q/pallas_call | solution.py:246
  120.8 0.0 copy-start.6
  120.8 0.7 copy-done.6
  121.5 11.3 %collective-permute-done.3.pair_oth = bf16[8,128,128]{2,1,0:T(8,128)(2,1)} collective-permute-done((bf16[8,128,128]{2,1,0:T(8,128)(2,1)}, bf16[8,128,128]{2,1,0:T(8,128)(2,1)}, u32[]{:S(2)}, u32[]{:S(2)}) %collective-permute-start.3) | collective-permute-done | bytes 262176 | tf_op jit(solution)/shard_map/ppermute | solution.py:191
  132.8 1.9 %copy-done.1 = bf16[2176,768]{1,0:T(8,128)(2,1)S(1)} copy-done((bf16[2176,768]{1,0:T(8,128)(2,1)S(1)}, bf16[2176,768]{1,0:T(8,128)(2,1)}, u32[]{:S(2)}) %copy-start.1) | copy-done | bytes 3342360
  134.8 0.9 copy-done.7
  135.7 0.7 copy-done.9
  136.4 6.0 %attn.1 = (bf16[8,128,128]{2,1,0:T(8,128)(2,1)}, bf16[128,384]{1,0:T(8,128)(2,1)S(1)}, bf16[128,384]{1,0:T(8,128)(2,1)S(1)}) custom-call(s32[3]{0:T(128)S(1)} %pad_add_fusion.place, bf16[256,384]{1,0:T(8,128)(2,1)S(1)} %copy-done.7, bf16[8,272,768]{2,1,0:T(8,128)(2,1)S(1)} %bitcast.10, bf16[8,128,128]{2,1,0:T(8,128)(2,1)} %bitcast.5.pair_own, ...), custom_call_target="tpu_custom_call" | custom-call | tf_op jit(solution)/shard_map/attn/pallas_call | solution.py:259
  142.4 4.6 %collective-permute-start.4 = (bf16[128,384]{1,0:T(8,128)(2,1)S(1)}, bf16[128,384]{1,0:T(8,128)(2,1)S(1)}, u32[]{:S(2)}, u32[]{:S(2)}) collective-permute-start(bf16[128,384]{1,0:T(8,128)(2,1)S(1)} %get-tuple-element.18), channel_id=1, source_target_pairs={{0,8},{8,0},{1,9},{9,1},{2,10},{10,2},{3,11},{11,3},{4,12},{12,4},... | collective-permute-start | bytes 294920 | tf_op jit(solution)/shard_map/ppermute | solution.py:191
  147.0 5.5 %collective-permute-done.4.a_oth = bf16[128,384]{1,0:T(8,128)(2,1)S(1)} collective-permute-done((bf16[128,384]{1,0:T(8,128)(2,1)S(1)}, bf16[128,384]{1,0:T(8,128)(2,1)S(1)}, u32[]{:S(2)}, u32[]{:S(2)}) %collective-permute-start.4) | collective-permute-done | bytes 98336 | tf_op jit(solution)/shard_map/ppermute | solution.py:191
  152.6 3.2 %out.1 = bf16[128,1536]{1,0:T(8,128)(2,1)} custom-call(s32[3]{0:T(128)S(1)} %pad_add_fusion.place, bf16[128,1536]{1,0:T(8,128)(2,1)S(1)} %bitcast.13, bf16[128,384]{1,0:T(8,128)(2,1)S(1)} %get-tuple-element.17.a_own, bf16[128,384]{1,0:T(8,128)(2,1)S(1)} %collective-permute-done.4.a_oth, bf16[4,4,48,1152]{3,2,1,0:T(8,128)(2,1)S(1)} %all_to_all.22.w_own, ...), custom_call_target="tpu_custom_call" | custom-call | tf_op jit(solution)/shard_map/out/pallas_call | solution.py:269
  (28 shorter events, 0.1 us)
Async XLA Ops:
  7.2 110.6 %copy-start = (f32[128,6]{0,1:T(8,128)S(1)}, f32[128,6]{0,1:T(8,128)}, u32[]{:S(2)}) copy-start(f32[128,6]{0,1:T(8,128)} %param.14) | copy-start | bytes 9220
  23.2 7.2 %copy-start.4 = (bf16[1,128,1536]{2,1,0:T(8,128)(2,1)S(1)}, bf16[1,128,1536]{2,1,0:T(8,128)(2,1)}, u32[]{:S(2)}) copy-start(bf16[1,128,1536]{2,1,0:T(8,128)(2,1)} %param.8) | copy-start | bytes 1179652
  23.2 13.1 %copy-start.11 = (f32[1536]{0:T(1024)S(1)}, f32[1536]{0:T(1024)}, u32[]{:S(2)}) copy-start(f32[1536]{0:T(1024)} %param.11) | copy-start | bytes 18436
  23.2 31.8 %all-to-all-start.1 = ((bf16[4,4,48,1024]{3,2,1,0:T(8,128)(2,1)}), bf16[4,4,48,1024]{3,2,1,0:T(8,128)(2,1)S(1)}, u32[]{:S(2)}, u32[]{:S(2)}) async-start(bf16[4,4,48,1024]{3,2,1,0:T(8,128)(2,1)} %broadcast_in_dim.16), calls=%async_computation.1 | async-start | bytes 3145728 | tf_op jit(solution)/shard_map/all_to_all | solution.py:187
  30.4 102.4 %all-gather.3.cloned.1.call-start = ((), (), s32[]{:S(2)}) async-start(), calls=%async_computation.4 | async-start | bytes 3760128 | tf_op jit(solution)/shard_map/all_gather | solution.py:241
  30.4 23.8 %collective-permute-start = (bf16[128,1536]{1,0:T(8,128)(2,1)S(1)}, bf16[128,1536]{1,0:T(8,128)(2,1)S(1)}, u32[]{:S(2)}, u32[]{:S(2)}) collective-permute-start(bf16[128,1536]{1,0:T(8,128)(2,1)S(1)} %bitcast.11), channel_id=1, source_target_pairs={{0,8},{8,0},{1,9},{9,1},{2,10},{10,2},{3,11},{11,3},{4,12},{12,4},... | collective-permute-start | bytes 1179656 | tf_op jit(solution)/shard_map/ppermute | solution.py:191
  54.9 13.1 %copy-start.2 = (bf16[256,1536]{1,0:T(8,128)(2,1)}, bf16[256,1536]{1,0:T(8,128)(2,1)S(1)}, u32[]{:S(2)}) copy-start(bf16[256,1536]{1,0:T(8,128)(2,1)S(1)} %get-tuple-element.11.normed) | copy-start | bytes 2359300
  55.0 7.1 %collective-permute-start.2 = (bf16[4,4,48,1024]{3,2,1,0:T(8,128)(2,1)S(1)}, bf16[4,4,48,1024]{3,2,1,0:T(8,128)(2,1)}, u32[]{:S(2)}, u32[]{:S(2)}) collective-permute-start(bf16[4,4,48,1024]{3,2,1,0:T(8,128)(2,1)S(1)} %all-to-all-done.1.w_own), channel_id=1, source_target_pairs={{0,16},{16,0},{1,17},{17,1},{2,18},{18,2},{3,19},{19,3},{4,20},{20... | collective-permute-start | bytes 4718600 | tf_op jit(solution)/shard_map/ppermute | solution.py:191
  62.1 6.0 %copy-start.10 = (bf16[768,48]{0,1:T(8,128)(2,1)S(1)}, bf16[768,48]{0,1:T(8,128)(2,1)}, u32[]{:S(2)}) copy-start(bf16[768,48]{0,1:T(8,128)(2,1)} %param.15) | copy-start | bytes 221188
  68.1 15.3 %copy-start.8 = (f32[16,128]{1,0:T(8,128)}, f32[16,128]{1,0:T(8,128)S(1)}, u32[]{:S(2)}) copy-start(f32[16,128]{1,0:T(8,128)S(1)} %get-tuple-element.16.left) | copy-start | bytes 24580
  108.4 9.4 %collective-permute-start.1 = (bf16[4,4,48,1152]{3,2,1,0:T(8,128)(2,1)S(1)}, bf16[4,4,48,1152]{3,2,1,0:T(8,128)(2,1)S(1)}, u32[]{:S(2)}, u32[]{:S(2)}) collective-permute-start(bf16[4,4,48,1152]{3,2,1,0:T(8,128)(2,1)S(1)} %all_to_all.22.w_own), channel_id=1, source_target_pairs={{0,16},{16,0},{1,17},{17,1},{2,18},{18,2},{3,19},{19,3},{4,20},{20... | collective-permute-start | bytes 5308424 | tf_op jit(solution)/shard_map/ppermute | solution.py:191
  113.1 19.7 %collective-permute-start.3 = (bf16[8,128,128]{2,1,0:T(8,128)(2,1)}, bf16[8,128,128]{2,1,0:T(8,128)(2,1)}, u32[]{:S(2)}, u32[]{:S(2)}) collective-permute-start(bf16[8,128,128]{2,1,0:T(8,128)(2,1)} %bitcast.5.pair_own), channel_id=1, source_target_pairs={{0,8},{8,0},{1,9},{9,1},{2,10},{10,2},{3,11},{11,3},{4,12},{12,4},... | collective-permute-start | bytes 786440 | tf_op jit(solution)/shard_map/ppermute | solution.py:191
  117.8 1.1 copy-start.3
  120.8 0.7 copy-start.6
  132.8 1.9 %copy-start.1 = (bf16[2176,768]{1,0:T(8,128)(2,1)S(1)}, bf16[2176,768]{1,0:T(8,128)(2,1)}, u32[]{:S(2)}) copy-start(bf16[2176,768]{1,0:T(8,128)(2,1)} %all-gather.3.cloned.1.call-done) | copy-start | bytes 10027012
  134.7 0.9 copy-start.7
  135.7 0.7 copy-start.9
  136.4 16.2 %copy-start.5 = (bf16[1,128,1536]{2,1,0:T(8,128)(2,1)S(1)}, bf16[1,128,1536]{2,1,0:T(8,128)(2,1)}, u32[]{:S(2)}) copy-start(bf16[1,128,1536]{2,1,0:T(8,128)(2,1)} %param.8) | copy-start | bytes 1179652
  142.4 10.2 %collective-permute-start.4 = (bf16[128,384]{1,0:T(8,128)(2,1)S(1)}, bf16[128,384]{1,0:T(8,128)(2,1)S(1)}, u32[]{:S(2)}, u32[]{:S(2)}) collective-permute-start(bf16[128,384]{1,0:T(8,128)(2,1)S(1)} %get-tuple-element.18), channel_id=1, source_target_pairs={{0,8},{8,0},{1,9},{9,1},{2,10},{10,2},{3,11},{11,3},{4,12},{12,4},... | collective-permute-start | bytes 294920 | tf_op jit(solution)/shard_map/ppermute | solution.py:191
Sparse Core Ops, SparseCore 0:
  68.2 52.4 all-gather.2

commit v4 on v3

--- a/solution.py
+++ b/solution.py
@@ -13,7 +13,7 @@
 POOL = 16
 HALF = HEADS // 2
 HW = HALF * HD
-VMEM = 48 * 1024 * 1024
+VMEM = 14 * 1024 * 1024
 
 BF = jnp.bfloat16
 F32 = jnp.float32
@@ -26,6 +26,10 @@
 
 def params():
     return pltpu.CompilerParams(vmem_limit_bytes=VMEM)
+
+
+def cost(gflop):
+    return pl.CostEstimate(flops=gflop * 10**9, bytes_accessed=1 << 20, transcendentals=0)
 
 
 def vm():
@@ -111,7 +115,15 @@
     q[...] = jnp.dot(normed[...], buf[...], preferred_element_type=F32).astype(BF)
 
 
-def attn_body(place, q, kvg, pair_own, pair_oth, left, wt, pair_out, own, oth):
+def attn_body(place, q_at, kvg_at, pair_own_at, pair_oth_at, left, wt, pair_out, own, oth, *held):
+    refs, sem = held[:4], held[4]
+    copies = [
+        pltpu.make_async_copy(src, dst, sem.at[i])
+        for i, (src, dst) in enumerate(zip((kvg_at, pair_own_at, pair_oth_at, q_at), refs))
+    ]
+    for c in copies:
+        c.start()
+    kvg, pair_own, pair_oth, q = refs
     side = place[0]
     limit = place[2]
     nz = kvg.shape[0]
@@ -123,6 +135,8 @@
     npair = half_bins * 2 // POOL
     scale = 1.0 / (HD**0.5)
 
+    for c in copies:
+        c.wait()
     slots = ([], [])
     for z in range(nz):
         r = kvg[z, nrow:, :CP].astype(F32)
@@ -210,7 +224,6 @@
         return [pltpu.VMEM((depth, n), BF), pltpu.SemaphoreType.DMA((2, NX * NY))]
 
     x_oth = swap(x_own, "yh")
-    pair_oth = swap(pair_in[0], "yh")
     w = jnp.concatenate([mine(1), mine(2), w_pair], axis=1)
     w = spread(spread(w, "yl", NY), "x", NX)
     normed, means = pl.pallas_call(
@@ -222,9 +235,9 @@
         in_specs=[vm()] * 3,
         out_specs=(vm(), vm()),
         compiler_params=params(),
+        cost_estimate=cost(20),
         name="norm",
     )(x_own, x_oth, gain[None])
-    w = after(w, normed)
     w_oth = swap(w, "c")
     kv, left = pl.pallas_call(
         kv_body,
@@ -236,13 +249,16 @@
         out_specs=(vm(), vm()),
         scratch_shapes=weights(2 * HW + 2 * CP),
         compiler_params=params(),
+        cost_estimate=cost(10),
         name="kv",
     )(place, normed, means, w, w_oth)
     kvg = lax.all_gather(kv, "z", axis=0)
 
     u = jnp.concatenate([mine(0), w_out.T], axis=1)
-    u = spread(spread(after(u, w), "yl", NY), "x", NX)
-    u_oth = swap(u, "c")
+    u = spread(after(u, w), "yl", NY)
+    pair_oth = swap(after(pair_in[0], u), "yh")
+    u = spread(u, "x", NX)
+    u_oth = swap(after(u, pair_oth), "c")
     q = pl.pallas_call(
         q_body,
         out_shape=jax.ShapeDtypeStruct((2 * rows, HW), BF),
@@ -260,9 +276,12 @@
         attn_body,
         out_shape=(jax.ShapeDtypeStruct(pair_in.shape[1:], BF),)
         + (jax.ShapeDtypeStruct((rows, HW), BF),) * 2,
-        in_specs=[sm()] + [vm()] * 6,
+        in_specs=[sm()] + [hbm()] * 4 + [vm()] * 2,
         out_specs=(vm(), vm(), vm()),
-        compiler_params=params(),
+        scratch_shapes=[pltpu.VMEM(x.shape, BF) for x in (kvg, pair_oth, pair_oth, q)]
+        + [pltpu.SemaphoreType.DMA((4,))],
+        compiler_params=pltpu.CompilerParams(vmem_limit_bytes=56 * 1024 * 1024),
+        cost_estimate=cost(10),
         name="attn",
     )(place, q, kvg, pair_in[0], pair_oth, left, wt)
     got = swap(oth, "yh")

time: 164 us -> 150 us (0.915)
  blocking collectives: 53 us -> 28.2 us
  starting transfers between devices: 31 us -> 37.9 us
  Pallas kernels: 17.8 us -> 21.3 us
    all_to_all x3 -> x2, blocking collectives: 53 us -> 28.2 us  [spread(): lax.all_to_all(jnp.broadcast_to(x[None], (n,) + x.shape), axis, 0, 0, til...]
    ppermute x5, waiting for transfers between devices: 37.2 us -> 20.8 us  [swap(): return lax.ppermute(x, axis, [(0, 1), (1, 0)])]
    all_to_all x1 -> x2, waiting for transfers between devices: 0.01 us -> 14.8 us  [spread(): lax.all_to_all(jnp.broadcast_to(x[None], (n,) + x.shape), axis, 0, 0, til...]
    all_to_all x1 -> x2, starting transfers between devices: 7.22 us -> 10.9 us  [spread(): lax.all_to_all(jnp.broadcast_to(x[None], (n,) + x.shape), axis, 0, 0, til...]
    ppermute x5, starting transfers between devices: 23.8 us -> 27 us  [swap(): return lax.ppermute(x, axis, [(0, 1), (1, 0)])]
    pallas_call x1, Pallas kernels: 6.01 us -> 8.41 us  [on_device(): pl.pallas_call(attn_body, out_shape=(jax.ShapeDtypeStruct(pair_in.shape[1...]
    unnamed x24 -> x28, local copies, waits for them, and re-layouts: 5.4 us -> 4.01 us
  transfers between devices with their start and end apart: 7 -> 8, of which waited for: 4 -> 7; matrix products, arithmetic and copies ran while one was open for 0% -> 1% of each run, Pallas kernels for 2% -> 2%
where the time goes in v4:
time: 150 us; the launch traced here: 147 us
  starting transfers between devices  37.9 us (25%)
  waiting for transfers between devices  35.7 us (24%)
  blocking collectives  28.2 us (19%)
  Pallas kernels  21.3 us (14%)
  between operations  14.9 us (10%)
  local copies, waits for them, and re-layouts  7.66 us (5%)
    all_to_all x2, blocking collectives, spread(): lax.all_to_all(jnp.broadcast_to(x[None], (n,) + x.shape), axis, 0, 0, til...  28.2 us
    ppermute x5, starting transfers between devices, swap(): return lax.ppermute(x, axis, [(0, 1), (1, 0)])  27 us
    ppermute x5, waiting for transfers between devices, swap(): return lax.ppermute(x, axis, [(0, 1), (1, 0)])  20.8 us
    all_to_all x2, waiting for transfers between devices, spread(): lax.all_to_all(jnp.broadcast_to(x[None], (n,) + x.shape), axis, 0, 0, til...  14.8 us
    all_to_all x2, starting transfers between devices, spread(): lax.all_to_all(jnp.broadcast_to(x[None], (n,) + x.shape), axis, 0, 0, til...  10.9 us
    pallas_call x1, Pallas kernels, on_device(): pl.pallas_call(attn_body, out_shape=(jax.ShapeDtypeStruct(pair_in.shape[1...  8.41 us
    pallas_call x1, Pallas kernels, on_device(): pl.pallas_call(kv_body, out_shape=(jax.ShapeDtypeStruct((2 * rows + 2 * n...  7.12 us
    unnamed x28, local copies, waits for them, and re-layouts  4.01 us
  transfers between devices with their start and end apart: 8, of which 7 were waited for; matrix products, arithmetic and copies ran while one was open for 1% of the time, Pallas kernels for 2%

profile of v4, /device:TPU:1, one launch (start us, length us, event | category | flops | bytes accessed | tf_op | source)
XLA Modules:
  0.0 147.1 jit_solution(7363540280010717100)
XLA Ops:
  7.2 0.8 constant_dynamic-slice_fusion.1
  8.0 0.7 pad_maximum_fusion.1
  8.8 13.0 %all_to_all.20 = bf16[4,48,1024]{2,1,0:T(8,128)(2,1)S(1)} all-to-all(bf16[4,48,1024]{2,1,0:T(8,128)(2,1)S(1)} %broadcast_in_dim.15), channel_id=1, replica_groups=mesh['yl'=4,'x'=4,'c'=2,'yh'=2,'z'=8] {'yl'}, dimensions={0} | all-to-all | bytes 786432 | tf_op jit(solution)/shard_map/all_to_all | solution.py:201
  21.8 1.4 broadcast_in_dim.16
  23.2 7.2 %all-to-all-start.1 = ((bf16[4,4,48,1024]{3,2,1,0:T(8,128)(2,1)}), bf16[4,4,48,1024]{3,2,1,0:T(8,128)(2,1)S(1)}, u32[]{:S(2)}, u32[]{:S(2)}) async-start(bf16[4,4,48,1024]{3,2,1,0:T(8,128)(2,1)} %broadcast_in_dim.16), calls=%async_computation.1 | async-start | bytes 3145728 | tf_op jit(solution)/shard_map/all_to_all | solution.py:201
  30.4 5.8 %collective-permute-start = (bf16[128,1536]{1,0:T(8,128)(2,1)S(1)}, bf16[128,1536]{1,0:T(8,128)(2,1)S(1)}, u32[]{:S(2)}, u32[]{:S(2)}) collective-permute-start(bf16[128,1536]{1,0:T(8,128)(2,1)S(1)} %bitcast.10), channel_id=1, source_target_pairs={{0,8},{8,0},{1,9},{9,1},{2,10},{10,2},{3,11},{11,3},{4,12},{12,4},... | collective-permute-start | bytes 1179656 | tf_op jit(solution)/shard_map/ppermute | solution.py:205
  36.9 0.1 pad_add_fusion.place
  37.0 12.0 %all-to-all-done.1.w_own = bf16[4,4,48,1024]{3,2,1,0:T(8,128)(2,1)S(1)} async-done(((bf16[4,4,48,1024]{3,2,1,0:T(8,128)(2,1)}), bf16[4,4,48,1024]{3,2,1,0:T(8,128)(2,1)S(1)}, u32[]{:S(2)}, u32[]{:S(2)}) %all-to-all-start.1) | async-done | bytes 1572896 | tf_op jit(solution)/shard_map/all_to_all | solution.py:201
  49.1 4.9 %collective-permute-start.3 = (bf16[4,4,48,1024]{3,2,1,0:T(8,128)(2,1)S(1)}, bf16[4,4,48,1024]{3,2,1,0:T(8,128)(2,1)S(1)}, u32[]{:S(2)}, u32[]{:S(2)}) collective-permute-start(bf16[4,4,48,1024]{3,2,1,0:T(8,128)(2,1)S(1)} %all-to-all-done.1.w_own), channel_id=1, source_target_pairs={{0,16},{16,0},{1,17},{17,1},{2,18},{18,2},{3,19},{19,3},{4,20},{20... | collective-permute-start | bytes 4718600 | tf_op jit(solution)/shard_map/ppermute | solution.py:205
  54.0 0.2 collective-permute-done.x_oth
  54.2 0.8 norm.1
  55.0 2.0 %collective-permute-done.3.w_oth = bf16[4,4,48,1024]{3,2,1,0:T(8,128)(2,1)S(1)} collective-permute-done((bf16[4,4,48,1024]{3,2,1,0:T(8,128)(2,1)S(1)}, bf16[4,4,48,1024]{3,2,1,0:T(8,128)(2,1)S(1)}, u32[]{:S(2)}, u32[]{:S(2)}) %collective-permute-start.3) | collective-permute-done | bytes 1572896 | tf_op jit(solution)/shard_map/ppermute | solution.py:205
  57.0 7.1 %kv.1 = (bf16[272,768]{1,0:T(8,128)(2,1)}, f32[16,128]{1,0:T(8,128)S(1)}) custom-call(s32[3]{0:T(128)S(1)} %pad_add_fusion.place, bf16[256,1536]{1,0:T(8,128)(2,1)S(1)} %get-tuple-element.12.normed, bf16[32,1536]{1,0:T(8,128)(2,1)S(1)} %get-tuple-element.16.means, bf16[4,4,48,1024]{3,2,1,0:T(8,128)(2,1)S(1)} %all-to-all-done.1.w_own, ...), custom_call_target="tpu_custom_call" | custom-call | flops 10000000000 | bytes 1048576 | tf_op jit(solution)/shard_map/kv/pallas_call | solution.py:242
  64.1 0.6 copy-done.9
  64.8 15.2 %all_to_all.21 = bf16[4,48,1152]{2,1,0:T(8,128)(2,1)S(1)} all-to-all(bf16[4,48,1152]{2,1,0:T(8,128)(2,1)S(1)} %broadcast_in_dim.17), channel_id=1, replica_groups=mesh['yl'=4,'x'=4,'c'=2,'yh'=2,'z'=8] {'yl'}, dimensions={0} | all-to-all | bytes 884736 | tf_op jit(solution)/shard_map/all_to_all | solution.py:201
  80.0 1.4 broadcast_in_dim.18
  81.4 3.7 %all-to-all-start.3 = ((bf16[4,4,48,1152]{3,2,1,0:T(8,128)(2,1)}), bf16[4,4,48,1152]{3,2,1,0:T(8,128)(2,1)S(1)}, u32[]{:S(2)}, u32[]{:S(2)}) async-start(bf16[4,4,48,1152]{3,2,1,0:T(8,128)(2,1)} %broadcast_in_dim.18), calls=%async_computation.3 | async-start | bytes 3538944 | tf_op jit(solution)/shard_map/all_to_all | solution.py:201
  85.1 5.5 %collective-permute-start.1 = (bf16[8,128,128]{2,1,0:T(8,128)(2,1)S(1)}, bf16[8,128,128]{2,1,0:T(8,128)(2,1)S(1)}, u32[]{:S(2)}, u32[]{:S(2)}) collective-permute-start(bf16[8,128,128]{2,1,0:T(8,128)(2,1)S(1)} %bitcast.17), channel_id=1, source_target_pairs={{0,8},{8,0},{1,9},{9,1},{2,10},{10,2},{3,11},{11,3},{4,12},{12,4},... | collective-permute-start | bytes 786440 | tf_op jit(solution)/shard_map/ppermute | solution.py:205
  90.6 12.4 %collective-permute-done.1.pair_oth_at = bf16[8,128,128]{2,1,0:T(8,128)(2,1)S(1)} collective-permute-done((bf16[8,128,128]{2,1,0:T(8,128)(2,1)S(1)}, bf16[8,128,128]{2,1,0:T(8,128)(2,1)S(1)}, u32[]{:S(2)}, u32[]{:S(2)}) %collective-permute-start.1) | collective-permute-done | bytes 262176 | tf_op jit(solution)/shard_map/ppermute | solution.py:205
  103.0 0.7 copy-done.13
  103.7 2.8 %all-to-all-done.3.w_own = bf16[4,4,48,1152]{3,2,1,0:T(8,128)(2,1)S(1)} async-done(((bf16[4,4,48,1152]{3,2,1,0:T(8,128)(2,1)}), bf16[4,4,48,1152]{3,2,1,0:T(8,128)(2,1)S(1)}, u32[]{:S(2)}, u32[]{:S(2)}) %all-to-all-start.3) | async-done | bytes 1769504 | tf_op jit(solution)/shard_map/all_to_all | solution.py:201
  106.5 4.2 %collective-permute-start.2 = (bf16[4,4,48,1152]{3,2,1,0:T(8,128)(2,1)S(1)}, bf16[4,4,48,1152]{3,2,1,0:T(8,128)(2,1)S(1)}, u32[]{:S(2)}, u32[]{:S(2)}) collective-permute-start(bf16[4,4,48,1152]{3,2,1,0:T(8,128)(2,1)S(1)} %all-to-all-done.3.w_own), channel_id=1, source_target_pairs={{0,16},{16,0},{1,17},{17,1},{2,18},{18,2},{3,19},{19,3},{4,20},{20... | collective-permute-start | bytes 5308424 | tf_op jit(solution)/shard_map/ppermute | solution.py:205
  110.8 0.6 pad_maximum_fusion.2.wt
  111.4 2.7 %collective-permute-done.2.w_oth = bf16[4,4,48,1152]{3,2,1,0:T(8,128)(2,1)S(1)} collective-permute-done((bf16[4,4,48,1152]{3,2,1,0:T(8,128)(2,1)S(1)}, bf16[4,4,48,1152]{3,2,1,0:T(8,128)(2,1)S(1)}, u32[]{:S(2)}, u32[]{:S(2)}) %collective-permute-start.2) | collective-permute-done | bytes 1769504 | tf_op jit(solution)/shard_map/ppermute | solution.py:205
  114.0 1.1 copy-done.2
  115.2 1.8 %q.1.q_at = bf16[256,384]{1,0:T(8,128)(2,1)S(1)} custom-call(s32[3]{0:T(128)S(1)} %pad_add_fusion.place, bf16[256,1536]{1,0:T(8,128)(2,1)S(1)} %copy-done.2, bf16[4,4,48,1152]{3,2,1,0:T(8,128)(2,1)S(1)} %all-to-all-done.3.w_own, bf16[4,4,48,1152]{3,2,1,0:T(8,128)(2,1)S(1)} %collective-permute-done.2.w_oth), custom_call_target="tpu_custom_call" | custom-call | tf_op jit(solution)/shard_map/q/pallas_call | solution.py:262
  117.0 0.7 copy-done.5
  117.6 8.4 %attn.1 = (bf16[8,128,128]{2,1,0:T(8,128)(2,1)}, bf16[128,384]{1,0:T(8,128)(2,1)}, bf16[128,384]{1,0:T(8,128)(2,1)}) custom-call(s32[3]{0:T(128)} %copy-done.7, bf16[256,384]{1,0:T(8,128)(2,1)} %copy-done.5, bf16[8,272,768]{2,1,0:T(8,128)(2,1)} %bitcast.15, bf16[8,128,128]{2,1,0:T(8,128)(2,1)} %bitcast.16, bf16[8,128,128]{2,1,0:T(8,128)(2,1)} %copy-done.13, ...), custom_call_target="tpu_custom_call" | custom-call | flops 10000000000 | bytes 1048576 | tf_op jit(solution)/shard_map/attn/pallas_call | solution.py:275
  126.1 6.5 %collective-permute-start.4 = (bf16[128,384]{1,0:T(8,128)(2,1)}, bf16[128,384]{1,0:T(8,128)(2,1)S(1)}, u32[]{:S(2)}, u32[]{:S(2)}) collective-permute-start(bf16[128,384]{1,0:T(8,128)(2,1)} %get-tuple-element.20), channel_id=1, source_target_pairs={{0,8},{8,0},{1,9},{9,1},{2,10},{10,2},{3,11},{11,3},{4,12},{12,4},... | collective-permute-start | bytes 294920 | tf_op jit(solution)/shard_map/ppermute | solution.py:205
  132.6 3.5 %collective-permute-done.4.a_oth = bf16[128,384]{1,0:T(8,128)(2,1)S(1)} collective-permute-done((bf16[128,384]{1,0:T(8,128)(2,1)}, bf16[128,384]{1,0:T(8,128)(2,1)S(1)}, u32[]{:S(2)}, u32[]{:S(2)}) %collective-permute-start.4) | collective-permute-done | bytes 98336 | tf_op jit(solution)/shard_map/ppermute | solution.py:205
  136.1 0.9 copy-done.6
  137.0 3.2 %out.1 = bf16[128,1536]{1,0:T(8,128)(2,1)} custom-call(s32[3]{0:T(128)S(1)} %copy-done.8, bf16[128,1536]{1,0:T(8,128)(2,1)S(1)} %bitcast.12, bf16[128,384]{1,0:T(8,128)(2,1)S(1)} %copy-done.6, bf16[128,384]{1,0:T(8,128)(2,1)S(1)} %collective-permute-done.4.a_oth, bf16[4,4,48,1152]{3,2,1,0:T(8,128)(2,1)S(1)} %all-to-all-done.3.w_own, ...), custom_call_target="tpu_custom_call" | custom-call | tf_op jit(solution)/shard_map/out/pallas_call | solution.py:288
  (33 shorter events, 0.2 us)
Async XLA Ops:
  7.2 103.6 %copy-start = (f32[128,6]{0,1:T(8,128)S(1)}, f32[128,6]{0,1:T(8,128)}, u32[]{:S(2)}) copy-start(f32[128,6]{0,1:T(8,128)} %param.14) | copy-start | bytes 9220
  23.2 7.2 %copy-start.3 = (bf16[1,128,1536]{2,1,0:T(8,128)(2,1)S(1)}, bf16[1,128,1536]{2,1,0:T(8,128)(2,1)}, u32[]{:S(2)}) copy-start(bf16[1,128,1536]{2,1,0:T(8,128)(2,1)} %param.8) | copy-start | bytes 1179652
  23.2 13.7 %copy-start.11 = (f32[1536]{0:T(1024)S(1)}, f32[1536]{0:T(1024)}, u32[]{:S(2)}) copy-start(f32[1536]{0:T(1024)} %param.11) | copy-start | bytes 18436
  23.2 25.9 %all-to-all-start.1 = ((bf16[4,4,48,1024]{3,2,1,0:T(8,128)(2,1)}), bf16[4,4,48,1024]{3,2,1,0:T(8,128)(2,1)S(1)}, u32[]{:S(2)}, u32[]{:S(2)}) async-start(bf16[4,4,48,1024]{3,2,1,0:T(8,128)(2,1)} %broadcast_in_dim.16), calls=%async_computation.1 | async-start | bytes 3145728 | tf_op jit(solution)/shard_map/all_to_all | solution.py:201
  30.4 87.2 %all-gather.3.cloned.1.call-start = ((), (), s32[]{:S(2)}) async-start(), calls=%async_computation.4 | async-start | bytes 3760128 | tf_op jit(solution)/shard_map/all_gather | solution.py:255
  30.4 23.8 %collective-permute-start = (bf16[128,1536]{1,0:T(8,128)(2,1)S(1)}, bf16[128,1536]{1,0:T(8,128)(2,1)S(1)}, u32[]{:S(2)}, u32[]{:S(2)}) collective-permute-start(bf16[128,1536]{1,0:T(8,128)(2,1)S(1)} %bitcast.10), channel_id=1, source_target_pairs={{0,8},{8,0},{1,9},{9,1},{2,10},{10,2},{3,11},{11,3},{4,12},{12,4},... | collective-permute-start | bytes 1179656 | tf_op jit(solution)/shard_map/ppermute | solution.py:205
  37.0 77.0 %copy-start.7 = (s32[3]{0:T(128)}, s32[3]{0:T(128)S(1)}, u32[]{:S(2)}) copy-start(s32[3]{0:T(128)S(1)} %pad_add_fusion.place) | copy-start | bytes 40
  49.1 7.9 %collective-permute-start.3 = (bf16[4,4,48,1024]{3,2,1,0:T(8,128)(2,1)S(1)}, bf16[4,4,48,1024]{3,2,1,0:T(8,128)(2,1)S(1)}, u32[]{:S(2)}, u32[]{:S(2)}) collective-permute-start(bf16[4,4,48,1024]{3,2,1,0:T(8,128)(2,1)S(1)} %all-to-all-done.1.w_own), channel_id=1, source_target_pairs={{0,16},{16,0},{1,17},{17,1},{2,18},{18,2},{3,19},{19,3},{4,20},{20... | collective-permute-start | bytes 4718600 | tf_op jit(solution)/shard_map/ppermute | solution.py:205
  55.0 9.2 %copy-start.1 = (bf16[256,1536]{1,0:T(8,128)(2,1)}, bf16[256,1536]{1,0:T(8,128)(2,1)S(1)}, u32[]{:S(2)}) copy-start(bf16[256,1536]{1,0:T(8,128)(2,1)S(1)} %get-tuple-element.12.normed) | copy-start | bytes 2359300
  57.0 7.8 %copy-start.10 = (bf16[768,48]{0,1:T(8,128)(2,1)S(1)}, bf16[768,48]{0,1:T(8,128)(2,1)}, u32[]{:S(2)}) copy-start(bf16[768,48]{0,1:T(8,128)(2,1)} %param.15) | copy-start | bytes 221188
  64.1 0.6 copy-start.9
  81.4 3.7 %copy-start.12 = (bf16[1,8,128,128]{3,2,1,0:T(8,128)(2,1)S(1)}, bf16[1,8,128,128]{3,2,1,0:T(8,128)(2,1)}, u32[]{:S(2)}) copy-start(bf16[1,8,128,128]{3,2,1,0:T(8,128)(2,1)} %param.9) | copy-start | bytes 786436
  81.4 25.1 %all-to-all-start.3 = ((bf16[4,4,48,1152]{3,2,1,0:T(8,128)(2,1)}), bf16[4,4,48,1152]{3,2,1,0:T(8,128)(2,1)S(1)}, u32[]{:S(2)}, u32[]{:S(2)}) async-start(bf16[4,4,48,1152]{3,2,1,0:T(8,128)(2,1)} %broadcast_in_dim.18), calls=%async_computation.3 | async-start | bytes 3538944 | tf_op jit(solution)/shard_map/all_to_all | solution.py:201
  85.1 17.9 %collective-permute-start.1 = (bf16[8,128,128]{2,1,0:T(8,128)(2,1)S(1)}, bf16[8,128,128]{2,1,0:T(8,128)(2,1)S(1)}, u32[]{:S(2)}, u32[]{:S(2)}) collective-permute-start(bf16[8,128,128]{2,1,0:T(8,128)(2,1)S(1)} %bitcast.17), channel_id=1, source_target_pairs={{0,8},{8,0},{1,9},{9,1},{2,10},{10,2},{3,11},{11,3},{4,12},{12,4},... | collective-permute-start | bytes 786440 | tf_op jit(solution)/shard_map/ppermute | solution.py:205
  103.0 0.7 copy-start.13
  106.5 7.5 %collective-permute-start.2 = (bf16[4,4,48,1152]{3,2,1,0:T(8,128)(2,1)S(1)}, bf16[4,4,48,1152]{3,2,1,0:T(8,128)(2,1)S(1)}, u32[]{:S(2)}, u32[]{:S(2)}) collective-permute-start(bf16[4,4,48,1152]{3,2,1,0:T(8,128)(2,1)S(1)} %all-to-all-done.3.w_own), channel_id=1, source_target_pairs={{0,16},{16,0},{1,17},{17,1},{2,18},{18,2},{3,19},{19,3},{4,20},{20... | collective-permute-start | bytes 5308424 | tf_op jit(solution)/shard_map/ppermute | solution.py:205
  114.0 1.1 copy-start.2
  117.0 0.7 copy-start.5
  117.6 18.5 %copy-start.4 = (bf16[1,128,1536]{2,1,0:T(8,128)(2,1)S(1)}, bf16[1,128,1536]{2,1,0:T(8,128)(2,1)}, u32[]{:S(2)}) copy-start(bf16[1,128,1536]{2,1,0:T(8,128)(2,1)} %param.8) | copy-start | bytes 1179652
  117.6 18.5 %copy-start.8 = (s32[3]{0:T(128)S(1)}, s32[3]{0:T(128)}, u32[]{:S(2)}) copy-start(s32[3]{0:T(128)} %copy-done.7) | copy-start | bytes 40
  126.1 10.0 %collective-permute-start.4 = (bf16[128,384]{1,0:T(8,128)(2,1)}, bf16[128,384]{1,0:T(8,128)(2,1)S(1)}, u32[]{:S(2)}, u32[]{:S(2)}) collective-permute-start(bf16[128,384]{1,0:T(8,128)(2,1)} %get-tuple-element.20), channel_id=1, source_target_pairs={{0,8},{8,0},{1,9},{9,1},{2,10},{10,2},{3,11},{11,3},{4,12},{12,4},... | collective-permute-start | bytes 294920 | tf_op jit(solution)/shard_map/ppermute | solution.py:205
  136.1 0.9 copy-start.6
Sparse Core Ops, SparseCore 0:
  64.9 52.1 all-gather.2

commit v5 on v4

v5 whole, which is shorter than its diff:
```python
import functools

import jax
import jax.numpy as jnp
from jax import lax
from jax.experimental import pallas as pl
from jax.experimental.pallas import tpu as pltpu
from jax.sharding import Mesh, PartitionSpec as P

HEADS = 6
HD = 128
CP = 128
POOL = 16
HALF = HEADS // 2
HW = HALF * HD
VMEM = 14 * 1024 * 1024

BF = jnp.bfloat16
F32 = jnp.float32

AXES = ("yl", "x", "c", "yh", "z")
SIZES = (4, 4, 2, 2, 8)
DP, SEQ = AXES[:3], AXES[3:]
NY, NX, NZ = 4, 4, 8


def params():
    return pltpu.CompilerParams(vmem_limit_bytes=VMEM)


def cost(gflop):
    return pl.CostEstimate(flops=gflop * 10**9, bytes_accessed=1 << 20, transcendentals=0)


def vm():
    return pl.BlockSpec(memory_space=pltpu.VMEM)


def sm():
    return pl.BlockSpec(memory_space=pltpu.SMEM)


def hbm():
    return pl.BlockSpec(memory_space=pl.ANY)


def nt(a, b):
    return lax.dot_general(a, b, (((1,), (1,)), ((), ())), preferred_element_type=F32)


def split(x):
    hi = x.astype(BF)
    return hi, (x - hi.astype(F32)).astype(BF)


def weight_copies(place, own, other, buf, sem):
    return [
        pltpu.make_async_copy(src.at[x], buf.at[:, x, core], sem.at[which, x])
        for which, src, core in ((0, own, place[1]), (1, other, 1 - place[1]))
        for x in range(NX)
    ]


def rows_of(buf):
    x = buf[...]
    return x.reshape(-1, x.shape[-1])


def project(means, w):
    both = jnp.dot(means, w, preferred_element_type=F32)
    half = both.shape[0] // 2
    return (both[:half] + both[half:]).astype(BF)


def norm_rows(x, gain):
    f = x.astype(F32)
    meansq = jnp.mean(f * f, axis=-1, keepdims=True)
    return (f * lax.rsqrt(meansq + 1e-06) * gain).astype(BF)


def norm_body(x_own, x_oth, gain, normed, means):
    rows, depth = x_own.shape
    g = gain[...]
    parts = []
    for at, x in ((0, x_own), (rows, x_oth)):
        n = norm_rows(x[...], g)
        normed[at : at + rows, :] = n
        parts.append(n.astype(F32).reshape(rows // POOL, POOL, depth).mean(axis=1))
    hi, lo = split(jnp.concatenate(parts, axis=0))
    means[...] = jnp.concatenate([hi, lo], axis=0)


def kv_body(place, normed, means, w_own, w_oth, kv, buf, sem):
    copies = weight_copies(place, w_own, w_oth, buf, sem)
    for c in copies:
        c.start()
    for c in copies:
        c.wait()
    w = rows_of(buf)
    n = normed.shape[0]
    kv[:n, :] = jnp.dot(normed[...], w[:, : 2 * HW], preferred_element_type=F32).astype(BF)
    right = project(means[...], w[:, 2 * HW :])
    kv[n:, :CP] = right
    kv[n:, CP:] = jnp.zeros((right.shape[0], 2 * HW - CP), BF)


def q_body(place, normed, means, w_own, w_oth, q, left, buf, sem):
    copies = weight_copies(place, w_own, w_oth, buf, sem)
    for c in copies:
        c.start()
    for c in copies:
        c.wait()
    w = rows_of(buf)
    q[...] = jnp.dot(normed[...], w[:, CP:], preferred_element_type=F32).astype(BF)
    left[...] = project(means[...], w[:, :CP]).astype(F32)


def pair_bias_body(pair_in, wt, bias):
    w = wt[...]
    for i in range(pair_in.shape[0]):
        both = nt(w, pair_in[i])
        bias[i] = both[:8] + both[8:]


def attn_body(place, q_at, kvg_at, pair_own_at, bias_oth, left, wt, wt32, pair_out, own, oth, *held):
    feats, pair_own, q, kvg, sem = held
    rows = q.shape[0] // 2
    copies = [
        pltpu.make_async_copy(src, dst, sem.at[i])
        for i, (src, dst) in enumerate(
            (
                (kvg_at.at[:, pl.ds(2 * rows, feats.shape[1]), pl.ds(0, CP)], feats),
                (pair_own_at, pair_own),
                (q_at, q),
                (kvg_at.at[:, pl.ds(0, 2 * rows), :], kvg),
            )
        )
    ]
    for c in copies:
        c.start()
    side = place[0]
    limit = place[2]
    nz = kvg.shape[0]
    npr = rows // POOL
    nrow = 2 * rows
    width = nz * nrow
    half_bins = nz * rows
    npair = half_bins * 2 // POOL
    scale = 1.0 / (HD**0.5)

    for c in copies[:2]:
        c.wait()
    slots = ([], [])
    for z in range(nz):
        r = feats[z].astype(F32)
        slots[0].append(r[:npr])
        slots[1].append(r[npr:])
    first, second = (jnp.concatenate(x, axis=0) for x in slots)
    right = jnp.concatenate(
        [jnp.where(side == 0, first, second), jnp.where(side == 0, second, first)], axis=0
    )
    w = wt[...]

    col = lax.broadcasted_iota(jnp.int32, (1, width), 1)
    within = col % nrow
    yh = jnp.where(within // rows == 0, side, 1 - side)
    bin_at = yh * half_bins + (col // nrow) * rows + within % rows
    live = bin_at < limit
    onehot = (lax.broadcasted_iota(jnp.int32, (npair, width), 0) == bin_at // POOL).astype(F32)
    onehot = onehot.astype(BF)

    biases = []
    for i in range(npr):
        out = (pair_own[i].astype(F32) + left[i : i + 1, :] * right).astype(BF)
        pair_out[i] = out
        both = nt(w, out)
        biases.append(both[:8] + both[8:])
    biases = [jnp.stack(biases)]
    lw = (left[npr:, :][:, None, :] * wt32[...][None, :, :]).reshape(8 * npr, CP)
    feats_bf = right.astype(BF)
    hi, lo = split(lw)
    biases.append(bias_oth[...] + (nt(hi, feats_bf) + nt(lo, feats_bf)).reshape(npr, 8, npair))
    parts = [pb[:, h, :] for pb in biases for h in range(HALF)]
    hi, lo = split(jnp.concatenate(parts, axis=0))
    bias = jnp.dot(hi, onehot, preferred_element_type=F32) + jnp.dot(lo, onehot, preferred_element_type=F32)
    bias = jnp.where(live, bias, F32(-1e30))
    for c in copies[2:]:
        c.wait()

    for h in range(HALF):
        k = kvg[:, :, h * HD : (h + 1) * HD].reshape(width, HD)
        v = kvg[:, :, HW + h * HD : HW + (h + 1) * HD].reshape(width, HD)
        for s, dest in enumerate((own, oth)):
            qh = q[s * rows : (s + 1) * rows, h * HD : (h + 1) * HD]
            first = (s * HALF + h) * npr
            sc = nt(qh, k) * scale
            sc = sc.reshape(npr, POOL, width) + bias[first : first + npr, None, :]
            sc = sc.reshape(rows, width)
            top = jnp.max(sc, axis=-1, keepdims=True)
            e = jnp.exp(sc - top)
            total = jnp.sum(e, axis=-1, keepdims=True)
            acc = jnp.dot(e.astype(BF), v, preferred_element_type=F32)
            dest[:, h * HD : (h + 1) * HD] = (acc / total).astype(BF)


def out_body(place, x_own, a_own, a_oth, w_own, w_oth, mixed, buf, sem, full):
    copies = weight_copies(place, w_own, w_oth, buf, sem)
    for c in copies:
        c.start()
    side = place[0]
    full[:, pl.ds(pl.multiple_of(side * HW, 128), HW)] = a_own[...]
    full[:, pl.ds(pl.multiple_of((1 - side) * HW, 128), HW)] = a_oth[...]
    for c in copies:
        c.wait()
    update = nt(full[...], rows_of(buf))
    mixed[...] = (x_own[...].astype(F32) + update).astype(BF)


def spread(x, axis, n):
    return lax.all_to_all(jnp.broadcast_to(x[None], (n,) + x.shape), axis, 0, 0, tiled=True)


def swap(x, axis):
    return lax.ppermute(x, axis, [(0, 1), (1, 0)])


def after(x, *others):
    return lax.optimization_barrier((x,) + others)[0]


def on_device(bins, pair_in, valid, gain, w_qkv, w_pair, w_bias, w_out):
    side = lax.axis_index("yh")
    core = lax.axis_index("c")
    place = jnp.stack([side, core, valid[0]]).astype(jnp.int32)
    x_own = bins[0]
    rows, depth = x_own.shape
    npr = rows // POOL
    shard = w_qkv.shape[0]

    def mine(first):
        return lax.dynamic_slice_in_dim(w_qkv, first * HEADS * HD + side * HW, HW, axis=1)

    def weights(n):
        return [pltpu.VMEM((NY, NX, 2, shard, n), BF), pltpu.SemaphoreType.DMA((2, NX))]

    def heads(at):
        x = lax.dynamic_slice_in_dim(w_bias.T, at * HALF, HALF, axis=0)
        x = jnp.concatenate([x, jnp.zeros((8 - HALF, CP), F32)], axis=0)
        return x, jnp.concatenate(split(x), axis=0)

    wt32, wt = heads(side)
    bias_for_oth = pl.pallas_call(
        pair_bias_body,
        out_shape=jax.ShapeDtypeStruct((npr, 8, pair_in.shape[2]), F32),
        in_specs=[vm()] * 2,
        out_specs=vm(),
        compiler_params=params(),
        name="pair_bias",
    )(pair_in[0], heads(1 - side)[1])

    x_oth = swap(x_own, "yh")
    w = jnp.concatenate([mine(1), mine(2), w_pair[:, CP:]], axis=1)
    w = spread(spread(w, "yl", NY), "x", NX)
    normed, means = pl.pallas_call(
        norm_body,
        out_shape=(
            jax.ShapeDtypeStruct((2 * rows, depth), BF),
            jax.ShapeDtypeStruct((4 * npr, depth), BF),
        ),
        in_specs=[vm()] * 3,
        out_specs=(vm(), vm()),
        compiler_params=params(),
        cost_estimate=cost(20),
        name="norm",
    )(x_own, x_oth, gain[None])
    w_oth = swap(w, "c")
    kv = pl.pallas_call(
        kv_body,
        out_shape=jax.ShapeDtypeStruct((2 * rows + 2 * npr, 2 * HW), BF),
        in_specs=[sm(), vm(), vm(), hbm(), hbm()],
        out_specs=vm(),
        scratch_shapes=weights(2 * HW + CP),
        compiler_params=params(),
        cost_estimate=cost(10),
        name="kv",
    )(place, normed, means, w, w_oth)
    kvg = lax.all_gather(kv, "z", axis=0)

    u = jnp.concatenate([w_pair[:, :CP], mine(0), w_out.T], axis=1)
    u = spread(after(u, w), "yl", NY)
    bias_oth = swap(after(bias_for_oth, u), "yh")
    u, wo = u[:, :, : CP + HW], u[:, :, CP + HW :]
    u = after(spread(u, "x", NX), bias_oth)
    q, left = pl.pallas_call(
        q_body,
        out_shape=(jax.ShapeDtypeStruct((2 * rows, HW), BF), jax.ShapeDtypeStruct((2 * npr, CP), F32)),
        in_specs=[sm(), vm(), vm(), hbm(), hbm()],
        out_specs=(vm(), vm()),
        scratch_shapes=weights(CP + HW),
        compiler_params=params(),
        name="q",
    )(place, normed, means, u, swap(u, "c"))
    wo = spread(after(wo, u), "x", NX)

    pair_out, own, oth = pl.pallas_call(
        attn_body,
        out_shape=(jax.ShapeDtypeStruct(pair_in.shape[1:], BF),)
        + (jax.ShapeDtypeStruct((rows, HW), BF),) * 2,
        in_specs=[sm()] + [hbm()] * 3 + [vm()] * 4,
        out_specs=(vm(), vm(), vm()),
        scratch_shapes=[
            pltpu.VMEM(shape, BF)
            for shape in (
                (NZ, 2 * npr, CP),
                pair_in.shape[1:],
                q.shape,
                (NZ, 2 * rows, 2 * HW),
            )
        ]
        + [pltpu.SemaphoreType.DMA((4,))],
        compiler_params=pltpu.CompilerParams(vmem_limit_bytes=56 * 1024 * 1024),
        cost_estimate=cost(10),
        name="attn",
    )(place, q, kvg, pair_in[0], bias_oth, left, wt, wt32)
    got = swap(oth, "yh")
    wo_oth = swap(after(wo, oth), "c")
    mixed = pl.pallas_call(
        out_body,
        out_shape=jax.ShapeDtypeStruct((rows, depth), BF),
        in_specs=[sm(), vm(), vm(), vm(), hbm(), hbm()],
        out_specs=vm(),
        scratch_shapes=weights(HEADS * HD) + [pltpu.VMEM((rows, HEADS * HD), BF)],
        compiler_params=params(),
        name="out",
    )(place, x_own, own, got, wo, wo_oth)
    return (mixed[None], pair_out[None])


def solution(mesh):
    fine = Mesh(mesh.devices.reshape(SIZES), AXES)
    placed = (
        P(DP, SEQ, None),
        P(DP, SEQ, None, None),
        P(DP),
        P(),
        P(DP, None),
        P(DP, None),
        P(),
        P(None, DP),
    )
    return jax.shard_map(
        on_device,
        mesh=fine,
        in_specs=placed,
        out_specs=(P(DP, SEQ, None), P(DP, SEQ, None, None)),
        check_vma=False,
    )
```

time: 150 us -> 144 us (0.960)
  waiting for transfers between devices: 35.7 us -> 28.6 us
  Pallas kernels: 21.3 us -> 14.9 us
  starting transfers between devices: 37.9 us -> 44.2 us
    ppermute x5 -> x6, waiting for transfers between devices: 20.8 us -> 9.29 us  [swap(): return lax.ppermute(x, axis, [(0, 1), (1, 0)])]
    all_gather x1, waiting for transfers between devices: 0.01 us -> 7.75 us  [on_device(): kvg = lax.all_gather(kv, 'z', axis=0)]
    pallas_call x2 -> x3, Pallas kernels: 8.92 us -> 4.59 us  [the longest x1 2.62 us: on_device(): pl.pallas_call(kv_body, out_shape=jax.ShapeDtypeStruct((2 * rows + 2 * np...]
    all_to_all x2 -> x3, starting transfers between devices: 10.9 us -> 14.4 us  [spread(): lax.all_to_all(jnp.broadcast_to(x[None], (n,) + x.shape), axis, 0, 0, til...]
    all_to_all x2 -> x3, waiting for transfers between devices: 14.8 us -> 11.5 us  [spread(): lax.all_to_all(jnp.broadcast_to(x[None], (n,) + x.shape), axis, 0, 0, til...]
    ppermute x5 -> x6, starting transfers between devices: 27 us -> 29.7 us  [swap(): return lax.ppermute(x, axis, [(0, 1), (1, 0)])]
    broadcast_in_dim x4 -> x5, local copies, waits for them, and re-layouts: 2.81 us -> 3.34 us  [spread(): jnp.broadcast_to(x[None], (n,) + x.shape)]
  transfers between devices with their start and end apart: 8 -> 10, of which waited for: 7 -> 6; matrix products, arithmetic and copies ran while one was open for 1% -> 2% of each run, Pallas kernels for 2% -> 7%
where the time goes in v5:
time: 144 us; the launch traced here: 141 us
  starting transfers between devices  44.2 us (31%)
  blocking collectives  29.4 us (20%)
  waiting for transfers between devices  28.6 us (20%)
  between operations  15 us (10%)
  Pallas kernels  14.9 us (10%)
  local copies, waits for them, and re-layouts  8.02 us (6%)
    ppermute x6, starting transfers between devices, swap(): return lax.ppermute(x, axis, [(0, 1), (1, 0)])  29.7 us
    all_to_all x2, blocking collectives, spread(): lax.all_to_all(jnp.broadcast_to(x[None], (n,) + x.shape), axis, 0, 0, til...  29.4 us
    all_to_all x3, starting transfers between devices, spread(): lax.all_to_all(jnp.broadcast_to(x[None], (n,) + x.shape), axis, 0, 0, til...  14.4 us
    all_to_all x3, waiting for transfers between devices, spread(): lax.all_to_all(jnp.broadcast_to(x[None], (n,) + x.shape), axis, 0, 0, til...  11.5 us
    ppermute x6, waiting for transfers between devices, swap(): return lax.ppermute(x, axis, [(0, 1), (1, 0)])  9.29 us
    all_gather x1, waiting for transfers between devices, on_device(): kvg = lax.all_gather(kv, 'z', axis=0)  7.75 us
    pallas_call x1, Pallas kernels, on_device(): pl.pallas_call(attn_body, out_shape=(jax.ShapeDtypeStruct(pair_in.shape[1...  7.02 us
    broadcast_in_dim x5, local copies, waits for them, and re-layouts, spread(): jnp.broadcast_to(x[None], (n,) + x.shape)  3.34 us
  transfers between devices with their start and end apart: 10, of which 6 were waited for; matrix products, arithmetic and copies ran while one was open for 2% of the time, Pallas kernels for 7%

profile of v5, /device:TPU:1, one launch (start us, length us, event | category | flops | bytes accessed | tf_op | source)
XLA Modules:
  0.0 141.4 jit_solution(18369597751015700454)
XLA Ops:
  7.2 0.7 fusion.1
  7.9 0.8 constant_dynamic-slice_fusion.1
  8.8 12.5 %all_to_all.25 = bf16[4,48,896]{2,1,0:T(8,128)(2,1)S(1)} all-to-all(bf16[4,48,896]{2,1,0:T(8,128)(2,1)S(1)} %broadcast_in_dim.17), channel_id=1, replica_groups=mesh['yl'=4,'x'=4,'c'=2,'yh'=2,'z'=8] {'yl'}, dimensions={0} | all-to-all | bytes 688128 | tf_op jit(solution)/shard_map/all_to_all | solution.py:220
  21.3 1.2 broadcast_in_dim.18
  22.5 6.6 %all-to-all-start.1 = ((bf16[4,4,48,896]{3,2,1,0:T(8,128)(2,1)}), bf16[4,4,48,896]{3,2,1,0:T(8,128)(2,1)S(1)}, u32[]{:S(2)}, u32[]{:S(2)}) async-start(bf16[4,4,48,896]{3,2,1,0:T(8,128)(2,1)} %broadcast_in_dim.18), calls=%async_computation.1 | async-start | bytes 2752512 | tf_op jit(solution)/shard_map/all_to_all | solution.py:220
  29.2 5.5 %collective-permute-start = (bf16[128,1536]{1,0:T(8,128)(2,1)S(1)}, bf16[128,1536]{1,0:T(8,128)(2,1)S(1)}, u32[]{:S(2)}, u32[]{:S(2)}) collective-permute-start(bf16[128,1536]{1,0:T(8,128)(2,1)S(1)} %bitcast.12), channel_id=1, source_target_pairs={{0,8},{8,0},{1,9},{9,1},{2,10},{10,2},{3,11},{11,3},{4,12},{12,4},... | collective-permute-start | bytes 1179656 | tf_op jit(solution)/shard_map/ppermute | solution.py:224
  35.4 10.3 %all-to-all-done.1.w_own = bf16[4,4,48,896]{3,2,1,0:T(8,128)(2,1)S(1)} async-done(((bf16[4,4,48,896]{3,2,1,0:T(8,128)(2,1)}), bf16[4,4,48,896]{3,2,1,0:T(8,128)(2,1)S(1)}, u32[]{:S(2)}, u32[]{:S(2)}) %all-to-all-start.1) | async-done | bytes 1376288 | tf_op jit(solution)/shard_map/all_to_all | solution.py:220
  45.7 4.9 %collective-permute-start.3 = (bf16[4,4,48,896]{3,2,1,0:T(8,128)(2,1)S(1)}, bf16[4,4,48,896]{3,2,1,0:T(8,128)(2,1)S(1)}, u32[]{:S(2)}, u32[]{:S(2)}) collective-permute-start(bf16[4,4,48,896]{3,2,1,0:T(8,128)(2,1)S(1)} %all-to-all-done.1.w_own), channel_id=1, source_target_pairs={{0,16},{16,0},{1,17},{17,1},{2,18},{18,2},{3,19},{19,3},{4,20},{20... | collective-permute-start | bytes 4128776 | tf_op jit(solution)/shard_map/ppermute | solution.py:224
  50.6 2.0 %collective-permute-done.x_oth = bf16[128,1536]{1,0:T(8,128)(2,1)S(1)} collective-permute-done((bf16[128,1536]{1,0:T(8,128)(2,1)S(1)}, bf16[128,1536]{1,0:T(8,128)(2,1)S(1)}, u32[]{:S(2)}, u32[]{:S(2)}) %collective-permute-start) | collective-permute-done | bytes 393248 | tf_op jit(solution)/shard_map/ppermute | solution.py:224
  52.6 0.8 norm.1
  53.4 2.6 %kv.1 = bf16[272,768]{1,0:T(8,128)(2,1)} custom-call(s32[3]{0:T(128)S(1)} %pad_add_fusion.place, bf16[256,1536]{1,0:T(8,128)(2,1)S(1)} %get-tuple-element.14.normed, bf16[32,1536]{1,0:T(8,128)(2,1)S(1)} %get-tuple-element.15.means, bf16[4,4,48,896]{3,2,1,0:T(8,128)(2,1)S(1)} %all-to-all-done.1.w_own, bf16[4,4,48,896]{3,2,1,0:T(8,128)(2,1)S(1)} %collective-permute-done.3.w_oth), custom_call_target="tpu_custom_call" | custom-call | flops 10000000000 | bytes 1048576 | tf_op jit(solution)/shard_map/kv/pallas_call | solution.py:277
  56.2 16.9 %all_to_all.26 = bf16[4,48,1280]{2,1,0:T(8,128)(2,1)S(1)} all-to-all(bf16[4,48,1280]{2,1,0:T(8,128)(2,1)S(1)} %broadcast_in_dim.19), channel_id=1, replica_groups=mesh['yl'=4,'x'=4,'c'=2,'yh'=2,'z'=8] {'yl'}, dimensions={0} | all-to-all | bytes 983040 | tf_op jit(solution)/shard_map/all_to_all | solution.py:220
  73.1 1.0 broadcast_in_dim.20
  74.0 4.2 %all-to-all-start.3 = ((bf16[4,4,48,512]{3,2,1,0:T(8,128)(2,1)}), bf16[4,4,48,512]{3,2,1,0:T(8,128)(2,1)S(1)}, u32[]{:S(2)}, u32[]{:S(2)}) async-start(bf16[4,4,48,512]{3,2,1,0:T(8,128)(2,1)} %broadcast_in_dim.20), calls=%async_computation.3 | async-start | bytes 1572864 | tf_op jit(solution)/shard_map/all_to_all | solution.py:220
  78.6 4.6 %collective-permute-start.1 = (f32[8,8,128]{2,1,0:T(8,128)S(1)}, f32[8,8,128]{2,1,0:T(8,128)S(1)}, u32[]{:S(2)}, u32[]{:S(2)}) collective-permute-start(f32[8,8,128]{2,1,0:T(8,128)S(1)} %pair_bias.1), channel_id=1, source_target_pairs={{0,8},{8,0},{1,9},{9,1},{2,10},{10,2},{3,11},{11,3},{4,12},{12,4},... | collective-permute-start | bytes 98312 | tf_op jit(solution)/shard_map/ppermute | solution.py:224
  83.2 3.9 %collective-permute-done.1.bias_oth = f32[8,8,128]{2,1,0:T(8,128)S(1)} collective-permute-done((f32[8,8,128]{2,1,0:T(8,128)S(1)}, f32[8,8,128]{2,1,0:T(8,128)S(1)}, u32[]{:S(2)}, u32[]{:S(2)}) %collective-permute-start.1) | collective-permute-done | bytes 32800 | tf_op jit(solution)/shard_map/ppermute | solution.py:224
  87.2 1.2 all-to-all-done.3.w_own
  88.4 5.1 %collective-permute-start.2 = (bf16[4,4,48,512]{3,2,1,0:T(8,128)(2,1)S(1)}, bf16[4,4,48,512]{3,2,1,0:T(8,128)(2,1)S(1)}, u32[]{:S(2)}, u32[]{:S(2)}) collective-permute-start(bf16[4,4,48,512]{3,2,1,0:T(8,128)(2,1)S(1)} %all-to-all-done.3.w_own), channel_id=1, source_target_pairs={{0,16},{16,0},{1,17},{17,1},{2,18},{18,2},{3,19},{19,3},{4,20},{20... | collective-permute-start | bytes 2359304 | tf_op jit(solution)/shard_map/ppermute | solution.py:224
  93.5 0.6 fusion.2
  94.0 0.6 pad_maximum_fusion.3.wt
  94.7 1.1 broadcast_in_dim.21
  95.8 3.5 %all-to-all-start.4 = ((bf16[4,4,48,768]{3,2,1,0:T(8,128)(2,1)}), bf16[4,4,48,768]{3,2,1,0:T(8,128)(2,1)S(1)}, u32[]{:S(2)}, u32[]{:S(2)}) async-start(bf16[4,4,48,768]{3,2,1,0:T(8,128)(2,1)} %broadcast_in_dim.21), calls=%async_computation.4 | async-start | bytes 2359296 | tf_op jit(solution)/shard_map/all_to_all | solution.py:220
  99.4 0.9 copy-done.5
  100.2 1.7 %q.1 = (bf16[256,384]{1,0:T(8,128)(2,1)S(1)}, f32[16,128]{1,0:T(8,128)S(1)}) custom-call(s32[3]{0:T(128)S(1)} %pad_add_fusion.place, bf16[256,1536]{1,0:T(8,128)(2,1)S(1)} %get-tuple-element.14.normed, bf16[32,1536]{1,0:T(8,128)(2,1)S(1)} %copy-done.5, bf16[4,4,48,512]{3,2,1,0:T(8,128)(2,1)S(1)} %all-to-all-done.3.w_own, ...), custom_call_target="tpu_custom_call" | custom-call | tf_op jit(solution)/shard_map/q/pallas_call | solution.py:294
  102.0 0.7 copy-done.8
  103.3 7.8 %all-gather.3.cloned.1.call-done = bf16[2176,768]{1,0:T(8,128)(2,1)} async-done(((bf16[272,768]{1,0:T(8,128)(2,1)}), bf16[2176,768]{1,0:T(8,128)(2,1)}) %all-gather.3.cloned.1.call-update) | async-done | bytes 3342352 | tf_op jit(solution)/shard_map/all_gather | solution.py:287
  111.0 7.0 %attn.1 = (bf16[8,128,128]{2,1,0:T(8,128)(2,1)}, bf16[128,384]{1,0:T(8,128)(2,1)}, bf16[128,384]{1,0:T(8,128)(2,1)}) custom-call(s32[3]{0:T(128)} %copy-done.6, bf16[256,384]{1,0:T(8,128)(2,1)} %copy-done.8, bf16[8,272,768]{2,1,0:T(8,128)(2,1)} %bitcast.19, bf16[8,128,128]{2,1,0:T(8,128)(2,1)} %bitcast.15, f32[8,8,128]{2,1,0:T(8,128)} %copy-done.13, ...), custom_call_target="tpu_custom_call" | custom-call | flops 10000000000 | bytes 1048576 | tf_op jit(solution)/shard_map/attn/pallas_call | solution.py:305
  118.1 2.6 %collective-permute-start.5 = (bf16[4,4,48,768]{3,2,1,0:T(8,128)(2,1)S(1)}, bf16[4,4,48,768]{3,2,1,0:T(8,128)(2,1)S(1)}, u32[]{:S(2)}, u32[]{:S(2)}) collective-permute-start(bf16[4,4,48,768]{3,2,1,0:T(8,128)(2,1)S(1)} %all-to-all-done.4.w_own), channel_id=1, source_target_pairs={{0,16},{16,0},{1,17},{17,1},{2,18},{18,2},{3,19},{19,3},{4,20},{20... | collective-permute-start | bytes 3538952 | tf_op jit(solution)/shard_map/ppermute | solution.py:224
  120.6 7.1 %collective-permute-start.4 = (bf16[128,384]{1,0:T(8,128)(2,1)}, bf16[128,384]{1,0:T(8,128)(2,1)S(1)}, u32[]{:S(2)}, u32[]{:S(2)}) collective-permute-start(bf16[128,384]{1,0:T(8,128)(2,1)} %get-tuple-element.22), channel_id=1, source_target_pairs={{0,8},{8,0},{1,9},{9,1},{2,10},{10,2},{3,11},{11,3},{4,12},{12,4},... | collective-permute-start | bytes 294920 | tf_op jit(solution)/shard_map/ppermute | solution.py:224
  127.7 3.3 %collective-permute-done.4.a_oth = bf16[128,384]{1,0:T(8,128)(2,1)S(1)} collective-permute-done((bf16[128,384]{1,0:T(8,128)(2,1)}, bf16[128,384]{1,0:T(8,128)(2,1)S(1)}, u32[]{:S(2)}, u32[]{:S(2)}) %collective-permute-start.4) | collective-permute-done | bytes 98336 | tf_op jit(solution)/shard_map/ppermute | solution.py:224
  131.1 0.9 copy-done.3
  132.0 2.5 %out.1 = bf16[128,1536]{1,0:T(8,128)(2,1)} custom-call(s32[3]{0:T(128)S(1)} %copy-done.7, bf16[128,1536]{1,0:T(8,128)(2,1)S(1)} %bitcast.14, bf16[128,384]{1,0:T(8,128)(2,1)S(1)} %copy-done.3, bf16[128,384]{1,0:T(8,128)(2,1)S(1)} %collective-permute-done.4.a_oth, bf16[4,4,48,768]{3,2,1,0:T(8,128)(2,1)S(1)} %all-to-all-done.4.w_own, ...), custom_call_target="tpu_custom_call" | custom-call | tf_op jit(solution)/shard_map/out/pallas_call | solution.py:327
  (45 shorter events, 1.1 us)
Async XLA Ops:
  22.5 6.6 %copy-start = (bf16[1,128,1536]{2,1,0:T(8,128)(2,1)S(1)}, bf16[1,128,1536]{2,1,0:T(8,128)(2,1)}, u32[]{:S(2)}) copy-start(bf16[1,128,1536]{2,1,0:T(8,128)(2,1)} %param.8) | copy-start | bytes 1179652
  22.5 12.8 %copy-start.11 = (f32[1536]{0:T(1024)S(1)}, f32[1536]{0:T(1024)}, u32[]{:S(2)}) copy-start(f32[1536]{0:T(1024)} %param.11) | copy-start | bytes 18436
  22.5 23.2 %all-to-all-start.1 = ((bf16[4,4,48,896]{3,2,1,0:T(8,128)(2,1)}), bf16[4,4,48,896]{3,2,1,0:T(8,128)(2,1)S(1)}, u32[]{:S(2)}, u32[]{:S(2)}) async-start(bf16[4,4,48,896]{3,2,1,0:T(8,128)(2,1)} %broadcast_in_dim.18), calls=%async_computation.1 | async-start | bytes 2752512 | tf_op jit(solution)/shard_map/all_to_all | solution.py:220
  29.2 81.9 %all-gather.3.cloned.1.call-start = ((), (), s32[]{:S(2)}) async-start(), calls=%async_computation.5 | async-start | bytes 3760128 | tf_op jit(solution)/shard_map/all_gather | solution.py:287
  29.2 23.5 %collective-permute-start = (bf16[128,1536]{1,0:T(8,128)(2,1)S(1)}, bf16[128,1536]{1,0:T(8,128)(2,1)S(1)}, u32[]{:S(2)}, u32[]{:S(2)}) collective-permute-start(bf16[128,1536]{1,0:T(8,128)(2,1)S(1)} %bitcast.12), channel_id=1, source_target_pairs={{0,8},{8,0},{1,9},{9,1},{2,10},{10,2},{3,11},{11,3},{4,12},{12,4},... | collective-permute-start | bytes 1179656 | tf_op jit(solution)/shard_map/ppermute | solution.py:224
  35.4 63.9 %copy-start.6 = (s32[3]{0:T(128)}, s32[3]{0:T(128)S(1)}, u32[]{:S(2)}) copy-start(s32[3]{0:T(128)S(1)} %pad_add_fusion.place) | copy-start | bytes 40
  45.7 7.7 %collective-permute-start.3 = (bf16[4,4,48,896]{3,2,1,0:T(8,128)(2,1)S(1)}, bf16[4,4,48,896]{3,2,1,0:T(8,128)(2,1)S(1)}, u32[]{:S(2)}, u32[]{:S(2)}) collective-permute-start(bf16[4,4,48,896]{3,2,1,0:T(8,128)(2,1)S(1)} %all-to-all-done.1.w_own), channel_id=1, source_target_pairs={{0,16},{16,0},{1,17},{17,1},{2,18},{18,2},{3,19},{19,3},{4,20},{20... | collective-permute-start | bytes 4128776 | tf_op jit(solution)/shard_map/ppermute | solution.py:224
  53.4 2.7 %copy-start.4 = (bf16[32,1536]{1,0:T(8,128)(2,1)}, bf16[32,1536]{1,0:T(8,128)(2,1)S(1)}, u32[]{:S(2)}) copy-start(bf16[32,1536]{1,0:T(8,128)(2,1)S(1)} %get-tuple-element.15.means) | copy-start | bytes 294916
  53.4 2.7 %copy-start.10 = (bf16[768,48]{0,1:T(8,128)(2,1)S(1)}, bf16[768,48]{0,1:T(8,128)(2,1)}, u32[]{:S(2)}) copy-start(bf16[768,48]{0,1:T(8,128)(2,1)} %param.15) | copy-start | bytes 221188
  73.1 5.2 %copy-start.12 = (f32[128,6]{0,1:T(8,128)S(1)}, f32[128,6]{0,1:T(8,128)}, u32[]{:S(2)}) copy-start(f32[128,6]{0,1:T(8,128)} %param.14) | copy-start | bytes 9220
  73.1 5.3 %copy-start.2 = (bf16[1,8,128,128]{3,2,1,0:T(8,128)(2,1)S(1)}, bf16[1,8,128,128]{3,2,1,0:T(8,128)(2,1)}, u32[]{:S(2)}) copy-start(bf16[1,8,128,128]{3,2,1,0:T(8,128)(2,1)} %param.9) | copy-start | bytes 786436
  74.0 14.3 %all-to-all-start.3 = ((bf16[4,4,48,512]{3,2,1,0:T(8,128)(2,1)}), bf16[4,4,48,512]{3,2,1,0:T(8,128)(2,1)S(1)}, u32[]{:S(2)}, u32[]{:S(2)}) async-start(bf16[4,4,48,512]{3,2,1,0:T(8,128)(2,1)} %broadcast_in_dim.20), calls=%async_computation.3 | async-start | bytes 1572864 | tf_op jit(solution)/shard_map/all_to_all | solution.py:220
  78.6 8.6 %collective-permute-start.1 = (f32[8,8,128]{2,1,0:T(8,128)S(1)}, f32[8,8,128]{2,1,0:T(8,128)S(1)}, u32[]{:S(2)}, u32[]{:S(2)}) collective-permute-start(f32[8,8,128]{2,1,0:T(8,128)S(1)} %pair_bias.1), channel_id=1, source_target_pairs={{0,8},{8,0},{1,9},{9,1},{2,10},{10,2},{3,11},{11,3},{4,12},{12,4},... | collective-permute-start | bytes 98312 | tf_op jit(solution)/shard_map/ppermute | solution.py:224
  87.1 6.3 %copy-start.13 = (f32[8,8,128]{2,1,0:T(8,128)}, f32[8,8,128]{2,1,0:T(8,128)S(1)}, u32[]{:S(2)}) copy-start(f32[8,8,128]{2,1,0:T(8,128)S(1)} %collective-permute-done.1.bias_oth) | copy-start | bytes 98308
  88.4 11.0 %collective-permute-start.2 = (bf16[4,4,48,512]{3,2,1,0:T(8,128)(2,1)S(1)}, bf16[4,4,48,512]{3,2,1,0:T(8,128)(2,1)S(1)}, u32[]{:S(2)}, u32[]{:S(2)}) collective-permute-start(bf16[4,4,48,512]{3,2,1,0:T(8,128)(2,1)S(1)} %all-to-all-done.3.w_own), channel_id=1, source_target_pairs={{0,16},{16,0},{1,17},{17,1},{2,18},{18,2},{3,19},{19,3},{4,20},{20... | collective-permute-start | bytes 2359304 | tf_op jit(solution)/shard_map/ppermute | solution.py:224
  95.8 22.3 %all-to-all-start.4 = ((bf16[4,4,48,768]{3,2,1,0:T(8,128)(2,1)}), bf16[4,4,48,768]{3,2,1,0:T(8,128)(2,1)S(1)}, u32[]{:S(2)}, u32[]{:S(2)}) async-start(bf16[4,4,48,768]{3,2,1,0:T(8,128)(2,1)} %broadcast_in_dim.21), calls=%async_computation.4 | async-start | bytes 2359296 | tf_op jit(solution)/shard_map/all_to_all | solution.py:220
  99.3 0.9 copy-start.5
  102.0 0.7 copy-start.8
  102.7 0.6 copy-start.9
  111.0 20.1 %copy-start.1 = (bf16[1,128,1536]{2,1,0:T(8,128)(2,1)S(1)}, bf16[1,128,1536]{2,1,0:T(8,128)(2,1)}, u32[]{:S(2)}) copy-start(bf16[1,128,1536]{2,1,0:T(8,128)(2,1)} %param.8) | copy-start | bytes 1179652
  111.0 20.1 %copy-start.7 = (s32[3]{0:T(128)S(1)}, s32[3]{0:T(128)}, u32[]{:S(2)}) copy-start(s32[3]{0:T(128)} %copy-done.6) | copy-start | bytes 40
  118.1 13.0 %collective-permute-start.5 = (bf16[4,4,48,768]{3,2,1,0:T(8,128)(2,1)S(1)}, bf16[4,4,48,768]{3,2,1,0:T(8,128)(2,1)S(1)}, u32[]{:S(2)}, u32[]{:S(2)}) collective-permute-start(bf16[4,4,48,768]{3,2,1,0:T(8,128)(2,1)S(1)} %all-to-all-done.4.w_own), channel_id=1, source_target_pairs={{0,16},{16,0},{1,17},{17,1},{2,18},{18,2},{3,19},{19,3},{4,20},{20... | collective-permute-start | bytes 3538952 | tf_op jit(solution)/shard_map/ppermute | solution.py:224
  120.6 10.4 %collective-permute-start.4 = (bf16[128,384]{1,0:T(8,128)(2,1)}, bf16[128,384]{1,0:T(8,128)(2,1)S(1)}, u32[]{:S(2)}, u32[]{:S(2)}) collective-permute-start(bf16[128,384]{1,0:T(8,128)(2,1)} %get-tuple-element.22), channel_id=1, source_target_pairs={{0,8},{8,0},{1,9},{9,1},{2,10},{10,2},{3,11},{11,3},{4,12},{12,4},... | collective-permute-start | bytes 294920 | tf_op jit(solution)/shard_map/ppermute | solution.py:224
  131.1 0.9 copy-start.3
Sparse Core Ops, SparseCore 0:
  56.2 54.7 all-gather.2

commit v6 on v5

--- a/solution.py
+++ b/solution.py
@@ -98,10 +98,10 @@
         c.wait()
     w = rows_of(buf)
     n = normed.shape[0]
-    kv[:n, :] = jnp.dot(normed[...], w[:, : 2 * HW], preferred_element_type=F32).astype(BF)
-    right = project(means[...], w[:, 2 * HW :])
-    kv[n:, :CP] = right
-    kv[n:, CP:] = jnp.zeros((right.shape[0], 2 * HW - CP), BF)
+    both = jnp.dot(normed[...], w[:, : 2 * HW], preferred_element_type=F32).astype(BF)
+    for i in range(2 * HALF):
+        kv[i * n : (i + 1) * n, :] = both[:, i * HD : (i + 1) * HD]
+    kv[2 * HALF * n :, :] = project(means[...], w[:, 2 * HW :])
 
 
 def q_body(place, normed, means, w_own, w_oth, q, left, buf, sem):
@@ -115,24 +115,38 @@
     left[...] = project(means[...], w[:, :CP]).astype(F32)
 
 
-def pair_bias_body(pair_in, wt, bias):
-    w = wt[...]
+def head_weights(w, at):
+    x = jnp.where(at == 0, w[:HALF, :], w[HALF:, :])
+    x = jnp.concatenate([x, jnp.zeros((8 - HALF, x.shape[1]), F32)], axis=0)
+    return x, jnp.concatenate(split(x), axis=0)
+
+
+def pair_bias_body(place, pair_in, w_bias, bias):
+    w = head_weights(w_bias[...], 1 - place[0])[1]
     for i in range(pair_in.shape[0]):
         both = nt(w, pair_in[i])
         bias[i] = both[:8] + both[8:]
 
 
-def attn_body(place, q_at, kvg_at, pair_own_at, bias_oth, left, wt, wt32, pair_out, own, oth, *held):
-    feats, pair_own, q, kvg, sem = held
+def attn_body(place, *refs):
+    q_at, kvg_at, pair_at, bias_at, left_at, w_at, pair_out_at, own, oth = refs[:9]
+    feats, pair_own, q, kvg, bias_oth, left, w_bias, pair_out, sem, sem_out = refs[9:]
     rows = q.shape[0] // 2
     copies = [
         pltpu.make_async_copy(src, dst, sem.at[i])
         for i, (src, dst) in enumerate(
             (
-                (kvg_at.at[:, pl.ds(2 * rows, feats.shape[1]), pl.ds(0, CP)], feats),
-                (pair_own_at, pair_own),
+                (kvg_at.at[:, pl.ds(4 * HALF * rows, feats.shape[1]), :], feats),
+                (pair_at, pair_own),
+                (bias_at, bias_oth),
+                (left_at, left),
+                (w_at, w_bias),
                 (q_at, q),
-                (kvg_at.at[:, pl.ds(0, 2 * rows), :], kvg),
+            )
+            + tuple(
+                (kvg_at.at[:, pl.ds(2 * rows * i, 2 * rows), :], kvg.at[i])
+                for h in range(HALF)
+                for i in (h, HALF + h)
             )
         )
     ]
@@ -140,15 +154,16 @@
         c.start()
     side = place[0]
     limit = place[2]
-    nz = kvg.shape[0]
+    nz = kvg.shape[1]
     npr = rows // POOL
     nrow = 2 * rows
     width = nz * nrow
     half_bins = nz * rows
     npair = half_bins * 2 // POOL
     scale = 1.0 / (HD**0.5)
-
-    for c in copies[:2]:
+    log2e = 1.4426950408889634
+
+    for c in copies[:5]:
         c.wait()
     slots = ([], [])
     for z in range(nz):
@@ -159,7 +174,7 @@
     right = jnp.concatenate(
         [jnp.where(side == 0, first, second), jnp.where(side == 0, second, first)], axis=0
     )
-    w = wt[...]
+    w32, w = head_weights(w_bias[...], side)
 
     col = lax.broadcasted_iota(jnp.int32, (1, width), 1)
     within = col % nrow
@@ -169,42 +184,48 @@
     onehot = (lax.broadcasted_iota(jnp.int32, (npair, width), 0) == bin_at // POOL).astype(F32)
     onehot = onehot.astype(BF)
 
-    biases = []
+    outs = []
     for i in range(npr):
         out = (pair_own[i].astype(F32) + left[i : i + 1, :] * right).astype(BF)
         pair_out[i] = out
-        both = nt(w, out)
-        biases.append(both[:8] + both[8:])
-    biases = [jnp.stack(biases)]
-    lw = (left[npr:, :][:, None, :] * wt32[...][None, :, :]).reshape(8 * npr, CP)
+        outs.append(out)
+    written = pltpu.make_async_copy(pair_out, pair_out_at, sem_out.at[0])
+    written.start()
+    both = nt(w, jnp.concatenate(outs, axis=0))
+    both = both[:8] + both[8:]
+    biases = [jnp.stack([both[:, i * npair : (i + 1) * npair] for i in range(npr)])]
+    lw = (left[npr:, :][:, None, :] * w32[None, :, :]).reshape(8 * npr, CP)
     feats_bf = right.astype(BF)
     hi, lo = split(lw)
     biases.append(bias_oth[...] + (nt(hi, feats_bf) + nt(lo, feats_bf)).reshape(npr, 8, npair))
-    parts = [pb[:, h, :] for pb in biases for h in range(HALF)]
-    hi, lo = split(jnp.concatenate(parts, axis=0))
-    bias = jnp.dot(hi, onehot, preferred_element_type=F32) + jnp.dot(lo, onehot, preferred_element_type=F32)
+    parts = [pb[:, h, :] for h in range(HALF) for pb in biases]
+    hi, lo = split(jnp.concatenate(parts, axis=0) * (1.0 / scale))
+    bias = jnp.dot(jnp.concatenate([hi, lo], axis=0), onehot, preferred_element_type=F32)
+    bias = bias[: hi.shape[0]] + bias[hi.shape[0] :]
     bias = jnp.where(live, bias, F32(-1e30))
-    for c in copies[2:]:
-        c.wait()
+    copies[5].wait()
 
     for h in range(HALF):
-        k = kvg[:, :, h * HD : (h + 1) * HD].reshape(width, HD)
-        v = kvg[:, :, HW + h * HD : HW + (h + 1) * HD].reshape(width, HD)
-        for s, dest in enumerate((own, oth)):
-            qh = q[s * rows : (s + 1) * rows, h * HD : (h + 1) * HD]
-            first = (s * HALF + h) * npr
-            sc = nt(qh, k) * scale
-            sc = sc.reshape(npr, POOL, width) + bias[first : first + npr, None, :]
-            sc = sc.reshape(rows, width)
-            top = jnp.max(sc, axis=-1, keepdims=True)
-            e = jnp.exp(sc - top)
-            total = jnp.sum(e, axis=-1, keepdims=True)
-            acc = jnp.dot(e.astype(BF), v, preferred_element_type=F32)
-            dest[:, h * HD : (h + 1) * HD] = (acc / total).astype(BF)
-
-
-def out_body(place, x_own, a_own, a_oth, w_own, w_oth, mixed, buf, sem, full):
+        cols = slice(h * HD, (h + 1) * HD)
+        for c in copies[6 + 2 * h : 8 + 2 * h]:
+            c.wait()
+        k = kvg[h].reshape(width, HD)
+        v = kvg[HALF + h].reshape(width, HD)
+        sc = nt(q[:, cols], k).reshape(2 * npr, POOL, width)
+        sc = (sc + bias[2 * h * npr : 2 * (h + 1) * npr, None, :]).reshape(2 * rows, width)
+        top = jnp.max(sc, axis=-1, keepdims=True)
+        e = jnp.exp2((sc - top) * (scale * log2e))
+        total = jnp.sum(e, axis=-1, keepdims=True)
+        acc = jnp.dot(e.astype(BF), v, preferred_element_type=F32)
+        res = (acc / total).astype(BF)
+        own[:, cols] = res[:rows]
+        oth[:, cols] = res[rows:]
+    written.wait()
+
+
+def out_body(place, x_at, a_own, a_oth, w_own, w_oth, mixed, buf, sem, full, x_own, sem_x):
     copies = weight_copies(place, w_own, w_oth, buf, sem)
+    copies.append(pltpu.make_async_copy(x_at, x_own, sem_x.at[0]))
     for c in copies:
         c.start()
     side = place[0]
@@ -243,20 +264,14 @@
     def weights(n):
         return [pltpu.VMEM((NY, NX, 2, shard, n), BF), pltpu.SemaphoreType.DMA((2, NX))]
 
-    def heads(at):
-        x = lax.dynamic_slice_in_dim(w_bias.T, at * HALF, HALF, axis=0)
-        x = jnp.concatenate([x, jnp.zeros((8 - HALF, CP), F32)], axis=0)
-        return x, jnp.concatenate(split(x), axis=0)
-
-    wt32, wt = heads(side)
     bias_for_oth = pl.pallas_call(
         pair_bias_body,
         out_shape=jax.ShapeDtypeStruct((npr, 8, pair_in.shape[2]), F32),
-        in_specs=[vm()] * 2,
+        in_specs=[sm(), vm(), vm()],
         out_specs=vm(),
         compiler_params=params(),
         name="pair_bias",
-    )(pair_in[0], heads(1 - side)[1])
+    )(place, pair_in[0], w_bias.T)
 
     x_oth = swap(x_own, "yh")
     w = jnp.concatenate([mine(1), mine(2), w_pair[:, CP:]], axis=1)
@@ -276,7 +291,7 @@
     w_oth = swap(w, "c")
     kv = pl.pallas_call(
         kv_body,
-        out_shape=jax.ShapeDtypeStruct((2 * rows + 2 * npr, 2 * HW), BF),
+        out_shape=jax.ShapeDtypeStruct((4 * HALF * rows + 2 * npr, HD), BF),
         in_specs=[sm(), vm(), vm(), hbm(), hbm()],
         out_specs=vm(),
         scratch_shapes=weights(2 * HW + CP),
@@ -306,30 +321,37 @@
         attn_body,
         out_shape=(jax.ShapeDtypeStruct(pair_in.shape[1:], BF),)
         + (jax.ShapeDtypeStruct((rows, HW), BF),) * 2,
-        in_specs=[sm()] + [hbm()] * 3 + [vm()] * 4,
-        out_specs=(vm(), vm(), vm()),
+        in_specs=[sm()] + [hbm()] * 6,
+        out_specs=(hbm(), vm(), vm()),
         scratch_shapes=[
-            pltpu.VMEM(shape, BF)
-            for shape in (
-                (NZ, 2 * npr, CP),
-                pair_in.shape[1:],
-                q.shape,
-                (NZ, 2 * rows, 2 * HW),
-            )
-        ]
-        + [pltpu.SemaphoreType.DMA((4,))],
+            pltpu.VMEM((NZ, 2 * npr, CP), BF),
+            pltpu.VMEM(pair_in.shape[1:], BF),
+            pltpu.VMEM(q.shape, BF),
+            pltpu.VMEM((2 * HALF, NZ, 2 * rows, HD), BF),
+            pltpu.VMEM(bias_oth.shape, F32),
+            pltpu.VMEM(left.shape, F32),
+            pltpu.VMEM((HEADS, CP), F32),
+            pltpu.VMEM(pair_in.shape[1:], BF),
+            pltpu.SemaphoreType.DMA((6 + 2 * HALF,)),
+            pltpu.SemaphoreType.DMA((1,)),
+        ],
         compiler_params=pltpu.CompilerParams(vmem_limit_bytes=56 * 1024 * 1024),
         cost_estimate=cost(10),
         name="attn",
-    )(place, q, kvg, pair_in[0], bias_oth, left, wt, wt32)
+    )(place, q, kvg, pair_in[0], bias_oth, left, w_bias.T)
     got = swap(oth, "yh")
     wo_oth = swap(after(wo, oth), "c")
     mixed = pl.pallas_call(
         out_body,
         out_shape=jax.ShapeDtypeStruct((rows, depth), BF),
-        in_specs=[sm(), vm(), vm(), vm(), hbm(), hbm()],
+        in_specs=[sm(), hbm(), vm(), vm(), hbm(), hbm()],
         out_specs=vm(),
-        scratch_shapes=weights(HEADS * HD) + [pltpu.VMEM((rows, HEADS * HD), BF)],
+        scratch_shapes=weights(HEADS * HD)
+        + [
+            pltpu.VMEM((rows, HEADS * HD), BF),
+            pltpu.VMEM((rows, depth), BF),
+            pltpu.SemaphoreType.DMA((1,)),
+        ],
         compiler_params=params(),
         name="out",
     )(place, x_own, own, got, wo, wo_oth)

time: 144 us -> 142 us (0.986)
  waiting for transfers between devices: 28.6 us -> 27 us
where the time goes in v6:
time: 142 us; the launch traced here: 140 us
  starting transfers between devices  45 us (32%)
  blocking collectives  29.4 us (21%)
  waiting for transfers between devices  27 us (19%)
  Pallas kernels  15.1 us (11%)
  between operations  14.9 us (10%)
  local copies, waits for them, and re-layouts  8 us (6%)
    ppermute x6, starting transfers between devices, swap(): return lax.ppermute(x, axis, [(0, 1), (1, 0)])  29.8 us
    all_to_all x2, blocking collectives, spread(): lax.all_to_all(jnp.broadcast_to(x[None], (n,) + x.shape), axis, 0, 0, til...  29.4 us
    all_to_all x3, starting transfers between devices, spread(): lax.all_to_all(jnp.broadcast_to(x[None], (n,) + x.shape), axis, 0, 0, til...  15.2 us
    all_to_all x3, waiting for transfers between devices, spread(): lax.all_to_all(jnp.broadcast_to(x[None], (n,) + x.shape), axis, 0, 0, til...  11 us
    ppermute x6, waiting for transfers between devices, swap(): return lax.ppermute(x, axis, [(0, 1), (1, 0)])  9.3 us
    all_gather x1, waiting for transfers between devices, on_device(): kvg = lax.all_gather(kv, 'z', axis=0)  6.6 us
    pallas_call x1, Pallas kernels, on_device(): pl.pallas_call(attn_body, out_shape=(jax.ShapeDtypeStruct(pair_in.shape[1...  6.53 us
    broadcast_in_dim x5, local copies, waits for them, and re-layouts, spread(): jnp.broadcast_to(x[None], (n,) + x.shape)  3.33 us
  transfers between devices with their start and end apart: 10, of which 6 were waited for; matrix products, arithmetic and copies ran while one was open for 2% of the time, Pallas kernels for 7%

profile of v6, /device:TPU:1, one launch (start us, length us, event | category | flops | bytes accessed | tf_op | source)
XLA Modules:
  0.0 139.5 jit_solution(15159848753046259927)
XLA Ops:
  7.2 0.7 fusion
  7.9 0.8 constant_dynamic-slice_fusion.1
  8.8 12.5 %all_to_all.25 = bf16[4,48,896]{2,1,0:T(8,128)(2,1)S(1)} all-to-all(bf16[4,48,896]{2,1,0:T(8,128)(2,1)S(1)} %broadcast_in_dim.17), channel_id=1, replica_groups=mesh['yl'=4,'x'=4,'c'=2,'yh'=2,'z'=8] {'yl'}, dimensions={0} | all-to-all | bytes 688128 | tf_op jit(solution)/shard_map/all_to_all | solution.py:241
  21.3 1.2 broadcast_in_dim.18
  22.5 6.6 %all-to-all-start.1 = ((bf16[4,4,48,896]{3,2,1,0:T(8,128)(2,1)}), bf16[4,4,48,896]{3,2,1,0:T(8,128)(2,1)S(1)}, u32[]{:S(2)}, u32[]{:S(2)}) async-start(bf16[4,4,48,896]{3,2,1,0:T(8,128)(2,1)} %broadcast_in_dim.18), calls=%async_computation.1 | async-start | bytes 2752512 | tf_op jit(solution)/shard_map/all_to_all | solution.py:241
  29.2 5.5 %collective-permute-start = (bf16[128,1536]{1,0:T(8,128)(2,1)S(1)}, bf16[128,1536]{1,0:T(8,128)(2,1)S(1)}, u32[]{:S(2)}, u32[]{:S(2)}) collective-permute-start(bf16[128,1536]{1,0:T(8,128)(2,1)S(1)} %bitcast.9), channel_id=1, source_target_pairs={{0,8},{8,0},{1,9},{9,1},{2,10},{10,2},{3,11},{11,3},{4,12},{12,4},... | collective-permute-start | bytes 1179656 | tf_op jit(solution)/shard_map/ppermute | solution.py:245
  35.4 10.3 %all-to-all-done.1.w_own = bf16[4,4,48,896]{3,2,1,0:T(8,128)(2,1)S(1)} async-done(((bf16[4,4,48,896]{3,2,1,0:T(8,128)(2,1)}), bf16[4,4,48,896]{3,2,1,0:T(8,128)(2,1)S(1)}, u32[]{:S(2)}, u32[]{:S(2)}) %all-to-all-start.1) | async-done | bytes 1376288 | tf_op jit(solution)/shard_map/all_to_all | solution.py:241
  45.7 4.9 %collective-permute-start.3 = (bf16[4,4,48,896]{3,2,1,0:T(8,128)(2,1)S(1)}, bf16[4,4,48,896]{3,2,1,0:T(8,128)(2,1)S(1)}, u32[]{:S(2)}, u32[]{:S(2)}) collective-permute-start(bf16[4,4,48,896]{3,2,1,0:T(8,128)(2,1)S(1)} %all-to-all-done.1.w_own), channel_id=1, source_target_pairs={{0,16},{16,0},{1,17},{17,1},{2,18},{18,2},{3,19},{19,3},{4,20},{20... | collective-permute-start | bytes 4128776 | tf_op jit(solution)/shard_map/ppermute | solution.py:245
  50.6 2.0 %collective-permute-done.x_oth = bf16[128,1536]{1,0:T(8,128)(2,1)S(1)} collective-permute-done((bf16[128,1536]{1,0:T(8,128)(2,1)S(1)}, bf16[128,1536]{1,0:T(8,128)(2,1)S(1)}, u32[]{:S(2)}, u32[]{:S(2)}) %collective-permute-start) | collective-permute-done | bytes 393248 | tf_op jit(solution)/shard_map/ppermute | solution.py:245
  52.6 0.8 norm.1
  53.4 2.6 %kv.1 = bf16[1552,128]{1,0:T(8,128)(2,1)} custom-call(s32[3]{0:T(128)S(1)} %pad_add_fusion.place, bf16[256,1536]{1,0:T(8,128)(2,1)S(1)} %get-tuple-element.14.normed, bf16[32,1536]{1,0:T(8,128)(2,1)S(1)} %get-tuple-element.15.means, bf16[4,4,48,896]{3,2,1,0:T(8,128)(2,1)S(1)} %all-to-all-done.1.w_own, bf16[4,4,48,896]{3,2,1,0:T(8,128)(2,1)S(1)} %collective-permute-done.3.w_oth), custom_call_target="tpu_custom_call" | custom-call | flops 10000000000 | bytes 1048576 | tf_op jit(solution)/shard_map/kv/pallas_call | solution.py:292
  56.2 16.9 %all_to_all.26 = bf16[4,48,1280]{2,1,0:T(8,128)(2,1)S(1)} all-to-all(bf16[4,48,1280]{2,1,0:T(8,128)(2,1)S(1)} %broadcast_in_dim.19), channel_id=1, replica_groups=mesh['yl'=4,'x'=4,'c'=2,'yh'=2,'z'=8] {'yl'}, dimensions={0} | all-to-all | bytes 983040 | tf_op jit(solution)/shard_map/all_to_all | solution.py:241
  73.1 1.0 broadcast_in_dim.20
  74.0 4.2 %all-to-all-start.3 = ((bf16[4,4,48,512]{3,2,1,0:T(8,128)(2,1)}), bf16[4,4,48,512]{3,2,1,0:T(8,128)(2,1)S(1)}, u32[]{:S(2)}, u32[]{:S(2)}) async-start(bf16[4,4,48,512]{3,2,1,0:T(8,128)(2,1)} %broadcast_in_dim.20), calls=%async_computation.3 | async-start | bytes 1572864 | tf_op jit(solution)/shard_map/all_to_all | solution.py:241
  78.3 0.8 pair_bias.1
  79.0 4.7 %collective-permute-start.1 = (f32[8,8,128]{2,1,0:T(8,128)S(1)}, f32[8,8,128]{2,1,0:T(8,128)S(1)}, u32[]{:S(2)}, u32[]{:S(2)}) collective-permute-start(f32[8,8,128]{2,1,0:T(8,128)S(1)} %pair_bias.1), channel_id=1, source_target_pairs={{0,8},{8,0},{1,9},{9,1},{2,10},{10,2},{3,11},{11,3},{4,12},{12,4},... | collective-permute-start | bytes 98312 | tf_op jit(solution)/shard_map/ppermute | solution.py:245
  83.7 3.9 %collective-permute-done.1.refs_3_ = f32[8,8,128]{2,1,0:T(8,128)S(1)} collective-permute-done((f32[8,8,128]{2,1,0:T(8,128)S(1)}, f32[8,8,128]{2,1,0:T(8,128)S(1)}, u32[]{:S(2)}, u32[]{:S(2)}) %collective-permute-start.1) | collective-permute-done | bytes 32800 | tf_op jit(solution)/shard_map/ppermute | solution.py:245
  87.6 0.7 all-to-all-done.3.w_own
  88.3 5.1 %collective-permute-start.2 = (bf16[4,4,48,512]{3,2,1,0:T(8,128)(2,1)S(1)}, bf16[4,4,48,512]{3,2,1,0:T(8,128)(2,1)S(1)}, u32[]{:S(2)}, u32[]{:S(2)}) collective-permute-start(bf16[4,4,48,512]{3,2,1,0:T(8,128)(2,1)S(1)} %all-to-all-done.3.w_own), channel_id=1, source_target_pairs={{0,16},{16,0},{1,17},{17,1},{2,18},{18,2},{3,19},{19,3},{4,20},{20... | collective-permute-start | bytes 2359304 | tf_op jit(solution)/shard_map/ppermute | solution.py:245
  93.4 1.1 broadcast_in_dim.21
  94.6 4.4 %all-to-all-start.4 = ((bf16[4,4,48,768]{3,2,1,0:T(8,128)(2,1)}), bf16[4,4,48,768]{3,2,1,0:T(8,128)(2,1)S(1)}, u32[]{:S(2)}, u32[]{:S(2)}) async-start(bf16[4,4,48,768]{3,2,1,0:T(8,128)(2,1)} %broadcast_in_dim.21), calls=%async_computation.4 | async-start | bytes 2359296 | tf_op jit(solution)/shard_map/all_to_all | solution.py:241
  98.9 0.9 copy-done.5
  99.8 1.7 %q.1 = (bf16[256,384]{1,0:T(8,128)(2,1)S(1)}, f32[16,128]{1,0:T(8,128)S(1)}) custom-call(s32[3]{0:T(128)S(1)} %pad_add_fusion.place, bf16[256,1536]{1,0:T(8,128)(2,1)S(1)} %get-tuple-element.14.normed, bf16[32,1536]{1,0:T(8,128)(2,1)S(1)} %copy-done.5, bf16[4,4,48,512]{3,2,1,0:T(8,128)(2,1)S(1)} %all-to-all-done.3.w_own, ...), custom_call_target="tpu_custom_call" | custom-call | tf_op jit(solution)/shard_map/q/pallas_call | solution.py:309
  101.6 0.7 copy-done.9
  102.3 0.6 copy-done.10
  102.9 6.6 %all-gather.3.cloned.1.call-done = bf16[12416,128]{1,0:T(8,128)(2,1)} async-done(((bf16[1552,128]{1,0:T(8,128)(2,1)}), bf16[12416,128]{1,0:T(8,128)(2,1)}) %all-gather.3.cloned.1.call-update) | async-done | bytes 3178512 | tf_op jit(solution)/shard_map/all_gather | solution.py:302
  109.5 6.5 %attn.1 = (bf16[8,128,128]{2,1,0:T(8,128)(2,1)}, bf16[128,384]{1,0:T(8,128)(2,1)}, bf16[128,384]{1,0:T(8,128)(2,1)}) custom-call(s32[3]{0:T(128)} %copy-done.6, bf16[256,384]{1,0:T(8,128)(2,1)} %copy-done.9, bf16[8,1552,128]{2,1,0:T(8,128)(2,1)} %bitcast.18, bf16[8,128,128]{2,1,0:T(8,128)(2,1)} %bitcast.12, f32[8,8,128]{2,1,0:T(8,128)} %copy-done.13, ...), custom_call_target="tpu_custom_call" | custom-call | flops 10000000000 | bytes 1048576 | tf_op jit(solution)/shard_map/attn/pallas_call | solution.py:320
  116.0 2.6 %collective-permute-start.5 = (bf16[4,4,48,768]{3,2,1,0:T(8,128)(2,1)S(1)}, bf16[4,4,48,768]{3,2,1,0:T(8,128)(2,1)S(1)}, u32[]{:S(2)}, u32[]{:S(2)}) collective-permute-start(bf16[4,4,48,768]{3,2,1,0:T(8,128)(2,1)S(1)} %all-to-all-done.4.w_own), channel_id=1, source_target_pairs={{0,16},{16,0},{1,17},{17,1},{2,18},{18,2},{3,19},{19,3},{4,20},{20... | collective-permute-start | bytes 3538952 | tf_op jit(solution)/shard_map/ppermute | solution.py:245
  118.6 7.1 %collective-permute-start.4 = (bf16[128,384]{1,0:T(8,128)(2,1)}, bf16[128,384]{1,0:T(8,128)(2,1)S(1)}, u32[]{:S(2)}, u32[]{:S(2)}) collective-permute-start(bf16[128,384]{1,0:T(8,128)(2,1)} %get-tuple-element.22), channel_id=1, source_target_pairs={{0,8},{8,0},{1,9},{9,1},{2,10},{10,2},{3,11},{11,3},{4,12},{12,4},... | collective-permute-start | bytes 294920 | tf_op jit(solution)/shard_map/ppermute | solution.py:245
  125.7 3.3 %collective-permute-done.4.a_oth = bf16[128,384]{1,0:T(8,128)(2,1)S(1)} collective-permute-done((bf16[128,384]{1,0:T(8,128)(2,1)}, bf16[128,384]{1,0:T(8,128)(2,1)S(1)}, u32[]{:S(2)}, u32[]{:S(2)}) %collective-permute-start.4) | collective-permute-done | bytes 98336 | tf_op jit(solution)/shard_map/ppermute | solution.py:245
  129.1 0.9 copy-done.3
  129.9 2.7 %out.1 = bf16[128,1536]{1,0:T(8,128)(2,1)} custom-call(s32[3]{0:T(128)S(1)} %copy-done.7, bf16[128,1536]{1,0:T(8,128)(2,1)S(1)} %bitcast.11, bf16[128,384]{1,0:T(8,128)(2,1)S(1)} %copy-done.3, bf16[128,384]{1,0:T(8,128)(2,1)S(1)} %collective-permute-done.4.a_oth, bf16[4,4,48,768]{3,2,1,0:T(8,128)(2,1)S(1)} %all-to-all-done.4.w_own, ...), custom_call_target="tpu_custom_call" | custom-call | tf_op jit(solution)/shard_map/out/pallas_call | solution.py:344
  (38 shorter events, 0.3 us)
Async XLA Ops:
  22.5 6.6 %copy-start = (bf16[1,128,1536]{2,1,0:T(8,128)(2,1)S(1)}, bf16[1,128,1536]{2,1,0:T(8,128)(2,1)}, u32[]{:S(2)}) copy-start(bf16[1,128,1536]{2,1,0:T(8,128)(2,1)} %param.8) | copy-start | bytes 1179652
  22.5 12.8 %copy-start.12 = (f32[1536]{0:T(1024)S(1)}, f32[1536]{0:T(1024)}, u32[]{:S(2)}) copy-start(f32[1536]{0:T(1024)} %param.11) | copy-start | bytes 18436
  22.5 23.2 %all-to-all-start.1 = ((bf16[4,4,48,896]{3,2,1,0:T(8,128)(2,1)}), bf16[4,4,48,896]{3,2,1,0:T(8,128)(2,1)S(1)}, u32[]{:S(2)}, u32[]{:S(2)}) async-start(bf16[4,4,48,896]{3,2,1,0:T(8,128)(2,1)} %broadcast_in_dim.18), calls=%async_computation.1 | async-start | bytes 2752512 | tf_op jit(solution)/shard_map/all_to_all | solution.py:241
  29.1 80.3 %all-gather.3.cloned.1.call-start = ((), (), s32[]{:S(2)}) async-start(), calls=%async_computation.5 | async-start | bytes 3575808 | tf_op jit(solution)/shard_map/all_gather | solution.py:302
  29.2 23.5 %collective-permute-start = (bf16[128,1536]{1,0:T(8,128)(2,1)S(1)}, bf16[128,1536]{1,0:T(8,128)(2,1)S(1)}, u32[]{:S(2)}, u32[]{:S(2)}) collective-permute-start(bf16[128,1536]{1,0:T(8,128)(2,1)S(1)} %bitcast.9), channel_id=1, source_target_pairs={{0,8},{8,0},{1,9},{9,1},{2,10},{10,2},{3,11},{11,3},{4,12},{12,4},... | collective-permute-start | bytes 1179656 | tf_op jit(solution)/shard_map/ppermute | solution.py:245
  35.4 63.5 %copy-start.6 = (s32[3]{0:T(128)}, s32[3]{0:T(128)S(1)}, u32[]{:S(2)}) copy-start(s32[3]{0:T(128)S(1)} %pad_add_fusion.place) | copy-start | bytes 40
  45.7 7.7 %collective-permute-start.3 = (bf16[4,4,48,896]{3,2,1,0:T(8,128)(2,1)S(1)}, bf16[4,4,48,896]{3,2,1,0:T(8,128)(2,1)S(1)}, u32[]{:S(2)}, u32[]{:S(2)}) collective-permute-start(bf16[4,4,48,896]{3,2,1,0:T(8,128)(2,1)S(1)} %all-to-all-done.1.w_own), channel_id=1, source_target_pairs={{0,16},{16,0},{1,17},{17,1},{2,18},{18,2},{3,19},{19,3},{4,20},{20... | collective-permute-start | bytes 4128776 | tf_op jit(solution)/shard_map/ppermute | solution.py:245
  53.4 2.7 %copy-start.4 = (bf16[32,1536]{1,0:T(8,128)(2,1)}, bf16[32,1536]{1,0:T(8,128)(2,1)S(1)}, u32[]{:S(2)}) copy-start(bf16[32,1536]{1,0:T(8,128)(2,1)S(1)} %get-tuple-element.15.means) | copy-start | bytes 294916
  53.4 2.7 %copy-start.11 = (bf16[768,48]{0,1:T(8,128)(2,1)S(1)}, bf16[768,48]{0,1:T(8,128)(2,1)}, u32[]{:S(2)}) copy-start(bf16[768,48]{0,1:T(8,128)(2,1)} %param.15) | copy-start | bytes 221188
  73.0 5.2 %copy-start.2 = (bf16[1,8,128,128]{3,2,1,0:T(8,128)(2,1)S(1)}, bf16[1,8,128,128]{3,2,1,0:T(8,128)(2,1)}, u32[]{:S(2)}) copy-start(bf16[1,8,128,128]{3,2,1,0:T(8,128)(2,1)} %param.9) | copy-start | bytes 786436
  73.1 5.2 %copy-start.8 = (f32[128,6]{0,1:T(8,128)S(1)}, f32[128,6]{0,1:T(8,128)}, u32[]{:S(2)}) copy-start(f32[128,6]{0,1:T(8,128)} %param.14) | copy-start | bytes 9220
  74.0 14.3 %all-to-all-start.3 = ((bf16[4,4,48,512]{3,2,1,0:T(8,128)(2,1)}), bf16[4,4,48,512]{3,2,1,0:T(8,128)(2,1)S(1)}, u32[]{:S(2)}, u32[]{:S(2)}) async-start(bf16[4,4,48,512]{3,2,1,0:T(8,128)(2,1)} %broadcast_in_dim.20), calls=%async_computation.3 | async-start | bytes 1572864 | tf_op jit(solution)/shard_map/all_to_all | solution.py:241
  79.0 8.6 %collective-permute-start.1 = (f32[8,8,128]{2,1,0:T(8,128)S(1)}, f32[8,8,128]{2,1,0:T(8,128)S(1)}, u32[]{:S(2)}, u32[]{:S(2)}) collective-permute-start(f32[8,8,128]{2,1,0:T(8,128)S(1)} %pair_bias.1), channel_id=1, source_target_pairs={{0,8},{8,0},{1,9},{9,1},{2,10},{10,2},{3,11},{11,3},{4,12},{12,4},... | collective-permute-start | bytes 98312 | tf_op jit(solution)/shard_map/ppermute | solution.py:245
  87.6 0.7 copy-start.13
  88.3 10.6 %collective-permute-start.2 = (bf16[4,4,48,512]{3,2,1,0:T(8,128)(2,1)S(1)}, bf16[4,4,48,512]{3,2,1,0:T(8,128)(2,1)S(1)}, u32[]{:S(2)}, u32[]{:S(2)}) collective-permute-start(bf16[4,4,48,512]{3,2,1,0:T(8,128)(2,1)S(1)} %all-to-all-done.3.w_own), channel_id=1, source_target_pairs={{0,16},{16,0},{1,17},{17,1},{2,18},{18,2},{3,19},{19,3},{4,20},{20... | collective-permute-start | bytes 2359304 | tf_op jit(solution)/shard_map/ppermute | solution.py:245
  94.6 21.5 %all-to-all-start.4 = ((bf16[4,4,48,768]{3,2,1,0:T(8,128)(2,1)}), bf16[4,4,48,768]{3,2,1,0:T(8,128)(2,1)S(1)}, u32[]{:S(2)}, u32[]{:S(2)}) async-start(bf16[4,4,48,768]{3,2,1,0:T(8,128)(2,1)} %broadcast_in_dim.21), calls=%async_computation.4 | async-start | bytes 2359296 | tf_op jit(solution)/shard_map/all_to_all | solution.py:241
  98.9 0.9 copy-start.5
  101.6 0.7 copy-start.9
  102.3 0.6 copy-start.10
  109.5 19.6 %copy-start.1 = (bf16[1,128,1536]{2,1,0:T(8,128)(2,1)S(1)}, bf16[1,128,1536]{2,1,0:T(8,128)(2,1)}, u32[]{:S(2)}) copy-start(bf16[1,128,1536]{2,1,0:T(8,128)(2,1)} %param.8) | copy-start | bytes 1179652
  109.5 19.6 %copy-start.7 = (s32[3]{0:T(128)S(1)}, s32[3]{0:T(128)}, u32[]{:S(2)}) copy-start(s32[3]{0:T(128)} %copy-done.6) | copy-start | bytes 40
  116.0 13.0 %collective-permute-start.5 = (bf16[4,4,48,768]{3,2,1,0:T(8,128)(2,1)S(1)}, bf16[4,4,48,768]{3,2,1,0:T(8,128)(2,1)S(1)}, u32[]{:S(2)}, u32[]{:S(2)}) collective-permute-start(bf16[4,4,48,768]{3,2,1,0:T(8,128)(2,1)S(1)} %all-to-all-done.4.w_own), channel_id=1, source_target_pairs={{0,16},{16,0},{1,17},{17,1},{2,18},{18,2},{3,19},{19,3},{4,20},{20... | collective-permute-start | bytes 3538952 | tf_op jit(solution)/shard_map/ppermute | solution.py:245
  118.6 10.4 %collective-permute-start.4 = (bf16[128,384]{1,0:T(8,128)(2,1)}, bf16[128,384]{1,0:T(8,128)(2,1)S(1)}, u32[]{:S(2)}, u32[]{:S(2)}) collective-permute-start(bf16[128,384]{1,0:T(8,128)(2,1)} %get-tuple-element.22), channel_id=1, source_target_pairs={{0,8},{8,0},{1,9},{9,1},{2,10},{10,2},{3,11},{11,3},{4,12},{12,4},... | collective-permute-start | bytes 294920 | tf_op jit(solution)/shard_map/ppermute | solution.py:245
  129.0 0.9 copy-start.3
Sparse Core Ops, SparseCore 0:
  56.2 53.2 all-gather.2

commit v7 on v6

--- a/solution.py
+++ b/solution.py
@@ -91,17 +91,28 @@
 
 
 def kv_body(place, normed, means, w_own, w_oth, kv, buf, sem):
-    copies = weight_copies(place, w_own, w_oth, buf, sem)
+    copies = [
+        pltpu.make_async_copy(src.at[:, y], buf.at[y, :, core], sem.at[which, y])
+        for y in range(NY)
+        for which, src, core in ((0, w_own, place[1]), (1, w_oth, 1 - place[1]))
+    ]
     for c in copies:
         c.start()
-    for c in copies:
-        c.wait()
-    w = rows_of(buf)
     n = normed.shape[0]
-    both = jnp.dot(normed[...], w[:, : 2 * HW], preferred_element_type=F32).astype(BF)
+    m = means.shape[0] // 2
+    depth = normed.shape[1] // NY
+    both, pooled = 0.0, 0.0
+    for y in range(NY):
+        for c in copies[2 * y : 2 * y + 2]:
+            c.wait()
+        w = buf[y].reshape(depth, buf.shape[-1])
+        part = slice(y * depth, (y + 1) * depth)
+        both += jnp.dot(normed[:, part], w[:, : 2 * HW], preferred_element_type=F32)
+        pooled += jnp.dot(means[:, part], w[:, 2 * HW :], preferred_element_type=F32)
+    both = both.astype(BF)
     for i in range(2 * HALF):
         kv[i * n : (i + 1) * n, :] = both[:, i * HD : (i + 1) * HD]
-    kv[2 * HALF * n :, :] = project(means[...], w[:, 2 * HW :])
+    kv[2 * HALF * n :, :] = (pooled[:m] + pooled[m:]).astype(BF)
 
 
 def q_body(place, normed, means, w_own, w_oth, q, left, buf, sem):

time: 142 us -> 142 us (level)
  no operation moved by 1% of the time
where the time goes in v7:
time: 142 us; the launch traced here: 140 us
  starting transfers between devices  45 us (32%)
  blocking collectives  29.4 us (21%)
  waiting for transfers between devices  27 us (19%)
  Pallas kernels  15.7 us (11%)
  between operations  14.9 us (10%)
  local copies, waits for them, and re-layouts  8 us (6%)
    ppermute x6, starting transfers between devices, swap(): return lax.ppermute(x, axis, [(0, 1), (1, 0)])  29.8 us
    all_to_all x2, blocking collectives, spread(): lax.all_to_all(jnp.broadcast_to(x[None], (n,) + x.shape), axis, 0, 0, til...  29.4 us
    all_to_all x3, starting transfers between devices, spread(): lax.all_to_all(jnp.broadcast_to(x[None], (n,) + x.shape), axis, 0, 0, til...  15.2 us
    all_to_all x3, waiting for transfers between devices, spread(): lax.all_to_all(jnp.broadcast_to(x[None], (n,) + x.shape), axis, 0, 0, til...  11 us
    ppermute x6, waiting for transfers between devices, swap(): return lax.ppermute(x, axis, [(0, 1), (1, 0)])  9.29 us
    all_gather x1, waiting for transfers between devices, on_device(): kvg = lax.all_gather(kv, 'z', axis=0)  6.6 us
    pallas_call x1, Pallas kernels, on_device(): pl.pallas_call(attn_body, out_shape=(jax.ShapeDtypeStruct(pair_in.shape[1...  6.53 us
    broadcast_in_dim x5, local copies, waits for them, and re-layouts, spread(): jnp.broadcast_to(x[None], (n,) + x.shape)  3.33 us
  transfers between devices with their start and end apart: 10, of which 6 were waited for; matrix products, arithmetic and copies ran while one was open for 2% of the time, Pallas kernels for 7%

profile of v7, /device:TPU:1, one launch (start us, length us, event | category | flops | bytes accessed | tf_op | source)
XLA Modules:
  0.0 140.1 jit_solution(11750773734277435467)
XLA Ops:
  7.2 0.7 fusion
  7.9 0.8 constant_dynamic-slice_fusion.1
  8.8 12.5 %all_to_all.25 = bf16[4,48,896]{2,1,0:T(8,128)(2,1)S(1)} all-to-all(bf16[4,48,896]{2,1,0:T(8,128)(2,1)S(1)} %broadcast_in_dim.17), channel_id=1, replica_groups=mesh['yl'=4,'x'=4,'c'=2,'yh'=2,'z'=8] {'yl'}, dimensions={0} | all-to-all | bytes 688128 | tf_op jit(solution)/shard_map/all_to_all | solution.py:252
  21.3 1.2 broadcast_in_dim.18
  22.5 6.6 %all-to-all-start.1 = ((bf16[4,4,48,896]{3,2,1,0:T(8,128)(2,1)}), bf16[4,4,48,896]{3,2,1,0:T(8,128)(2,1)S(1)}, u32[]{:S(2)}, u32[]{:S(2)}) async-start(bf16[4,4,48,896]{3,2,1,0:T(8,128)(2,1)} %broadcast_in_dim.18), calls=%async_computation.1 | async-start | bytes 2752512 | tf_op jit(solution)/shard_map/all_to_all | solution.py:252
  29.2 5.5 %collective-permute-start = (bf16[128,1536]{1,0:T(8,128)(2,1)S(1)}, bf16[128,1536]{1,0:T(8,128)(2,1)S(1)}, u32[]{:S(2)}, u32[]{:S(2)}) collective-permute-start(bf16[128,1536]{1,0:T(8,128)(2,1)S(1)} %bitcast.9), channel_id=1, source_target_pairs={{0,8},{8,0},{1,9},{9,1},{2,10},{10,2},{3,11},{11,3},{4,12},{12,4},... | collective-permute-start | bytes 1179656 | tf_op jit(solution)/shard_map/ppermute | solution.py:256
  35.4 10.3 %all-to-all-done.1.w_own = bf16[4,4,48,896]{3,2,1,0:T(8,128)(2,1)S(1)} async-done(((bf16[4,4,48,896]{3,2,1,0:T(8,128)(2,1)}), bf16[4,4,48,896]{3,2,1,0:T(8,128)(2,1)S(1)}, u32[]{:S(2)}, u32[]{:S(2)}) %all-to-all-start.1) | async-done | bytes 1376288 | tf_op jit(solution)/shard_map/all_to_all | solution.py:252
  45.7 4.9 %collective-permute-start.3 = (bf16[4,4,48,896]{3,2,1,0:T(8,128)(2,1)S(1)}, bf16[4,4,48,896]{3,2,1,0:T(8,128)(2,1)S(1)}, u32[]{:S(2)}, u32[]{:S(2)}) collective-permute-start(bf16[4,4,48,896]{3,2,1,0:T(8,128)(2,1)S(1)} %all-to-all-done.1.w_own), channel_id=1, source_target_pairs={{0,16},{16,0},{1,17},{17,1},{2,18},{18,2},{3,19},{19,3},{4,20},{20... | collective-permute-start | bytes 4128776 | tf_op jit(solution)/shard_map/ppermute | solution.py:256
  50.6 2.0 %collective-permute-done.x_oth = bf16[128,1536]{1,0:T(8,128)(2,1)S(1)} collective-permute-done((bf16[128,1536]{1,0:T(8,128)(2,1)S(1)}, bf16[128,1536]{1,0:T(8,128)(2,1)S(1)}, u32[]{:S(2)}, u32[]{:S(2)}) %collective-permute-start) | collective-permute-done | bytes 393248 | tf_op jit(solution)/shard_map/ppermute | solution.py:256
  52.6 0.8 norm.1
  53.4 3.2 %kv.1 = bf16[1552,128]{1,0:T(8,128)(2,1)} custom-call(s32[3]{0:T(128)S(1)} %pad_add_fusion.place, bf16[256,1536]{1,0:T(8,128)(2,1)S(1)} %get-tuple-element.14.normed, bf16[32,1536]{1,0:T(8,128)(2,1)S(1)} %get-tuple-element.15.means, bf16[4,4,48,896]{3,2,1,0:T(8,128)(2,1)S(1)} %all-to-all-done.1.w_own, bf16[4,4,48,896]{3,2,1,0:T(8,128)(2,1)S(1)} %collective-permute-done.3.w_oth), custom_call_target="tpu_custom_call" | custom-call | flops 10000000000 | bytes 1048576 | tf_op jit(solution)/shard_map/kv/pallas_call | solution.py:303
  56.8 16.9 %all_to_all.26 = bf16[4,48,1280]{2,1,0:T(8,128)(2,1)S(1)} all-to-all(bf16[4,48,1280]{2,1,0:T(8,128)(2,1)S(1)} %broadcast_in_dim.19), channel_id=1, replica_groups=mesh['yl'=4,'x'=4,'c'=2,'yh'=2,'z'=8] {'yl'}, dimensions={0} | all-to-all | bytes 983040 | tf_op jit(solution)/shard_map/all_to_all | solution.py:252
  73.7 1.0 broadcast_in_dim.20
  74.7 4.2 %all-to-all-start.3 = ((bf16[4,4,48,512]{3,2,1,0:T(8,128)(2,1)}), bf16[4,4,48,512]{3,2,1,0:T(8,128)(2,1)S(1)}, u32[]{:S(2)}, u32[]{:S(2)}) async-start(bf16[4,4,48,512]{3,2,1,0:T(8,128)(2,1)} %broadcast_in_dim.20), calls=%async_computation.3 | async-start | bytes 1572864 | tf_op jit(solution)/shard_map/all_to_all | solution.py:252
  78.9 0.8 pair_bias.1
  79.6 4.7 %collective-permute-start.1 = (f32[8,8,128]{2,1,0:T(8,128)S(1)}, f32[8,8,128]{2,1,0:T(8,128)S(1)}, u32[]{:S(2)}, u32[]{:S(2)}) collective-permute-start(f32[8,8,128]{2,1,0:T(8,128)S(1)} %pair_bias.1), channel_id=1, source_target_pairs={{0,8},{8,0},{1,9},{9,1},{2,10},{10,2},{3,11},{11,3},{4,12},{12,4},... | collective-permute-start | bytes 98312 | tf_op jit(solution)/shard_map/ppermute | solution.py:256
  84.3 3.9 %collective-permute-done.1.refs_3_ = f32[8,8,128]{2,1,0:T(8,128)S(1)} collective-permute-done((f32[8,8,128]{2,1,0:T(8,128)S(1)}, f32[8,8,128]{2,1,0:T(8,128)S(1)}, u32[]{:S(2)}, u32[]{:S(2)}) %collective-permute-start.1) | collective-permute-done | bytes 32800 | tf_op jit(solution)/shard_map/ppermute | solution.py:256
  88.2 0.7 all-to-all-done.3.w_own
  89.0 5.1 %collective-permute-start.2 = (bf16[4,4,48,512]{3,2,1,0:T(8,128)(2,1)S(1)}, bf16[4,4,48,512]{3,2,1,0:T(8,128)(2,1)S(1)}, u32[]{:S(2)}, u32[]{:S(2)}) collective-permute-start(bf16[4,4,48,512]{3,2,1,0:T(8,128)(2,1)S(1)} %all-to-all-done.3.w_own), channel_id=1, source_target_pairs={{0,16},{16,0},{1,17},{17,1},{2,18},{18,2},{3,19},{19,3},{4,20},{20... | collective-permute-start | bytes 2359304 | tf_op jit(solution)/shard_map/ppermute | solution.py:256
  94.1 1.1 broadcast_in_dim.21
  95.2 4.4 %all-to-all-start.4 = ((bf16[4,4,48,768]{3,2,1,0:T(8,128)(2,1)}), bf16[4,4,48,768]{3,2,1,0:T(8,128)(2,1)S(1)}, u32[]{:S(2)}, u32[]{:S(2)}) async-start(bf16[4,4,48,768]{3,2,1,0:T(8,128)(2,1)} %broadcast_in_dim.21), calls=%async_computation.4 | async-start | bytes 2359296 | tf_op jit(solution)/shard_map/all_to_all | solution.py:252
  99.6 0.9 copy-done.5
  100.5 1.7 %q.1 = (bf16[256,384]{1,0:T(8,128)(2,1)S(1)}, f32[16,128]{1,0:T(8,128)S(1)}) custom-call(s32[3]{0:T(128)S(1)} %pad_add_fusion.place, bf16[256,1536]{1,0:T(8,128)(2,1)S(1)} %get-tuple-element.14.normed, bf16[32,1536]{1,0:T(8,128)(2,1)S(1)} %copy-done.5, bf16[4,4,48,512]{3,2,1,0:T(8,128)(2,1)S(1)} %all-to-all-done.3.w_own, ...), custom_call_target="tpu_custom_call" | custom-call | tf_op jit(solution)/shard_map/q/pallas_call | solution.py:320
  102.2 0.7 copy-done.9
  102.9 0.6 copy-done.10
  103.5 6.6 %all-gather.3.cloned.1.call-done = bf16[12416,128]{1,0:T(8,128)(2,1)} async-done(((bf16[1552,128]{1,0:T(8,128)(2,1)}), bf16[12416,128]{1,0:T(8,128)(2,1)}) %all-gather.3.cloned.1.call-update) | async-done | bytes 3178512 | tf_op jit(solution)/shard_map/all_gather | solution.py:313
  110.1 6.5 %attn.1 = (bf16[8,128,128]{2,1,0:T(8,128)(2,1)}, bf16[128,384]{1,0:T(8,128)(2,1)}, bf16[128,384]{1,0:T(8,128)(2,1)}) custom-call(s32[3]{0:T(128)} %copy-done.6, bf16[256,384]{1,0:T(8,128)(2,1)} %copy-done.9, bf16[8,1552,128]{2,1,0:T(8,128)(2,1)} %bitcast.18, bf16[8,128,128]{2,1,0:T(8,128)(2,1)} %bitcast.12, f32[8,8,128]{2,1,0:T(8,128)} %copy-done.13, ...), custom_call_target="tpu_custom_call" | custom-call | flops 10000000000 | bytes 1048576 | tf_op jit(solution)/shard_map/attn/pallas_call | solution.py:331
  116.6 2.6 %collective-permute-start.5 = (bf16[4,4,48,768]{3,2,1,0:T(8,128)(2,1)S(1)}, bf16[4,4,48,768]{3,2,1,0:T(8,128)(2,1)S(1)}, u32[]{:S(2)}, u32[]{:S(2)}) collective-permute-start(bf16[4,4,48,768]{3,2,1,0:T(8,128)(2,1)S(1)} %all-to-all-done.4.w_own), channel_id=1, source_target_pairs={{0,16},{16,0},{1,17},{17,1},{2,18},{18,2},{3,19},{19,3},{4,20},{20... | collective-permute-start | bytes 3538952 | tf_op jit(solution)/shard_map/ppermute | solution.py:256
  119.2 7.1 %collective-permute-start.4 = (bf16[128,384]{1,0:T(8,128)(2,1)}, bf16[128,384]{1,0:T(8,128)(2,1)S(1)}, u32[]{:S(2)}, u32[]{:S(2)}) collective-permute-start(bf16[128,384]{1,0:T(8,128)(2,1)} %get-tuple-element.22), channel_id=1, source_target_pairs={{0,8},{8,0},{1,9},{9,1},{2,10},{10,2},{3,11},{11,3},{4,12},{12,4},... | collective-permute-start | bytes 294920 | tf_op jit(solution)/shard_map/ppermute | solution.py:256
  126.3 3.3 %collective-permute-done.4.a_oth = bf16[128,384]{1,0:T(8,128)(2,1)S(1)} collective-permute-done((bf16[128,384]{1,0:T(8,128)(2,1)}, bf16[128,384]{1,0:T(8,128)(2,1)S(1)}, u32[]{:S(2)}, u32[]{:S(2)}) %collective-permute-start.4) | collective-permute-done | bytes 98336 | tf_op jit(solution)/shard_map/ppermute | solution.py:256
  129.7 0.9 copy-done.3
  130.6 2.7 %out.1 = bf16[128,1536]{1,0:T(8,128)(2,1)} custom-call(s32[3]{0:T(128)S(1)} %copy-done.7, bf16[128,1536]{1,0:T(8,128)(2,1)S(1)} %bitcast.11, bf16[128,384]{1,0:T(8,128)(2,1)S(1)} %copy-done.3, bf16[128,384]{1,0:T(8,128)(2,1)S(1)} %collective-permute-done.4.a_oth, bf16[4,4,48,768]{3,2,1,0:T(8,128)(2,1)S(1)} %all-to-all-done.4.w_own, ...), custom_call_target="tpu_custom_call" | custom-call | tf_op jit(solution)/shard_map/out/pallas_call | solution.py:355
  (38 shorter events, 0.3 us)
Async XLA Ops:
  22.5 6.6 %copy-start = (bf16[1,128,1536]{2,1,0:T(8,128)(2,1)S(1)}, bf16[1,128,1536]{2,1,0:T(8,128)(2,1)}, u32[]{:S(2)}) copy-start(bf16[1,128,1536]{2,1,0:T(8,128)(2,1)} %param.8) | copy-start | bytes 1179652
  22.5 12.8 %copy-start.12 = (f32[1536]{0:T(1024)S(1)}, f32[1536]{0:T(1024)}, u32[]{:S(2)}) copy-start(f32[1536]{0:T(1024)} %param.11) | copy-start | bytes 18436
  22.5 23.2 %all-to-all-start.1 = ((bf16[4,4,48,896]{3,2,1,0:T(8,128)(2,1)}), bf16[4,4,48,896]{3,2,1,0:T(8,128)(2,1)S(1)}, u32[]{:S(2)}, u32[]{:S(2)}) async-start(bf16[4,4,48,896]{3,2,1,0:T(8,128)(2,1)} %broadcast_in_dim.18), calls=%async_computation.1 | async-start | bytes 2752512 | tf_op jit(solution)/shard_map/all_to_all | solution.py:252
  29.1 80.9 %all-gather.3.cloned.1.call-start = ((), (), s32[]{:S(2)}) async-start(), calls=%async_computation.5 | async-start | bytes 3575808 | tf_op jit(solution)/shard_map/all_gather | solution.py:313
  29.2 23.5 %collective-permute-start = (bf16[128,1536]{1,0:T(8,128)(2,1)S(1)}, bf16[128,1536]{1,0:T(8,128)(2,1)S(1)}, u32[]{:S(2)}, u32[]{:S(2)}) collective-permute-start(bf16[128,1536]{1,0:T(8,128)(2,1)S(1)} %bitcast.9), channel_id=1, source_target_pairs={{0,8},{8,0},{1,9},{9,1},{2,10},{10,2},{3,11},{11,3},{4,12},{12,4},... | collective-permute-start | bytes 1179656 | tf_op jit(solution)/shard_map/ppermute | solution.py:256
  35.4 64.2 %copy-start.6 = (s32[3]{0:T(128)}, s32[3]{0:T(128)S(1)}, u32[]{:S(2)}) copy-start(s32[3]{0:T(128)S(1)} %pad_add_fusion.place) | copy-start | bytes 40
  45.7 7.7 %collective-permute-start.3 = (bf16[4,4,48,896]{3,2,1,0:T(8,128)(2,1)S(1)}, bf16[4,4,48,896]{3,2,1,0:T(8,128)(2,1)S(1)}, u32[]{:S(2)}, u32[]{:S(2)}) collective-permute-start(bf16[4,4,48,896]{3,2,1,0:T(8,128)(2,1)S(1)} %all-to-all-done.1.w_own), channel_id=1, source_target_pairs={{0,16},{16,0},{1,17},{17,1},{2,18},{18,2},{3,19},{19,3},{4,20},{20... | collective-permute-start | bytes 4128776 | tf_op jit(solution)/shard_map/ppermute | solution.py:256
  53.4 3.3 %copy-start.4 = (bf16[32,1536]{1,0:T(8,128)(2,1)}, bf16[32,1536]{1,0:T(8,128)(2,1)S(1)}, u32[]{:S(2)}) copy-start(bf16[32,1536]{1,0:T(8,128)(2,1)S(1)} %get-tuple-element.15.means) | copy-start | bytes 294916
  53.4 3.3 %copy-start.11 = (bf16[768,48]{0,1:T(8,128)(2,1)S(1)}, bf16[768,48]{0,1:T(8,128)(2,1)}, u32[]{:S(2)}) copy-start(bf16[768,48]{0,1:T(8,128)(2,1)} %param.15) | copy-start | bytes 221188
  73.7 5.2 %copy-start.2 = (bf16[1,8,128,128]{3,2,1,0:T(8,128)(2,1)S(1)}, bf16[1,8,128,128]{3,2,1,0:T(8,128)(2,1)}, u32[]{:S(2)}) copy-start(bf16[1,8,128,128]{3,2,1,0:T(8,128)(2,1)} %param.9) | copy-start | bytes 786436
  73.7 5.2 %copy-start.8 = (f32[128,6]{0,1:T(8,128)S(1)}, f32[128,6]{0,1:T(8,128)}, u32[]{:S(2)}) copy-start(f32[128,6]{0,1:T(8,128)} %param.14) | copy-start | bytes 9220
  74.7 14.3 %all-to-all-start.3 = ((bf16[4,4,48,512]{3,2,1,0:T(8,128)(2,1)}), bf16[4,4,48,512]{3,2,1,0:T(8,128)(2,1)S(1)}, u32[]{:S(2)}, u32[]{:S(2)}) async-start(bf16[4,4,48,512]{3,2,1,0:T(8,128)(2,1)} %broadcast_in_dim.20), calls=%async_computation.3 | async-start | bytes 1572864 | tf_op jit(solution)/shard_map/all_to_all | solution.py:252
  79.6 8.6 %collective-permute-start.1 = (f32[8,8,128]{2,1,0:T(8,128)S(1)}, f32[8,8,128]{2,1,0:T(8,128)S(1)}, u32[]{:S(2)}, u32[]{:S(2)}) collective-permute-start(f32[8,8,128]{2,1,0:T(8,128)S(1)} %pair_bias.1), channel_id=1, source_target_pairs={{0,8},{8,0},{1,9},{9,1},{2,10},{10,2},{3,11},{11,3},{4,12},{12,4},... | collective-permute-start | bytes 98312 | tf_op jit(solution)/shard_map/ppermute | solution.py:256
  88.2 0.7 copy-start.13
  89.0 10.6 %collective-permute-start.2 = (bf16[4,4,48,512]{3,2,1,0:T(8,128)(2,1)S(1)}, bf16[4,4,48,512]{3,2,1,0:T(8,128)(2,1)S(1)}, u32[]{:S(2)}, u32[]{:S(2)}) collective-permute-start(bf16[4,4,48,512]{3,2,1,0:T(8,128)(2,1)S(1)} %all-to-all-done.3.w_own), channel_id=1, source_target_pairs={{0,16},{16,0},{1,17},{17,1},{2,18},{18,2},{3,19},{19,3},{4,20},{20... | collective-permute-start | bytes 2359304 | tf_op jit(solution)/shard_map/ppermute | solution.py:256
  95.2 21.5 %all-to-all-start.4 = ((bf16[4,4,48,768]{3,2,1,0:T(8,128)(2,1)}), bf16[4,4,48,768]{3,2,1,0:T(8,128)(2,1)S(1)}, u32[]{:S(2)}, u32[]{:S(2)}) async-start(bf16[4,4,48,768]{3,2,1,0:T(8,128)(2,1)} %broadcast_in_dim.21), calls=%async_computation.4 | async-start | bytes 2359296 | tf_op jit(solution)/shard_map/all_to_all | solution.py:252
  99.6 0.9 copy-start.5
  102.2 0.7 copy-start.9
  102.9 0.6 copy-start.10
  110.1 19.6 %copy-start.1 = (bf16[1,128,1536]{2,1,0:T(8,128)(2,1)S(1)}, bf16[1,128,1536]{2,1,0:T(8,128)(2,1)}, u32[]{:S(2)}) copy-start(bf16[1,128,1536]{2,1,0:T(8,128)(2,1)} %param.8) | copy-start | bytes 1179652
  110.1 19.6 %copy-start.7 = (s32[3]{0:T(128)S(1)}, s32[3]{0:T(128)}, u32[]{:S(2)}) copy-start(s32[3]{0:T(128)} %copy-done.6) | copy-start | bytes 40
  116.6 13.0 %collective-permute-start.5 = (bf16[4,4,48,768]{3,2,1,0:T(8,128)(2,1)S(1)}, bf16[4,4,48,768]{3,2,1,0:T(8,128)(2,1)S(1)}, u32[]{:S(2)}, u32[]{:S(2)}) collective-permute-start(bf16[4,4,48,768]{3,2,1,0:T(8,128)(2,1)S(1)} %all-to-all-done.4.w_own), channel_id=1, source_target_pairs={{0,16},{16,0},{1,17},{17,1},{2,18},{18,2},{3,19},{19,3},{4,20},{20... | collective-permute-start | bytes 3538952 | tf_op jit(solution)/shard_map/ppermute | solution.py:256
  119.2 10.4 %collective-permute-start.4 = (bf16[128,384]{1,0:T(8,128)(2,1)}, bf16[128,384]{1,0:T(8,128)(2,1)S(1)}, u32[]{:S(2)}, u32[]{:S(2)}) collective-permute-start(bf16[128,384]{1,0:T(8,128)(2,1)} %get-tuple-element.22), channel_id=1, source_target_pairs={{0,8},{8,0},{1,9},{9,1},{2,10},{10,2},{3,11},{11,3},{4,12},{12,4},... | collective-permute-start | bytes 294920 | tf_op jit(solution)/shard_map/ppermute | solution.py:256
  129.7 0.9 copy-start.3
Sparse Core Ops, SparseCore 0:
  56.8 53.2 all-gather.2
